TPU v7x, 32 devices: a whole 2x2x4 slice. The times are simulated.
32 devices in a mesh: dp: 2 (over core), seq: 4 (over y, x), tensor: 4 (over z).
Axes of the slice: x: 2, y: 2, z: 4, core: 2. Of those that a mesh axis runs over, the one named last changes fastest.
Arguments:
- hidden: bfloat16 [2, 2112, 2048], P('dp', 'seq'), may hold values from -6 to 6
- teacher: bfloat16 [2, 2112, 2048], P('dp', 'seq'), may hold values from -6 to 6
- valid_length: int32 [2], replicated, may hold values from 1585 to 2112, as said below
- mamba_norm: bfloat16 [2048], P(('dp', 'seq')), may hold values from 0.5 to 1.5
- mamba_in: bfloat16 [2048, 2, 4096], P(('dp', 'seq'), None, 'tensor'), may hold values from -0.125 to 0.125
- conv_kernel: float32 [4, 4096], P(None, 'tensor'), may hold values from -3 to 3
- conv_bias: float32 [4096], P('tensor'), may hold values from -3 to 3
- select_weight: bfloat16 [4096, 160], P('tensor'), may hold values from -0.09375 to 0.09375
- step_weight: bfloat16 [128, 4096], P(None, 'tensor'), may hold values from -0.5 to 0.5
- step_bias: float32 [4096], P('tensor'), may hold values from -7 to -2.5
- decay_log: float32 [16, 4096], P(None, 'tensor'), may hold values from 0 to 2.77
- skip_gain: float32 [4096], P('tensor'), may hold values from 0.5 to 1.5
- mamba_out: bfloat16 [2048, 4096], P(('dp', 'seq'), 'tensor'), may hold values from -0.1875 to 0.1875
- attn_norm: bfloat16 [2048], P(('dp', 'seq')), may hold values from 0.5 to 1.5
- attn_qkv: bfloat16 [2048, 3, 2048], P(('dp', 'seq'), None, 'tensor'), may hold values from -0.125 to 0.125
- attn_out: bfloat16 [2048, 2048], P(('dp', 'seq'), 'tensor'), may hold values from -2 to 2
- first_norm: bfloat16 [2048], P(('dp', 'seq')), may hold values from 0.5 to 1.5
- first_gate_up: bfloat16 [2048, 2, 8192], P(('dp', 'seq'), None, 'tensor'), may hold values from -0.125 to 0.125
- first_down: bfloat16 [2048, 8192], P(('dp', 'seq'), 'tensor'), may hold values from -0.125 to 0.125
- second_norm: bfloat16 [2048], P(('dp', 'seq')), may hold values from 0.5 to 1.5
- second_gate_up: bfloat16 [2048, 2, 8192], P(('dp', 'seq'), None, 'tensor'), may hold values from -0.125 to 0.125
- second_down: bfloat16 [2048, 8192], P(('dp', 'seq'), 'tensor'), may hold values from -0.125 to 0.125
Outputs:
- loss: float32 [], replicated
- output: bfloat16 [2, 2112, 2048], P('dp', 'seq')
- input_grad: float32 [2, 2112, 2048], P('dp', 'seq')
- grad_mamba_norm: float32 [2048], P(('dp', 'seq'))
- grad_mamba_in: float32 [2048, 2, 4096], P(('dp', 'seq'), None, 'tensor')
- grad_conv_kernel: float32 [4, 4096], P(None, 'tensor')
- grad_conv_bias: float32 [4096], P('tensor')
- grad_select_weight: float32 [4096, 160], P('tensor')
- grad_step_weight: float32 [128, 4096], P(None, 'tensor')
- grad_step_bias: float32 [4096], P('tensor')
- grad_decay_log: float32 [16, 4096], P(None, 'tensor')
- grad_skip_gain: float32 [4096], P('tensor')
- grad_mamba_out: float32 [2048, 4096], P(('dp', 'seq'), 'tensor')
- grad_attn_norm: float32 [2048], P(('dp', 'seq'))
- grad_attn_qkv: float32 [2048, 3, 2048], P(('dp', 'seq'), None, 'tensor')
- grad_attn_out: float32 [2048, 2048], P(('dp', 'seq'), 'tensor')
- grad_first_norm: float32 [2048], P(('dp', 'seq'))
- grad_first_gate_up: float32 [2048, 2, 8192], P(('dp', 'seq'), None, 'tensor')
- grad_first_down: float32 [2048, 8192], P(('dp', 'seq'), 'tensor')
- grad_second_norm: float32 [2048], P(('dp', 'seq'))
- grad_second_gate_up: float32 [2048, 2, 8192], P(('dp', 'seq'), None, 'tensor')
- grad_second_down: float32 [2048, 8192], P(('dp', 'seq'), 'tensor')
Inputs may be any that keep to these rules, and one draw needn't show every extreme that they name: valid_length[s] counts the leading valid positions of sequence s; in every draw some sequence is valid over all 2112 positions.
All inputs are finite; a program needn't handle non-finite values.
Results may differ from a plain program's by a relative error of at most 0.024.
Values may be sent and summed in bfloat16 or wider, within the bound.
A program may use at most 384 MiB of HBM per device.

v0:
```python
import jax
import jax.numpy as jnp
from jax import lax
from jax.sharding import PartitionSpec as P

HD = 64
WINDOW = 2048


epsilon = 1e-05
group_count = 16
head_groups = 2


def shifted(block, axis, distance):
    devices = range(lax.axis_size(axis))
    route = [(i - distance, i) for i in devices if i - distance in devices]
    return lax.ppermute(block, axis, route)


def product(left, right):
    return jnp.dot(left, right, preferred_element_type=jnp.float32)


def product_t(left, right):
    return lax.dot_general(
        left, right, (((1,), (1,)), ((), ())), preferred_element_type=jnp.float32
    )


def product_tl(left, right):
    return lax.dot_general(
        left, right, (((0,), (0,)), ((), ())), preferred_element_type=jnp.float32
    )


def expand(acting, weight):
    return jnp.einsum("td,dge->tge", acting, weight, preferred_element_type=jnp.float32)


def contract(grads, weight):
    return jnp.einsum("tge,dge->td", grads, weight, preferred_element_type=jnp.float32)


def weight_grad(acting, grads):
    return jnp.einsum("td,tge->dge", acting, grads, preferred_element_type=jnp.float32)


def round_trip(values):
    return lax.optimization_barrier(values.astype(jnp.bfloat16)).astype(jnp.float32)


def norm_forward(values, gain_vec):
    inv_rms = lax.rsqrt(jnp.mean(values * values, axis=-1, keepdims=True) + epsilon)
    return (values * inv_rms * gain_vec, inv_rms)


def norm_backward(values, inv_rms, gain_vec, grad_normed):
    weighted = grad_normed * gain_vec
    mean_term = jnp.mean(weighted * values, axis=-1, keepdims=True)
    grad_values = inv_rms * weighted - values * (inv_rms * inv_rms * inv_rms) * mean_term
    grad_gain = jnp.sum(grad_normed * values * inv_rms, axis=0)
    return (grad_values, grad_gain)


def silu_slope(values):
    sigmoid_val = jax.nn.sigmoid(values)
    return sigmoid_val * (1.0 + values * (1.0 - sigmoid_val))


def gather_layer(norm_gain, first_matrix, second_matrix):
    return (
        lax.all_gather(norm_gain, ("dp", "seq"), axis=0, tiled=True),
        lax.all_gather(first_matrix, ("dp", "seq"), axis=0, tiled=True),
        lax.all_gather(second_matrix, ("dp", "seq"), axis=0, tiled=True),
    )


def gather_again(norm_gain, first_matrix, second_matrix):
    return (
        lax.all_gather(norm_gain, ("dp", "seq"), axis=0, tiled=True),
        lax.all_gather(first_matrix, ("dp", "seq"), axis=0, tiled=True),
        lax.all_gather(second_matrix, ("dp", "seq"), axis=0, tiled=True),
    )


def layer_grads(gain_grad, first_grad, second_grad):
    return (
        lax.psum_scatter(
            gain_grad.astype(jnp.bfloat16), ("dp", "seq"), scatter_dimension=0, tiled=True
        ).astype(jnp.float32),
        lax.psum_scatter(
            first_grad.astype(jnp.bfloat16), ("dp", "seq"), scatter_dimension=0, tiled=True
        ).astype(jnp.float32),
        lax.psum_scatter(
            second_grad.astype(jnp.bfloat16), ("dp", "seq"), scatter_dimension=0, tiled=True
        ).astype(jnp.float32),
    )


def tensor_forward_sum(partial_sum):
    return lax.psum(partial_sum.astype(jnp.bfloat16), "tensor").astype(jnp.float32)


def tensor_backward_sum(partial_sum):
    return lax.psum(partial_sum.astype(jnp.bfloat16), "tensor").astype(jnp.float32)


def rope_tables(positions, head_dim):
    half_dim = head_dim // 2
    frequency = 10000.0 ** (-jnp.arange(half_dim, dtype=jnp.float32) / half_dim)
    angles = positions.astype(jnp.float32)[:, None] * frequency[None, :]
    return (jnp.cos(angles)[:, None, :], jnp.sin(angles)[:, None, :])


def rotate(values, cosine, sine_table):
    half_dim = values.shape[-1] // 2
    front_half = values[..., :half_dim]
    back_half = values[..., half_dim:]
    return jnp.concatenate(
        [
            front_half * cosine - back_half * sine_table,
            back_half * cosine + front_half * sine_table,
        ],
        axis=-1,
    )


def rotate_back(values, cosine, sine_table):
    half_dim = values.shape[-1] // 2
    front_half = values[..., :half_dim]
    back_half = values[..., half_dim:]
    return jnp.concatenate(
        [
            front_half * cosine + back_half * sine_table,
            back_half * cosine - front_half * sine_table,
        ],
        axis=-1,
    )


def local_scan(inputs, step_size, input_map, output_map, decay_rate):
    rows_here = inputs.shape[0]
    per_group = rows_here // group_count
    shaped = tuple(
        (
            piece.reshape(group_count, per_group, piece.shape[-1])
            for piece in (inputs, step_size, input_map, output_map)
        )
    )

    def advance(carried, pieces):
        value_rows, size_rows, in_rows, out_rows = pieces
        outputs = []
        for position in range(per_group):
            carried = (
                jnp.exp(size_rows[position][None, :] * decay_rate) * carried
                + in_rows[position][:, None] * (size_rows[position] * value_rows[position])[None, :]
            )
            outputs.append(jnp.sum(out_rows[position][:, None] * carried, axis=0))
        return (carried, jnp.stack(outputs))

    end_state, outputs = lax.scan(jax.checkpoint(advance), jnp.zeros_like(decay_rate), shaped)
    decay_total = jnp.exp(decay_rate * jnp.sum(step_size, axis=0)[None, :])
    return (outputs.reshape(rows_here, -1), decay_total, end_state)


def correction(step_size, output_map, decay_rate, start_state):
    cumulative = jnp.cumsum(step_size, axis=0)
    half_states = decay_rate.shape[0] // 2
    result = jnp.zeros_like(step_size)
    for half_index in range(2):
        lower = half_index * half_states
        rate_half = decay_rate[lower : lower + half_states]
        factor = jnp.exp(rate_half[None] * cumulative[:, None, :])
        result = result + jnp.sum(
            output_map[:, lower : lower + half_states, None]
            * factor
            * start_state[None, lower : lower + half_states],
            axis=1,
        )
    return result


def incoming_grad(step_size, output_map, decay_rate, grad_core):
    cumulative = jnp.cumsum(step_size, axis=0)
    half_states = decay_rate.shape[0] // 2
    pieces = []
    for half_index in range(2):
        lower = half_index * half_states
        rate_half = decay_rate[lower : lower + half_states]
        factor = jnp.exp(rate_half[None] * cumulative[:, None, :])
        pieces.append(
            jnp.sum(
                grad_core[:, None, :] * output_map[:, lower : lower + half_states, None] * factor,
                axis=0,
            )
        )
    return jnp.concatenate(pieces, axis=0)


def masked_scores(queries, key_rows, query_pos, key_pos):
    raw = jnp.einsum(
        "qhd,khd->hqk", queries, key_rows, preferred_element_type=jnp.float32
    ) * queries.shape[-1] ** (-0.5)
    distance = query_pos[:, None] - key_pos[None, :]
    visible = (key_pos[None, :] >= 0) & (distance >= 0) & (distance < WINDOW)
    return jnp.where(visible[None], raw, -1e30)


def attend_forward(queries, key_rows, value_rows, query_pos, key_pos):
    scores = masked_scores(queries, key_rows, query_pos, key_pos)
    row_top = jnp.max(scores, axis=-1, keepdims=True)
    exponent = jnp.exp(scores - row_top)
    row_sum = jnp.sum(exponent, axis=-1, keepdims=True)
    soft_low = (exponent / row_sum).astype(jnp.bfloat16)
    attended = jnp.einsum("hqk,khd->qhd", soft_low, value_rows, preferred_element_type=jnp.float32)
    return (attended, row_top + jnp.log(row_sum))


def attend_backward(queries, key_rows, value_rows, query_pos, key_pos, log_sum, grad_attended):
    scores = masked_scores(queries, key_rows, query_pos, key_pos)
    soft = jnp.exp(scores - log_sum)
    soft_low = soft.astype(jnp.bfloat16)
    grad_soft = jnp.einsum(
        "qhd,khd->hqk", grad_attended, value_rows, preferred_element_type=jnp.float32
    )
    grad_values = jnp.einsum(
        "hqk,qhd->khd", soft_low, grad_attended, preferred_element_type=jnp.float32
    )
    grad_scores = (soft * (grad_soft - jnp.sum(soft * grad_soft, axis=-1, keepdims=True))).astype(
        jnp.bfloat16
    )
    scaling = queries.shape[-1] ** (-0.5)
    grad_queries = (
        jnp.einsum("hqk,khd->qhd", grad_scores, key_rows, preferred_element_type=jnp.float32)
        * scaling
    )
    grad_keys = (
        jnp.einsum("hqk,qhd->khd", grad_scores, queries, preferred_element_type=jnp.float32)
        * scaling
    )
    return (grad_queries, grad_keys, grad_values)


def ffn_forward(stream, weights):
    gain_full, gate_up_full, down_full = weights
    normed, inv_rms = norm_forward(stream, gain_full.astype(jnp.float32))
    acting = normed.astype(jnp.bfloat16)
    both_parts = expand(acting, gate_up_full)
    gate_pre = both_parts[:, 0]
    up_pre = both_parts[:, 1]
    hidden_low = (jax.nn.silu(gate_pre) * up_pre).astype(jnp.bfloat16)
    branch = tensor_forward_sum(product_t(hidden_low, down_full))
    return (stream + branch, (inv_rms, acting, gate_pre, up_pre, hidden_low))


def ffn_backward(grad_out, stream, saved_rows, weights):
    inv_rms, acting, gate_pre, up_pre, hidden_low = saved_rows
    gain_full, gate_up_full, down_full = weights
    grad_low = grad_out.astype(jnp.bfloat16)
    grad_hidden = product(grad_low, down_full)
    grad_down = product_tl(grad_low, hidden_low)
    grad_gate = grad_hidden * up_pre * silu_slope(gate_pre)
    grad_up = grad_hidden * jax.nn.silu(gate_pre)
    grad_both = jnp.stack([grad_gate, grad_up], axis=1).astype(jnp.bfloat16)
    grad_gate_up = weight_grad(acting, grad_both)
    grad_normed = tensor_backward_sum(contract(grad_both, gate_up_full))
    grad_input, grad_gain = norm_backward(
        stream, inv_rms, gain_full.astype(jnp.float32), grad_normed
    )
    return (grad_out + grad_input, layer_grads(grad_gain, grad_gate_up, grad_down))


def shards(
    hidden,
    teacher,
    valid_length,
    mamba_norm,
    mamba_in,
    conv_kernel,
    conv_bias,
    select_weight,
    step_weight,
    step_bias,
    decay_log,
    skip_gain,
    mamba_out,
    attn_norm,
    attn_qkv,
    attn_out,
    first_norm,
    first_gate_up,
    first_down,
    second_norm,
    second_gate_up,
    second_down,
):
    rows_here = hidden.shape[1]
    model_width = hidden.shape[2]
    seq_count = lax.axis_size("seq")
    seq_place = lax.axis_index("seq")
    my_length = valid_length[lax.axis_index("dp")]
    positions = seq_place * rows_here + jnp.arange(rows_here, dtype=jnp.int32)
    valid_rows = (positions < my_length).astype(jnp.float32)[:, None]
    total_valid = jnp.sum(valid_length).astype(jnp.float32)
    total_slots = valid_length.shape[0] * rows_here * seq_count
    stream_zero = hidden[0].astype(jnp.float32)
    mamba_weights = gather_layer(mamba_norm, mamba_in, mamba_out)
    gain_mamba, in_full, out_full = mamba_weights
    normed_mamba, inv_rms_mamba = norm_forward(stream_zero, gain_mamba.astype(jnp.float32))
    acting_mamba = normed_mamba.astype(jnp.bfloat16)
    projected = expand(acting_mamba, in_full).astype(jnp.bfloat16)
    conv_input = projected[:, 0]
    gate_input = projected[:, 1].astype(jnp.float32)
    tap_count = conv_kernel.shape[0]
    edge_rows = shifted(conv_input[rows_here - (tap_count - 1) :], "seq", 1)
    padded = jnp.concatenate([edge_rows, conv_input], axis=0).astype(jnp.float32)
    conv_pre = conv_bias
    for tap_index in range(tap_count):
        conv_pre = conv_pre + conv_kernel[tap_index] * padded[tap_index : tap_index + rows_here]
    inputs_low = jax.nn.silu(conv_pre).astype(jnp.bfloat16)
    inputs = inputs_low.astype(jnp.float32)
    selected = tensor_forward_sum(product(inputs_low, select_weight))
    step_rank = step_weight.shape[0]
    states = decay_log.shape[0]
    step_in = selected[:, :step_rank].astype(jnp.bfloat16)
    input_map = selected[:, step_rank : step_rank + states]
    output_map = selected[:, step_rank + states :]
    step_pre = product(step_in, step_weight) + step_bias
    step_size = jax.nn.softplus(step_pre)
    decay_rate = -jnp.exp(decay_log)
    core_local, decay_total, end_state = local_scan(
        inputs, step_size, input_map, output_map, decay_rate
    )
    arriving = jnp.zeros_like(end_state)
    leaving = end_state
    for relay_turn in range(seq_count - 1):
        arriving = shifted(leaving.astype(jnp.bfloat16), "seq", 1).astype(leaving.dtype)
        leaving = decay_total * arriving + end_state
    start_state = arriving
    scanned = (
        core_local + correction(step_size, output_map, decay_rate, start_state) + skip_gain * inputs
    )
    gate_silu = jax.nn.silu(gate_input)
    gated_low = (scanned * gate_silu).astype(jnp.bfloat16)
    stream_one = stream_zero + tensor_forward_sum(product_t(gated_low, out_full))
    attn_weights = gather_layer(attn_norm, attn_qkv, attn_out)
    gain_attn, qkv_full, attn_full = attn_weights
    normed_attn, inv_rms_attn = norm_forward(stream_one, gain_attn.astype(jnp.float32))
    acting_attn = normed_attn.astype(jnp.bfloat16)
    projected_attn = expand(acting_attn, qkv_full)
    head_dim = HD
    heads_here = projected_attn.shape[2] // head_dim
    cosine, sine_table = rope_tables(positions, head_dim)
    queries = rotate(
        projected_attn[:, 0].reshape(rows_here, heads_here, head_dim), cosine, sine_table
    ).astype(jnp.bfloat16)
    key_rows = rotate(
        projected_attn[:, 1].reshape(rows_here, heads_here, head_dim), cosine, sine_table
    ).astype(jnp.bfloat16)
    value_rows = projected_attn[:, 2].reshape(rows_here, heads_here, head_dim).astype(jnp.bfloat16)
    hop_count = min(seq_count - 1, (WINDOW - 2) // rows_here + 1)
    key_parts = [key_rows]
    value_parts = [value_rows]
    for hop_index in range(1, hop_count + 1):
        far_keys, far_values = shifted((key_rows, value_rows), "seq", hop_index)
        key_parts.insert(0, far_keys)
        value_parts.insert(0, far_values)
    all_keys = jnp.concatenate(key_parts, axis=0)
    all_values = jnp.concatenate(value_parts, axis=0)
    key_pos = (seq_place - hop_count) * rows_here + jnp.arange(
        (hop_count + 1) * rows_here, dtype=jnp.int32
    )
    per_half = heads_here // head_groups
    attended_parts = []
    log_parts = []
    for half_index in range(head_groups):
        lower = half_index * per_half
        attended_part, log_part = attend_forward(
            queries[:, lower : lower + per_half],
            all_keys[:, lower : lower + per_half],
            all_values[:, lower : lower + per_half],
            positions,
            key_pos,
        )
        attended_parts.append(attended_part)
        log_parts.append(log_part)
    attended_low = (
        jnp.concatenate(attended_parts, axis=1).reshape(rows_here, -1).astype(jnp.bfloat16)
    )
    stream_two = stream_one + tensor_forward_sum(product_t(attended_low, attn_full))
    first_weights = gather_layer(first_norm, first_gate_up, first_down)
    stream_three, first_saved = ffn_forward(stream_two, first_weights)
    second_weights = gather_layer(second_norm, second_gate_up, second_down)
    stream_four, second_saved = ffn_forward(stream_three, second_weights)
    residue = (stream_four - teacher[0].astype(jnp.float32)) * valid_rows
    local_loss = jnp.sum(residue * residue) / (model_width * total_valid)
    grad_four = residue * (total_slots / total_valid)
    second_weights = gather_again(second_norm, second_gate_up, second_down)
    grad_three, second_grads = ffn_backward(grad_four, stream_three, second_saved, second_weights)
    first_weights = gather_again(first_norm, first_gate_up, first_down)
    grad_two, first_grads = ffn_backward(grad_three, stream_two, first_saved, first_weights)
    attn_weights = gather_again(attn_norm, attn_qkv, attn_out)
    gain_attn, qkv_full, attn_full = attn_weights
    grad_low_attn = grad_two.astype(jnp.bfloat16)
    grad_attended = (
        product(grad_low_attn, attn_full)
        .astype(jnp.bfloat16)
        .reshape(rows_here, heads_here, head_dim)
    )
    grad_attn_out_w = product_tl(grad_low_attn, attended_low)
    query_grads = []
    key_grads = []
    value_grads = []
    for half_index in range(head_groups):
        lower = half_index * per_half
        grad_q_part, grad_k_part, grad_v_part = attend_backward(
            queries[:, lower : lower + per_half],
            all_keys[:, lower : lower + per_half],
            all_values[:, lower : lower + per_half],
            positions,
            key_pos,
            log_parts[half_index],
            grad_attended[:, lower : lower + per_half],
        )
        query_grads.append(grad_q_part)
        key_grads.append(grad_k_part)
        value_grads.append(grad_v_part)
    grad_queries = jnp.concatenate(query_grads, axis=1)
    grad_keys_all = jnp.concatenate(key_grads, axis=1)
    grad_values_all = jnp.concatenate(value_grads, axis=1)
    own_keys = grad_keys_all[hop_count * rows_here :]
    own_values = grad_values_all[hop_count * rows_here :]
    for hop_index in range(1, hop_count + 1):
        first_row = (hop_count - hop_index) * rows_here
        back_keys, back_values = (
            shifted(
                grad_keys_all[first_row : first_row + rows_here].astype(jnp.bfloat16),
                "seq",
                -hop_index,
            ).astype(jnp.float32),
            shifted(
                grad_values_all[first_row : first_row + rows_here].astype(jnp.bfloat16),
                "seq",
                -hop_index,
            ).astype(jnp.float32),
        )
        own_keys = own_keys + back_keys
        own_values = own_values + back_values
    grad_query_pre = rotate_back(round_trip(grad_queries), cosine, sine_table).reshape(
        rows_here, -1
    )
    grad_key_pre = rotate_back(round_trip(own_keys), cosine, sine_table).reshape(rows_here, -1)
    grad_value_pre = round_trip(own_values).reshape(rows_here, -1)
    grad_projected_attn = jnp.stack([grad_query_pre, grad_key_pre, grad_value_pre], axis=1).astype(
        jnp.bfloat16
    )
    grad_qkv_w = weight_grad(acting_attn, grad_projected_attn)
    grad_normed_attn = tensor_backward_sum(contract(grad_projected_attn, qkv_full))
    grad_in_attn, grad_gain_attn = norm_backward(
        stream_one, inv_rms_attn, gain_attn.astype(jnp.float32), grad_normed_attn
    )
    grad_one = grad_two + grad_in_attn
    attn_grads = layer_grads(grad_gain_attn, grad_qkv_w, grad_attn_out_w)
    mamba_weights = gather_again(mamba_norm, mamba_in, mamba_out)
    gain_mamba, in_full, out_full = mamba_weights
    grad_low_mamba = grad_one.astype(jnp.bfloat16)
    grad_gated = product(grad_low_mamba, out_full)
    grad_mamba_out_w = product_tl(grad_low_mamba, gated_low)
    grad_scanned = grad_gated * gate_silu
    grad_gate_input = grad_gated * scanned * silu_slope(gate_input)
    grad_skip = jnp.sum(grad_scanned * inputs, axis=0)
    incoming = incoming_grad(step_size, output_map, decay_rate, grad_scanned)
    arriving_grad = jnp.zeros_like(incoming)
    total_grad = incoming
    for relay_turn in range(seq_count - 1):
        arriving_grad = shifted(total_grad.astype(jnp.bfloat16), "seq", -1).astype(total_grad.dtype)
        total_grad = incoming + decay_total * arriving_grad

    def local_piece(inputs_in, sizes_in, in_map, out_map, rate_in):
        core_part, total_decay, last_state = local_scan(
            inputs_in, sizes_in, in_map, out_map, rate_in
        )
        return (
            core_part + jax.checkpoint(correction)(sizes_in, out_map, rate_in, start_state),
            total_decay,
            last_state,
        )

    unused, pullback = jax.vjp(local_piece, inputs, step_size, input_map, output_map, decay_rate)
    grad_inputs_scan, grad_sizes, grad_in_map, grad_out_map, grad_rates = pullback(
        (grad_scanned, arriving_grad * start_state, arriving_grad)
    )
    grad_decay_log = grad_rates * decay_rate
    grad_inputs = grad_inputs_scan + grad_scanned * skip_gain
    grad_step_pre = grad_sizes * jax.nn.sigmoid(step_pre)
    grad_step_bias = jnp.sum(grad_step_pre, axis=0)
    grad_step_low = grad_step_pre.astype(jnp.bfloat16)
    grad_step_weight = product_tl(step_in, grad_step_low)
    grad_step_in = product_t(grad_step_low, step_weight)
    grad_selected = tensor_backward_sum(
        jnp.concatenate([grad_step_in, grad_in_map, grad_out_map], axis=1)
    ).astype(jnp.bfloat16)
    grad_select = product_tl(inputs_low, grad_selected)
    grad_inputs = grad_inputs + product_t(grad_selected, select_weight)
    grad_conv_pre = grad_inputs * silu_slope(conv_pre)
    grad_conv_bias = jnp.sum(grad_conv_pre, axis=0)
    grad_kernel = jnp.stack(
        [
            jnp.sum(padded[tap_index : tap_index + rows_here] * grad_conv_pre, axis=0)
            for tap_index in range(tap_count)
        ]
    )
    grad_padded = sum(
        (
            jnp.pad(
                conv_kernel[tap_index] * grad_conv_pre,
                ((tap_index, tap_count - 1 - tap_index), (0, 0)),
            )
            for tap_index in range(tap_count)
        )
    )
    back_edge = shifted(grad_padded[: tap_count - 1], "seq", -1)
    grad_conv_input = grad_padded[tap_count - 1 :] + jnp.pad(
        back_edge, ((rows_here - (tap_count - 1), 0), (0, 0))
    )
    grad_projected = jnp.stack([grad_conv_input, grad_gate_input], axis=1).astype(jnp.bfloat16)
    grad_in_w = weight_grad(acting_mamba, grad_projected)
    grad_normed_mamba = tensor_backward_sum(contract(grad_projected, in_full))
    grad_in_mamba, grad_gain_mamba = norm_backward(
        stream_zero, inv_rms_mamba, gain_mamba.astype(jnp.float32), grad_normed_mamba
    )
    input_grad = grad_one + grad_in_mamba
    mamba_grads = layer_grads(grad_gain_mamba, grad_in_w, grad_mamba_out_w)
    small_sums = (
        lax.psum(grad_kernel.astype(jnp.bfloat16), ("dp", "seq")).astype(jnp.float32),
        lax.psum(grad_conv_bias.astype(jnp.bfloat16), ("dp", "seq")).astype(jnp.float32),
        lax.psum(grad_select.astype(jnp.bfloat16), ("dp", "seq")).astype(jnp.float32),
        lax.psum(grad_step_weight.astype(jnp.bfloat16), ("dp", "seq")).astype(jnp.float32),
        lax.psum(grad_step_bias.astype(jnp.bfloat16), ("dp", "seq")).astype(jnp.float32),
        lax.psum(grad_decay_log.astype(jnp.bfloat16), ("dp", "seq")).astype(jnp.float32),
        lax.psum(grad_skip.astype(jnp.bfloat16), ("dp", "seq")).astype(jnp.float32),
        lax.psum(local_loss.astype(jnp.bfloat16), ("dp", "seq")).astype(jnp.float32),
    )
    (
        sum_kernel,
        sum_conv_bias,
        sum_select,
        sum_step_weight,
        sum_step_bias,
        sum_decay_log,
        sum_skip,
        loss_total,
    ) = small_sums
    return (
        loss_total,
        stream_four.astype(jnp.bfloat16)[None],
        input_grad[None],
        mamba_grads[0],
        mamba_grads[1],
        sum_kernel,
        sum_conv_bias,
        sum_select,
        sum_step_weight,
        sum_step_bias,
        sum_decay_log,
        sum_skip,
        mamba_grads[2],
        attn_grads[0],
        attn_grads[1],
        attn_grads[2],
        first_grads[0],
        first_grads[1],
        first_grads[2],
        second_grads[0],
        second_grads[1],
        second_grads[2],
    )


def solution(mesh):
    placed = (
        P("dp", "seq", None),
        P("dp", "seq", None),
        P(),
        P(("dp", "seq")),
        P(("dp", "seq"), None, "tensor"),
        P(None, "tensor"),
        P("tensor"),
        P("tensor", None),
        P(None, "tensor"),
        P("tensor"),
        P(None, "tensor"),
        P("tensor"),
        P(("dp", "seq"), "tensor"),
        P(("dp", "seq")),
        P(("dp", "seq"), None, "tensor"),
        P(("dp", "seq"), "tensor"),
        P(("dp", "seq")),
        P(("dp", "seq"), None, "tensor"),
        P(("dp", "seq"), "tensor"),
        P(("dp", "seq")),
        P(("dp", "seq"), None, "tensor"),
        P(("dp", "seq"), "tensor"),
    )
    return jax.shard_map(
        shards,
        mesh=mesh,
        in_specs=placed,
        out_specs=(
            P(),
            P("dp", "seq", None),
            P("dp", "seq", None),
            P(("dp", "seq")),
            P(("dp", "seq"), None, "tensor"),
            P(None, "tensor"),
            P("tensor"),
            P("tensor", None),
            P(None, "tensor"),
            P("tensor"),
            P(None, "tensor"),
            P("tensor"),
            P(("dp", "seq"), "tensor"),
            P(("dp", "seq")),
            P(("dp", "seq"), None, "tensor"),
            P(("dp", "seq"), "tensor"),
            P(("dp", "seq")),
            P(("dp", "seq"), None, "tensor"),
            P(("dp", "seq"), "tensor"),
            P(("dp", "seq")),
            P(("dp", "seq"), None, "tensor"),
            P(("dp", "seq"), "tensor"),
        ),
        check_vma=False,
    )
```

profile of v0, /device:TPU:0, one launch (start us, length us, event | category | flops | bytes accessed | tf_op | source)
XLA Modules:
  0.0 3026.4 jit_solution(8343954388791611145)
XLA Ops:
  10.0 14.8 all-gather
  26.0 41.6 %all-gather.13.cloned.1.call-done = bf16[2048,2,1024]{2,0,1:T(8,128)(2,1)} async-done(((bf16[256,2,1024]{2,0,1:T(8,128)(2,1)}), bf16[2048,2,1024]{2,0,1:T(8,128)(2,1)}) %all-gather.13.cloned.1.call-update) | async-done | bytes 8388624 | tf_op jit(solution)/shard_map/all_gather | solution.py:74
  90.6 32.1 %all-reduce.195.cloned.1.call-done = bf16[528,160]{0,1:T(8,128)(2,1)} async-done(((bf16[528,160]{0,1:T(8,128)(2,1)}), bf16[528,160]{0,1:T(8,128)(2,1)}) %all-reduce.195.cloned.1.call-update) | async-done | bytes 168976 | tf_op jit(solution)/shard_map/psum | solution.py:102
  133.9 245.7 %while.51 = (s32[]{:T(128)}, f32[16,1024]{1,0:T(8,128)S(1)}, f32[16,33,1024]{2,1,0:T(8,128)}, f32[16,33,1024]{2,1,0:T(8,128)}, f32[16,1024]{1,0:T(8,128)S(1)}, /...) while((s32[]{:T(128)}, f32[16,1024]{1,0:T(8,128)S(1)}, ...), condition=%wide.region_36.37_spmd.clone, body=%wide.region_2.36_spmd.clone.sunk | while | flops 4849699 | bytes 4099164 | solution.py:163
  412.3 20.2 multiply_reduce_fusion.173
  443.1 12.6 all-gather.1
  456.2 73.1 %all-reduce.197.cloned.1.call-done = bf16[528,2048]{1,0:T(8,128)(2,1)} async-done(((bf16[528,2048]{1,0:T(8,128)(2,1)}), bf16[528,2048]{1,0:T(8,128)(2,1)}) %all-reduce.197.cloned.1.call-update) | async-done | bytes 2162704 | tf_op jit(solution)/shard_map/psum | solution.py:102
  532.2 43.3 %all-gather.17.cloned.1.call-done = bf16[2048,3,512]{2,0,1:T(8,128)(2,1)} async-done(((bf16[256,3,512]{2,0,1:T(8,128)(2,1)}), bf16[2048,3,512]{2,0,1:T(8,128)(2,1)}) %all-gather.17.cloned.1.call-update) | async-done | bytes 6291472 | tf_op jit(solution)/shard_map/all_gather | solution.py:74
  618.1 25.8 collective-permute-done.8
  649.2 12.4 fusion.276
  723.3 15.2 all-gather.2
  738.5 71.1 %all-reduce.199.cloned.1.call-done = bf16[528,2048]{1,0:T(8,128)(2,1)} async-done(((bf16[528,2048]{1,0:T(8,128)(2,1)}), bf16[528,2048]{1,0:T(8,128)(2,1)}) %all-reduce.199.cloned.1.call-update) | async-done | bytes 2162704 | tf_op jit(solution)/shard_map/psum | solution.py:102
  815.6 85.6 %all-gather.21.cloned.1.call-done = bf16[2048,2,2048]{2,0,1:T(8,128)(2,1)} async-done(((bf16[256,2,2048]{2,0,1:T(8,128)(2,1)}), bf16[2048,2,2048]{2,0,1:T(8,128)(2,1)}) %all-gather.21.cloned.1.call-update) | async-done | bytes 16777232 | tf_op jit(solution)/shard_map/all_gather | solution.py:74
  901.2 13.5 fusion.241
  919.4 38.2 %all-gather.23.cloned.1.call-done = bf16[2048,2048]{1,0:T(8,128)(2,1)} async-done(((bf16[256,2048]{1,0:T(8,128)(2,1)}), bf16[2048,2048]{1,0:T(8,128)(2,1)}) %all-gather.23.cloned.1.call-update) | async-done | bytes 8388624 | tf_op jit(solution)/shard_map/all_gather | solution.py:75
  971.3 13.7 all-gather.3
  985.1 71.1 %all-reduce.201.cloned.1.call-done = bf16[528,2048]{1,0:T(8,128)(2,1)} async-done(((bf16[528,2048]{1,0:T(8,128)(2,1)}), bf16[528,2048]{1,0:T(8,128)(2,1)}) %all-reduce.201.cloned.1.call-update) | async-done | bytes 2162704 | tf_op jit(solution)/shard_map/psum | solution.py:102
  1061.6 85.9 %all-gather.25.cloned.1.call-done = bf16[2048,2,2048]{2,0,1:T(8,128)(2,1)} async-done(((bf16[256,2,2048]{2,0,1:T(8,128)(2,1)}), bf16[2048,2,2048]{2,0,1:T(8,128)(2,1)}) %all-gather.25.cloned.1.call-update) | async-done | bytes 16777232 | tf_op jit(solution)/shard_map/all_gather | solution.py:74
  1147.5 13.5 fusion.238
  1165.7 37.9 %all-gather.27.cloned.1.call-done = bf16[2048,2048]{1,0:T(8,128)(2,1)} async-done(((bf16[256,2048]{1,0:T(8,128)(2,1)}), bf16[2048,2048]{1,0:T(8,128)(2,1)}) %all-gather.27.cloned.1.call-update) | async-done | bytes 8388624 | tf_op jit(solution)/shard_map/all_gather | solution.py:75
  1215.8 86.5 %all-reduce.203.cloned.1.call-done = bf16[528,2048]{1,0:T(8,128)(2,1)} async-done(((bf16[528,2048]{1,0:T(8,128)(2,1)}), bf16[528,2048]{1,0:T(8,128)(2,1)}) %all-reduce.203.cloned.1.call-update) | async-done | bytes 2162704 | tf_op jit(solution)/shard_map/psum | solution.py:102
  1308.8 12.1 fusion.192
  1322.9 13.8 bitcast_convert_fusion.3
  1336.9 88.0 %all-reduce.205.cloned.1.call-done = bf16[528,2048]{1,0:T(8,128)(2,1)} async-done(((bf16[528,2048]{1,0:T(8,128)(2,1)}), bf16[528,2048]{1,0:T(8,128)(2,1)}) %all-reduce.205.cloned.1.call-update) | async-done | bytes 2162704 | tf_op jit(solution)/shard_map/psum | solution.py:106
  1434.4 12.1 fusion.193
  1447.8 14.4 bitcast_convert_fusion.2
  1462.7 87.8 %all-reduce.207.cloned.1.call-done = bf16[528,2048]{1,0:T(8,128)(2,1)} async-done(((bf16[528,2048]{1,0:T(8,128)(2,1)}), bf16[528,2048]{1,0:T(8,128)(2,1)}) %all-reduce.207.cloned.1.call-update) | async-done | bytes 2162704 | tf_op jit(solution)/shard_map/psum | solution.py:106
  1571.7 13.4 multiply_reduce_fusion.165
  1594.2 12.9 multiply_reduce_fusion.166
  1613.2 17.1 multiply_convert_fusion.1
  1681.0 12.4 collective-permute-done.11
  1706.7 148.6 %while.52 = (s32[]{:T(128)}, f32[16,1024]{1,0:T(8,128)S(1)}, f32[16,16,1024]{2,1,0:T(8,128)}, f32[16,33,1024]{2,1,0:T(8,128)}, f32[16,1024]{1,0:T(8,128)S(1)}, /...) while((s32[]{:T(128)}, f32[16,1024]{1,0:T(8,128)S(1)}, ...), condition=%wide.region_67.68_spmd.clone, body=%wide.region_66.67_spmd.clone.sunk | while | flops 2229283 | bytes 1551692 | solution.py:163
  1892.7 29.4 multiply_reduce_fusion.168
  1958.1 228.7 %while.53 = (s32[]{:T(128)}, f32[16,1024]{1,0:T(8,128)S(1)}, f32[16,1024]{1,0:T(8,128)S(1)}, f32[16,33,1024]{2,1,0:T(8,128)}, f32[16,33,1024]{2,1,0:T(8,128)}, /...) while((s32[]{:T(128)}, f32[16,1024]{1,0:T(8,128)S(1)}, ...), condition=%wide.region_201.202_spmd.clone, body=%wide.region_68.201_spmd.clone.sunk | while | flops 19990500 | bytes 11767131 | solution.py:163
  2205.6 27.7 all-reduce.211.cloned.1.call-done
  2263.9 11.3 convolution_convert_fusion.2
  2296.7 11.2 convolution_convert_fusion.3
  2320.0 19.9 convolution_convert_fusion
  2340.6 19.9 convolution_convert_fusion.1
  2368.7 59.9 %all-reduce.213.cloned.1.call-done = bf16[528,2048]{1,0:T(8,128)(2,1)} async-done(((bf16[528,2048]{1,0:T(8,128)(2,1)}), bf16[528,2048]{1,0:T(8,128)(2,1)}) %all-reduce.213.cloned.1.call-update) | async-done | bytes 2162704 | tf_op jit(solution)/shard_map/psum | solution.py:106
  2431.8 28.4 all-reduce.181
  2472.8 29.9 reduce-scatter.23.cloned.1.call-done
  2505.5 52.5 %reduce-scatter.11.cloned.1.call-done = bf16[256,1024]{1,0:T(8,128)(2,1)} async-done(((bf16[2048,1024]{1,0:T(8,128)(2,1)}), bf16[256,1024]{1,0:T(8,128)(2,1)}) %reduce-scatter.11.cloned.1.call-update) | async-done | bytes 524304 | tf_op jit(solution)/shard_map/reduce_scatter | solution.py:95
  2560.1 63.4 %reduce-scatter.13.cloned.1.call-done = bf16[256,3,512]{2,0,1:T(8,128)(2,1)} async-done(((bf16[2048,3,512]{2,0,1:T(8,128)(2,1)}), bf16[256,3,512]{2,0,1:T(8,128)(2,1)}) %reduce-scatter.13.cloned.1.call-update) | async-done | bytes 786448 | tf_op jit(solution)/shard_map/reduce_scatter | solution.py:92
  2626.1 72.1 %reduce-scatter.19.cloned.1.call-done = bf16[256,2048]{1,0:T(8,128)(2,1)} async-done(((bf16[2048,2048]{1,0:T(8,128)(2,1)}), bf16[256,2048]{1,0:T(8,128)(2,1)}) %reduce-scatter.19.cloned.1.call-update) | async-done | bytes 1048592 | tf_op jit(solution)/shard_map/reduce_scatter | solution.py:95
  2701.0 72.4 %reduce-scatter.9.cloned.1.call-done = bf16[256,2,1024]{2,0,1:T(8,128)(2,1)} async-done(((bf16[2048,2,1024]{2,0,1:T(8,128)(2,1)}), bf16[256,2,1024]{2,0,1:T(8,128)(2,1)}) %reduce-scatter.9.cloned.1.call-update) | async-done | bytes 1048592 | tf_op jit(solution)/shard_map/reduce_scatter | solution.py:92
  2776.9 115.8 %reduce-scatter.21.cloned.1.call-done = bf16[256,2,2048]{2,0,1:T(8,128)(2,1)} async-done(((bf16[2048,2,2048]{2,0,1:T(8,128)(2,1)}), bf16[256,2,2048]{2,0,1:T(8,128)(2,1)}) %reduce-scatter.21.cloned.1.call-update) | async-done | bytes 2097168 | tf_op jit(solution)/shard_map/reduce_scatter | solution.py:92
  2898.5 113.6 %reduce-scatter.17.cloned.1.call-done = bf16[256,2,2048]{2,0,1:T(8,128)(2,1)} async-done(((bf16[2048,2,2048]{2,0,1:T(8,128)(2,1)}), bf16[256,2,2048]{2,0,1:T(8,128)(2,1)}) %reduce-scatter.17.cloned.1.call-update) | async-done | bytes 2097168 | tf_op jit(solution)/shard_map/reduce_scatter | solution.py:92
  (2920 shorter events, 1172.0 us)
Async XLA Ops:
  7.2 60.4 %all-gather.13.cloned.1.call-start = ((), (), s32[]{:S(2)}) async-start(), calls=%async_computation.8 | async-start | bytes 9437184 | tf_op jit(solution)/shard_map/all_gather | solution.py:74
  9.9 112.8 %all-reduce.195.cloned.1.call-start = ((), (), s32[]{:S(2)}) async-start(), calls=%async_computation.9 | async-start | bytes 409600 | tf_op jit(solution)/shard_map/psum | solution.py:102
  76.2 4.9 collective-permute-start
  86.5 348.2 %all-gather.15.cloned.1.call-start = ((), (), s32[]{:S(2)}) async-start(), calls=%async_computation.10 | async-start | bytes 4718592 | tf_op jit(solution)/shard_map/all_gather | solution.py:75
  87.3 442.0 %all-reduce.197.cloned.1.call-start = ((), (), s32[]{:S(2)}) async-start(), calls=%async_computation.11 | async-start | bytes 4325376 | tf_op jit(solution)/shard_map/psum | solution.py:102
  379.7 11.4 collective-permute-start.1
  391.1 8.4 collective-permute-start.2
  399.6 12.6 collective-permute-start.3
  441.8 133.7 %all-gather.17.cloned.1.call-start = ((), (), s32[]{:S(2)}) async-start(), calls=%async_computation.12 | async-start | bytes 7077888 | tf_op jit(solution)/shard_map/all_gather | solution.py:74
  442.4 271.4 %all-gather.19.cloned.1.call-start = ((), (), s32[]{:S(2)}) async-start(), calls=%async_computation.13 | async-start | bytes 2359296 | tf_op jit(solution)/shard_map/all_gather | solution.py:75
  442.9 366.7 %all-reduce.199.cloned.1.call-start = ((), (), s32[]{:S(2)}) async-start(), calls=%async_computation.14 | async-start | bytes 4325376 | tf_op jit(solution)/shard_map/psum | solution.py:102
  594.9 21.0 collective-permute-start.7
  599.1 44.8 %collective-permute-start.8 = (bf16[528,8,64]{0,2,1:T(8,128)(2,1)}, bf16[528,8,64]{0,2,1:T(8,128)(2,1)}, u32[]{:S(2)}, u32[]{:S(2)}) collective-permute-start(bf16[528,8,64]{0,2,1:T(8,128)(2,1)} %pad_maximum_fusion.15), channel_id=1, source_target_pairs={{0,8},{4,12},{1,9},{5,13},{2,10},{6,14},{3,11},{7,15},{16,24},{20,... | collective-permute-start | bytes 1622024 | tf_op jit(solution)/shard_map/ppermute | solution.py:18
  601.3 42.6 %collective-permute-start.9 = (bf16[528,8,64]{0,2,1:T(8,128)(2,1)}, bf16[528,8,64]{0,2,1:T(8,128)(2,1)}, u32[]{:S(2)}, u32[]{:S(2)}) collective-permute-start(bf16[528,8,64]{0,2,1:T(8,128)(2,1)} %pad_maximum_fusion.15), channel_id=1, source_target_pairs={{0,4},{4,8},{8,12},{1,5},{5,9},{9,13},{2,6},{6,10},{10,14},{3,7},{... | collective-permute-start | bytes 1622024 | tf_op jit(solution)/shard_map/ppermute | solution.py:18
  609.6 69.6 %collective-permute-start.4 = (bf16[528,8,64]{0,2,1:T(8,128)(2,1)S(1)}, bf16[528,8,64]{0,2,1:T(8,128)(2,1)}, u32[]{:S(2)}, u32[]{:S(2)}) collective-permute-start(bf16[528,8,64]{0,2,1:T(8,128)(2,1)S(1)} %bitcast.1844), channel_id=1, source_target_pairs={{0,12},{1,13},{2,14},{3,15},{16,28},{17,29},{18,30},{19,31}} | collective-permute-start | bytes 1622024 | tf_op jit(solution)/shard_map/ppermute | solution.py:18
  611.8 67.5 %collective-permute-start.5 = (bf16[528,8,64]{0,2,1:T(8,128)(2,1)S(1)}, bf16[528,8,64]{0,2,1:T(8,128)(2,1)}, u32[]{:S(2)}, u32[]{:S(2)}) collective-permute-start(bf16[528,8,64]{0,2,1:T(8,128)(2,1)S(1)} %bitcast.1845), channel_id=1, source_target_pairs={{0,8},{4,12},{1,9},{5,13},{2,10},{6,14},{3,11},{7,15},{16,24},{20,... | collective-permute-start | bytes 1622024 | tf_op jit(solution)/shard_map/ppermute | solution.py:18
  615.8 63.5 %collective-permute-start.6 = (bf16[528,8,64]{0,2,1:T(8,128)(2,1)S(1)}, bf16[528,8,64]{0,2,1:T(8,128)(2,1)}, u32[]{:S(2)}, u32[]{:S(2)}) collective-permute-start(bf16[528,8,64]{0,2,1:T(8,128)(2,1)S(1)} %bitcast.1846), channel_id=1, source_target_pairs={{0,4},{4,8},{8,12},{1,5},{5,9},{9,13},{2,6},{6,10},{10,14},{3,7},{... | collective-permute-start | bytes 1622024 | tf_op jit(solution)/shard_map/ppermute | solution.py:18
  718.6 182.6 %all-gather.21.cloned.1.call-start = ((), (), s32[]{:S(2)}) async-start(), calls=%async_computation.15 | async-start | bytes 18874368 | tf_op jit(solution)/shard_map/all_gather | solution.py:74
  722.5 235.2 %all-gather.23.cloned.1.call-start = ((), (), s32[]{:S(2)}) async-start(), calls=%async_computation.16 | async-start | bytes 9437184 | tf_op jit(solution)/shard_map/all_gather | solution.py:75
  723.2 333.0 %all-reduce.201.cloned.1.call-start = ((), (), s32[]{:S(2)}) async-start(), calls=%async_computation.17 | async-start | bytes 4325376 | tf_op jit(solution)/shard_map/psum | solution.py:102
  738.5 816.9 %copy-start.88 = (f32[8,1,256]{2,1,0:T(1,128)}, f32[8,1,256]{2,1,0:T(1,128)S(1)}, u32[]{:S(2)}) copy-start(f32[8,1,256]{2,1,0:T(1,128)S(1)} %convert_element_type.520) | copy-start | bytes 24580
  966.9 180.6 %all-gather.25.cloned.1.call-start = ((), (), s32[]{:S(2)}) async-start(), calls=%async_computation.18 | async-start | bytes 18874368 | tf_op jit(solution)/shard_map/all_gather | solution.py:74
  970.7 233.0 %all-gather.27.cloned.1.call-start = ((), (), s32[]{:S(2)}) async-start(), calls=%async_computation.19 | async-start | bytes 9437184 | tf_op jit(solution)/shard_map/all_gather | solution.py:75
  971.3 331.0 %all-reduce.203.cloned.1.call-start = ((), (), s32[]{:S(2)}) async-start(), calls=%async_computation.20 | async-start | bytes 4325376 | tf_op jit(solution)/shard_map/psum | solution.py:102
  1213.0 211.9 %all-reduce.205.cloned.1.call-start = ((), (), s32[]{:S(2)}) async-start(), calls=%async_computation.21 | async-start | bytes 4325376 | tf_op jit(solution)/shard_map/psum | solution.py:106
  1336.7 213.8 %all-reduce.207.cloned.1.call-start = ((), (), s32[]{:S(2)}) async-start(), calls=%async_computation.22 | async-start | bytes 4325376 | tf_op jit(solution)/shard_map/psum | solution.py:106
  1462.2 393.1 %all-reduce.209.cloned.1.call-start = ((), (), s32[]{:S(2)}) async-start(), calls=%async_computation.23 | async-start | bytes 4325376 | tf_op jit(solution)/shard_map/psum | solution.py:106
  1609.2 57.0 %collective-permute-start.15 = (bf16[528,8,64]{0,2,1:T(8,128)(2,1)}, bf16[528,8,64]{0,2,1:T(8,128)(2,1)S(1)}, u32[]{:S(2)}, u32[]{:S(2)}) collective-permute-start(bf16[528,8,64]{0,2,1:T(8,128)(2,1)} %get-tuple-element.1587), channel_id=1, source_target_pairs={{12,0},{13,1},{14,2},{15,3},{28,16},{29,17},{30,18},{31,19}} | collective-permute-start | bytes 1622024 | tf_op jit(solution)/shard_map/ppermute | solution.py:18
  1610.5 63.1 %collective-permute-start.14 = (bf16[528,8,64]{0,2,1:T(8,128)(2,1)}, bf16[528,8,64]{0,2,1:T(8,128)(2,1)}, u32[]{:S(2)}, u32[]{:S(2)}) collective-permute-start(bf16[528,8,64]{0,2,1:T(8,128)(2,1)} %get-tuple-element.1588), channel_id=1, source_target_pairs={{8,0},{12,4},{9,1},{13,5},{10,2},{14,6},{11,3},{15,7},{24,16},{28,... | collective-permute-start | bytes 1622024 | tf_op jit(solution)/shard_map/ppermute | solution.py:18
  1611.8 61.8 %collective-permute-start.13 = (bf16[528,8,64]{0,2,1:T(8,128)(2,1)}, bf16[528,8,64]{0,2,1:T(8,128)(2,1)}, u32[]{:S(2)}, u32[]{:S(2)}) collective-permute-start(bf16[528,8,64]{0,2,1:T(8,128)(2,1)} %get-tuple-element.1586), channel_id=1, source_target_pairs={{4,0},{8,4},{12,8},{5,1},{9,5},{13,9},{6,2},{10,6},{14,10},{7,3},{... | collective-permute-start | bytes 1622024 | tf_op jit(solution)/shard_map/ppermute | solution.py:18
  1657.4 23.6 collective-permute-start.12
  1658.8 34.6 %collective-permute-start.11 = (bf16[528,8,64]{0,2,1:T(8,128)(2,1)}, bf16[528,8,64]{0,2,1:T(8,128)(2,1)}, u32[]{:S(2)}, u32[]{:S(2)}) collective-permute-start(bf16[528,8,64]{0,2,1:T(8,128)(2,1)} %get-tuple-element.1585), channel_id=1, source_target_pairs={{8,0},{12,4},{9,1},{13,5},{10,2},{14,6},{11,3},{15,7},{24,16},{28,... | collective-permute-start | bytes 1622024 | tf_op jit(solution)/shard_map/ppermute | solution.py:18
  1666.2 27.2 collective-permute-start.10
  1706.4 526.8 %all-reduce.211.cloned.1.call-start = ((), (), s32[]{:S(2)}) async-start(), calls=%async_computation.24 | async-start | bytes 540672 | tf_op jit(solution)/shard_map/psum | solution.py:106
  1878.6 54.5 %collective-permute-start.16 = (bf16[16,1024]{1,0:T(8,128)(2,1)S(1)}, bf16[16,1024]{1,0:T(8,128)(2,1)S(1)}, u32[]{:S(2)}, u32[]{:S(2)}) collective-permute-start(bf16[16,1024]{1,0:T(8,128)(2,1)S(1)} %fusion.243), channel_id=1, source_target_pairs={{4,0},{8,4},{12,8},{5,1},{9,5},{13,9},{6,2},{10,6},{14,10},{7,3},{... | collective-permute-start | bytes 98312 | tf_op jit(solution)/shard_map/ppermute | solution.py:18
  1933.1 7.6 collective-permute-start.17
  1940.8 13.6 collective-permute-start.18
  2195.5 167.6 %reduce-scatter.15.cloned.1.call-start = ((), (), s32[]{:S(2)}) async-start(), calls=%async_computation.29 | async-start | bytes 2359296 | tf_op jit(solution)/shard_map/reduce_scatter | solution.py:95
  2201.5 163.4 %all-reduce.215.cloned.1.call-start = ((), (), s32[]{:S(2)}) async-start(), calls=%async_computation.34 | async-start | bytes 1179648 | tf_op jit(solution)/shard_map/psum | solution.py:539
  2242.4 8.2 collective-permute-start.19
  2250.6 178.0 %all-reduce.213.cloned.1.call-start = ((), (), s32[]{:S(2)}) async-start(), calls=%async_computation.25 | async-start | bytes 4325376 | tf_op jit(solution)/shard_map/psum | solution.py:106
  2263.4 239.3 %reduce-scatter.23.cloned.1.call-start = ((), (), s32[]{:S(2)}) async-start(), calls=%async_computation.33 | async-start | bytes 9437184 | tf_op jit(solution)/shard_map/reduce_scatter | solution.py:95
  2275.3 282.7 %reduce-scatter.11.cloned.1.call-start = ((), (), s32[]{:S(2)}) async-start(), calls=%async_computation.27 | async-start | bytes 4718592 | tf_op jit(solution)/shard_map/reduce_scatter | solution.py:95
  2285.1 338.5 %reduce-scatter.13.cloned.1.call-start = ((), (), s32[]{:S(2)}) async-start(), calls=%async_computation.28 | async-start | bytes 7077888 | tf_op jit(solution)/shard_map/reduce_scatter | solution.py:92
  2296.4 401.7 %reduce-scatter.19.cloned.1.call-start = ((), (), s32[]{:S(2)}) async-start(), calls=%async_computation.31 | async-start | bytes 9437184 | tf_op jit(solution)/shard_map/reduce_scatter | solution.py:95
  2307.9 465.4 %reduce-scatter.9.cloned.1.call-start = ((), (), s32[]{:S(2)}) async-start(), calls=%async_computation.26 | async-start | bytes 9437184 | tf_op jit(solution)/shard_map/reduce_scatter | solution.py:92
  2319.3 573.5 %reduce-scatter.21.cloned.1.call-start = ((), (), s32[]{:S(2)}) async-start(), calls=%async_computation.32 | async-start | bytes 18874368 | tf_op jit(solution)/shard_map/reduce_scatter | solution.py:92
  2339.9 672.2 %reduce-scatter.17.cloned.1.call-start = ((), (), s32[]{:S(2)}) async-start(), calls=%async_computation.30 | async-start | bytes 18874368 | tf_op jit(solution)/shard_map/reduce_scatter | solution.py:92
  (159 other events, 5132.6 us)
Sparse Core Ops, SparseCore 0:
  10.5 57.0 all-gather.12
  86.7 36.0 all-reduce.194
  124.8 36.7 all-gather.14
  441.9 87.3 all-reduce.196
  531.0 44.4 all-gather.16
  577.3 27.8 all-gather.18
  718.7 90.8 all-reduce.198
  812.3 88.8 all-gather.20
  903.2 54.3 all-gather.22
  967.0 89.0 all-reduce.200
  1058.7 88.8 all-gather.24
  1149.3 54.3 all-gather.26
  1213.1 89.1 all-reduce.202
  1336.8 88.0 all-reduce.204
  1462.4 88.0 all-reduce.206
  1706.5 88.8 all-reduce.208
  2195.6 37.5 all-reduce.210
  2236.9 41.1 reduce-scatter.14
  2282.3 55.0 all-reduce.214
  2340.2 88.3 all-reduce.212
  2432.4 70.2 reduce-scatter.22
  2506.7 51.3 reduce-scatter.10
  2561.8 61.7 reduce-scatter.12
  2626.9 71.2 reduce-scatter.18
  2702.0 71.2 reduce-scatter.8
  2776.7 115.9 reduce-scatter.20
  2896.2 115.9 reduce-scatter.16
where the time goes:
time: 3060 us; the launch traced here: 3030 us
  waiting for transfers between devices  1500 us (49%)
  other arithmetic  527 us (17%)
  local copies, waits for them, and re-layouts  464 us (15%)
  matrix products  366 us (12%)
  blocking collectives  84.8 us (3%)
  starting transfers between devices  46.5 us (2%)
    reduce_scatter x4, waiting for transfers between devices, layer_grads(): lax.psum_scatter(first_grad.astype(jnp.bfloat16), ('dp', 'seq'), scatter_...  365 us
    psum x5, waiting for transfers between devices, tensor_forward_sum(): lax.psum(partial_sum.astype(jnp.bfloat16), 'tensor').astype(jnp.float32)  334 us
    psum x5, waiting for transfers between devices, tensor_backward_sum(): lax.psum(partial_sum.astype(jnp.bfloat16), 'tensor').astype(jnp.float32)  263 us
    all_gather x4, waiting for transfers between devices, gather_layer(): lax.all_gather(first_matrix, ('dp', 'seq'), axis=0, tiled=True)  256 us
    reduce_scatter x4, waiting for transfers between devices, layer_grads(): lax.psum_scatter(second_grad.astype(jnp.bfloat16), ('dp', 'seq'), scatter...  155 us
    reduce_sum x176, other arithmetic, advance(): outputs.append(jnp.sum(out_rows[position][:, None] * carried, axis=0))  98.4 us
    slice x64, local copies, waits for them, and re-layouts, advance(): value_rows[position]  87.5 us
    slice x96, local copies, waits for them, and re-layouts, advance(): size_rows[position][None, :] * decay_rate  87.4 us
  transfers between devices with their start and end apart: 47, of which 28 were waited for; matrix products, arithmetic and copies ran while one was open for 29% of the time, Pallas kernels for 0%

commit v1 on v0

v1 whole, which is shorter than its diff:
```python
import functools

import jax
import jax.numpy as jnp
from jax import lax
from jax.experimental import pallas as pl
from jax.experimental.pallas import tpu as pltpu
from jax.sharding import PartitionSpec as P

HD = 64
WINDOW = 2048
F32 = jnp.float32
BF16 = jnp.bfloat16
MESH = pl.DeviceIdType.MESH
LOG2E = 1.4426950408889634
LN2 = 0.6931471805599453

epsilon = 1e-05


def lasting(microseconds):
    return pl.CostEstimate(flops=int(microseconds * 1e7), bytes_accessed=0, transcendentals=0)

head_groups = 2


def state_kernel(dt_ref, dtx_ref, b_ref, rate_ref, out_ref, *, wide, chunk):
    @pl.when(pl.program_id(0) == 0)
    def _():
        out_ref[...] = jnp.zeros_like(out_ref)
    for j in range(out_ref.shape[1] // wide):
        cols = pl.ds(j * wide, wide)
        rate = rate_ref[:, cols]
        def group(g, h):
            base = pl.multiple_of(g * 8, 8)
            dts = dt_ref[pl.ds(base, 8), cols]
            dtxs = dtx_ref[pl.ds(base, 8), cols]
            for r in range(8):
                b = b_ref[base + r]
                b = jnp.concatenate([b] * (wide // 128), axis=1)
                h = jnp.exp2(dts[r:r+1] * rate) * h + b * dtxs[r:r+1]
            return h
        out_ref[:, cols] = lax.fori_loop(0, chunk // 8, group, out_ref[:, cols])

def scan_kernel(dt_ref, dtx_ref, b_ref, c_ref, rate_ref, h0_ref, y_ref, hp_ref, h_ref, *, wide, chunk):
    @pl.when(pl.program_id(0) == 0)
    def _():
        h_ref[...] = h0_ref[...]
    for j in range(h_ref.shape[1] // wide):
        cols = pl.ds(j * wide, wide)
        rate = rate_ref[:, cols]
        def group(g, h):
            base = pl.multiple_of(g * 8, 8)
            dts = dt_ref[pl.ds(base, 8), cols]
            dtxs = dtx_ref[pl.ds(base, 8), cols]
            ys = []
            for r in range(8):
                b = jnp.concatenate([b_ref[base + r]] * (wide // 128), axis=1)
                c = jnp.concatenate([c_ref[base + r]] * (wide // 128), axis=1)
                hp_ref[base + r, :, cols] = h
                h = jnp.exp2(dts[r:r+1] * rate) * h + b * dtxs[r:r+1]
                ys.append(jnp.sum(c * h, axis=0, keepdims=True))
            y_ref[pl.ds(base, 8), cols] = jnp.concatenate(ys, axis=0)
            return h
        h_ref[:, cols] = lax.fori_loop(0, chunk // 8, group, h_ref[:, cols])

def back_state_kernel(dt_ref, g_ref, c_ref, rate_ref, out_ref, *, wide, chunk):
    @pl.when(pl.program_id(0) == 0)
    def _():
        out_ref[...] = jnp.zeros_like(out_ref)
    for j in range(out_ref.shape[1] // wide):
        cols = pl.ds(j * wide, wide)
        rate = rate_ref[:, cols]
        def group(g, carry):
            base = pl.multiple_of(chunk - 8 - g * 8, 8)
            dts = dt_ref[pl.ds(base, 8), cols]
            gs = g_ref[pl.ds(base, 8), cols]
            for r in reversed(range(8)):
                c = jnp.concatenate([c_ref[base + r]] * (wide // 128), axis=1)
                carry = jnp.exp2(dts[r:r+1] * rate) * (carry + c * gs[r:r+1])
            return carry
        out_ref[:, cols] = lax.fori_loop(0, chunk // 8, group, out_ref[:, cols])

def back_kernel(dt_ref, x_ref, g_ref, b_ref, c_ref, rate_ref, hp_ref, l0_ref,
                gdt_ref, gx_ref, gb_out, gc_out, grate_ref, l_ref, gb_ref, gc_ref, *, wide, chunk):
    @pl.when(pl.program_id(0) == 0)
    def _():
        l_ref[...] = l0_ref[...]
        grate_ref[...] = jnp.zeros_like(grate_ref)
    for j in range(l_ref.shape[1] // wide):
        cols = pl.ds(j * wide, wide)
        rate = rate_ref[:, cols]
        def fold(v):
            out = v[:, :128]
            for i in range(1, wide // 128):
                out = out + v[:, i * 128:(i + 1) * 128]
            return out
        def group(g, state):
            carry, grate = state
            base = pl.multiple_of(chunk - 8 - g * 8, 8)
            dts = dt_ref[pl.ds(base, 8), cols]
            xs = x_ref[pl.ds(base, 8), cols].astype(F32)
            gs = g_ref[pl.ds(base, 8), cols]
            dtxs = dts * xs
            sw = [None] * 8
            sb = [None] * 8
            for r in reversed(range(8)):
                b = jnp.concatenate([b_ref[base + r]] * (wide // 128), axis=1)
                c = jnp.concatenate([c_ref[base + r]] * (wide // 128), axis=1)
                dt = dts[r:r+1]
                dtx = dtxs[r:r+1]
                gr = gs[r:r+1]
                da = jnp.exp2(dt * rate)
                q = da * hp_ref[base + r, :, cols]
                h = q + b * dtx
                lam = c * gr + carry
                w = lam * q
                carry = lam * da
                gb = fold(lam * dtx)
                gc = fold(h * gr)
                if j == 0:
                    gb_ref[base + r] = gb
                    gc_ref[base + r] = gc
                else:
                    gb_ref[base + r] += gb
                    gc_ref[base + r] += gc
                grate = grate + w * dt
                sw[r] = jnp.sum(w * rate, axis=0, keepdims=True)
                sb[r] = jnp.sum(lam * b, axis=0, keepdims=True)
            sbs = jnp.concatenate(sb, axis=0)
            sws = jnp.concatenate(sw, axis=0)
            gdt_ref[pl.ds(base, 8), cols] = sws * LN2 + xs * sbs
            gx_ref[pl.ds(base, 8), cols] = dts * sbs
            return carry, grate
        carry, grate = lax.fori_loop(0, chunk // 8, group, (l_ref[:, cols], grate_ref[:, cols]))
        l_ref[:, cols] = carry
        grate_ref[:, cols] = grate
    gb_out[...] = jnp.sum(gb_ref[...], axis=2)
    gc_out[...] = jnp.sum(gc_ref[...], axis=2)


SCAN_WIDE = 512


def scan_calls(rows, width, states):
    chunk = max(c for c in range(8, 57, 8) if rows % c == 0)
    steps = rows // chunk
    lanes = 128
    row = pl.BlockSpec((chunk, width), lambda i: (i, 0))
    maps = pl.BlockSpec((chunk, states, lanes), lambda i: (i, 0, 0))
    whole = pl.BlockSpec((states, width), lambda i: (0, 0))
    kept = pl.BlockSpec((chunk, states, width), lambda i: (i, 0, 0))
    row_back = pl.BlockSpec((chunk, width), lambda i: (steps - 1 - i, 0))
    maps_back = pl.BlockSpec((chunk, states, lanes), lambda i: (steps - 1 - i, 0, 0))
    narrow_back = pl.BlockSpec((chunk, states), lambda i: (steps - 1 - i, 0))
    kept_back = pl.BlockSpec((chunk, states, width), lambda i: (steps - 1 - i, 0, 0))

    def shape(*sizes):
        return jax.ShapeDtypeStruct(sizes, F32)

    params = pltpu.CompilerParams(vmem_limit_bytes=40 * 2**20)
    sizes = dict(wide=min(SCAN_WIDE, width), chunk=chunk)
    carried = [pltpu.VMEM((states, width), F32)]
    cells = rows * width * states
    state = pl.pallas_call(
        functools.partial(state_kernel, **sizes),
        grid=(steps,),
        in_specs=[row, row, maps, whole],
        out_specs=whole,
        out_shape=shape(states, width),
        compiler_params=params,
        cost_estimate=lasting(7),
        name="scan_state",
    )
    scan = pl.pallas_call(
        functools.partial(scan_kernel, **sizes),
        grid=(steps,),
        in_specs=[row, row, maps, maps, whole, whole],
        out_specs=[row, kept],
        out_shape=[shape(rows, width), shape(rows, states, width)],
        scratch_shapes=carried,
        compiler_params=params,
        cost_estimate=lasting(18),
        name="scan_rows",
    )
    back_state = pl.pallas_call(
        functools.partial(back_state_kernel, **sizes),
        grid=(steps,),
        in_specs=[row_back, row_back, maps_back, whole],
        out_specs=whole,
        out_shape=shape(states, width),
        compiler_params=params,
        cost_estimate=lasting(7),
        name="scan_back_state",
    )
    back = pl.pallas_call(
        functools.partial(back_kernel, **sizes),
        grid=(steps,),
        in_specs=[row_back, row_back, row_back, maps_back, maps_back, whole, kept_back, whole],
        out_specs=[row_back, row_back, narrow_back, narrow_back, whole],
        out_shape=[
            shape(rows, width),
            shape(rows, width),
            shape(rows, states),
            shape(rows, states),
            shape(states, width),
        ],
        scratch_shapes=carried + [pltpu.VMEM((chunk, states, lanes), F32)] * 2,
        compiler_params=params,
        cost_estimate=lasting(36),
        name="scan_back",
    )
    return state, scan, back_state, back


def gather_kernel(block_ref, out_ref, send, recv, own, *, axes):
    sizes = [lax.axis_size(a) for a in axes]
    total = 1
    for size in sizes:
        total *= size
    me = lax.axis_index(axes[0])
    for a in axes[1:]:
        me = me * lax.axis_size(a) + lax.axis_index(a)

    def coordinates(index):
        found = {}
        for a, size in zip(reversed(axes), reversed(sizes)):
            found[a] = lax.rem(index, size)
            index = index // size
        return found

    barrier = pltpu.get_barrier_semaphore()
    for step in range(1, total):
        pl.semaphore_signal(
            barrier, inc=1, device_id=coordinates(lax.rem(me + step, total)), device_id_type=MESH
        )
    pl.semaphore_wait(barrier, total - 1)
    mine = pltpu.make_async_copy(block_ref, out_ref.at[me], own)
    mine.start()
    copies = []
    for step in range(1, total):
        copy = pltpu.make_async_remote_copy(
            block_ref,
            out_ref.at[me],
            send.at[step],
            recv.at[step],
            device_id=coordinates(lax.rem(me + step, total)),
            device_id_type=MESH,
        )
        copy.start()
        copies.append(copy)
    mine.wait()
    for step in range(1, total):
        source = lax.rem(me - step + total, total)
        pltpu.make_async_remote_copy(
            block_ref,
            out_ref.at[source],
            send.at[step],
            recv.at[step],
            device_id=coordinates(source),
            device_id_type=MESH,
        ).wait_recv()
    for copy in copies:
        copy.wait_send()


def direct_gather(block, axes, identifier):
    total = 1
    for a in axes:
        total *= lax.axis_size(a)
    whole = pl.BlockSpec(memory_space=pltpu.VMEM)
    return pl.pallas_call(
        functools.partial(gather_kernel, axes=axes),
        out_shape=jax.ShapeDtypeStruct((total,) + block.shape, block.dtype),
        in_specs=[whole],
        out_specs=whole,
        scratch_shapes=[
            pltpu.SemaphoreType.DMA((total,)),
            pltpu.SemaphoreType.DMA((total,)),
            pltpu.SemaphoreType.DMA,
        ],
        compiler_params=pltpu.CompilerParams(
            collective_id=identifier, has_side_effects=True, vmem_limit_bytes=24 * 2**20
        ),
        name="gather_" + "_".join(axes),
        cost_estimate=lasting(6),
    )(block)


def ar_kernel(x_ref, out_ref, a_buf, b_buf, s_buf, a_send, a_recv, b_send, b_recv, c_send, c_recv, *, pieces, rows, lag):
    z = lax.axis_index("tensor")
    size = lax.axis_size("tensor")
    half = size // 2
    inner = (z == half - 1) | (z == half)
    low = z < half
    outer_dev = jnp.where(low, half - 2, half + 1)
    inner_dev = jnp.where(low, half - 1, half)
    other = jnp.where(low, half, half - 1)
    barrier = pltpu.get_barrier_semaphore()

    def at(ref, k):
        return ref.at[pl.ds(k * rows, rows)]

    def send_a(k):
        return pltpu.make_async_remote_copy(at(x_ref, k), at(a_buf, k), a_send.at[k], a_recv.at[k], device_id={"tensor": inner_dev}, device_id_type=MESH)
    def send_b(k):
        return pltpu.make_async_remote_copy(at(s_buf, k), at(b_buf, k), b_send.at[k], b_recv.at[k], device_id={"tensor": other}, device_id_type=MESH)
    def send_c(k):
        return pltpu.make_async_remote_copy(at(out_ref, k), at(out_ref, k), c_send.at[k], c_recv.at[k], device_id={"tensor": outer_dev}, device_id_type=MESH)

    @pl.when(jnp.logical_not(inner))
    def _():
        pl.semaphore_signal(barrier, inc=1, device_id={"tensor": inner_dev}, device_id_type=MESH)
        pl.semaphore_wait(barrier, 1)
        for k in range(pieces):
            send_a(k).start()
        for k in range(pieces):
            send_c(k).wait_recv()
        for k in range(pieces):
            send_a(k).wait_send()

    @pl.when(inner)
    def _():
        pl.semaphore_signal(barrier, inc=1, device_id={"tensor": outer_dev}, device_id_type=MESH)
        pl.semaphore_signal(barrier, inc=1, device_id={"tensor": other}, device_id_type=MESH)
        pl.semaphore_wait(barrier, 2)
        for t in range(pieces + lag):
            if t < pieces:
                send_a(t).wait_recv()
                part = pl.ds(t * rows, rows)
                s_buf[part] = (x_ref[part].astype(F32) + a_buf[part].astype(F32)).astype(BF16)
                send_b(t).start()
            if t >= lag:
                k = t - lag
                send_b(k).wait_recv()
                part = pl.ds(k * rows, rows)
                out_ref[part] = (s_buf[part].astype(F32) + b_buf[part].astype(F32)).astype(BF16)
                send_c(k).start()
        for k in range(pieces):
            send_b(k).wait_send()
            send_c(k).wait_send()


def tensor_sum(partial_sum, pieces, identifier):
    rows, width = partial_sum.shape
    lag = min(3, pieces)
    whole = pl.BlockSpec(memory_space=pltpu.VMEM)
    return pl.pallas_call(
        functools.partial(ar_kernel, pieces=pieces, rows=rows // pieces, lag=lag),
        out_shape=jax.ShapeDtypeStruct((rows, width), BF16),
        in_specs=[whole],
        out_specs=whole,
        scratch_shapes=[pltpu.VMEM((rows, width), BF16)] * 3
        + [pltpu.SemaphoreType.DMA((pieces,))] * 6,
        compiler_params=pltpu.CompilerParams(
            collective_id=identifier, has_side_effects=True, vmem_limit_bytes=24 * 2**20
        ),
        name="tensor_sum",
        cost_estimate=lasting(16),
    )(partial_sum)


def shifted(block, axis, distance):
    devices = range(lax.axis_size(axis))
    route = [(i - distance, i) for i in devices if i - distance in devices]
    return lax.ppermute(block, axis, route)


def product(left, right):
    return jnp.dot(left, right, preferred_element_type=F32)


def product_t(left, right):
    return lax.dot_general(
        left, right, (((1,), (1,)), ((), ())), preferred_element_type=F32
    )


def product_tl(left, right):
    return lax.dot_general(
        left, right, (((0,), (0,)), ((), ())), preferred_element_type=F32
    )


def norm_forward(values, gain_vec):
    inv_rms = lax.rsqrt(jnp.mean(values * values, axis=-1, keepdims=True) + epsilon)
    return values * inv_rms * gain_vec


def silu_slope(values):
    sigmoid_val = jax.nn.sigmoid(values)
    return sigmoid_val * (1.0 + values * (1.0 - sigmoid_val))


def join(*matrices):
    rows = matrices[0].shape[0]
    return jnp.concatenate([matrix.reshape(rows, -1) for matrix in matrices], axis=1)


def gather_joined(joined):
    return lax.all_gather(joined, ("dp", "seq"), axis=0, tiled=True)


def tensor_forward_sum(partial_sum):
    rows, width = partial_sum.shape
    low = partial_sum.astype(BF16)
    if width % 128:
        padded = jnp.pad(low, ((0, 0), (0, -width % 128)))
        return tensor_sum(padded, 11, 1)[:, :width].astype(F32)
    return tensor_sum(low, 33, 0).astype(F32)


tensor_backward_sum = tensor_forward_sum


def nt(a, b):
    return lax.dot_general(a, b, (((1,), (1,)), ((), ())), preferred_element_type=F32)

def nn(a, b):
    return lax.dot_general(a, b, (((1,), (0,)), ((), ())), preferred_element_type=F32)

def tn(a, b):
    return lax.dot_general(a, b, (((0,), (0,)), ((), ())), preferred_element_type=F32)

def head_lanes(shape, head):
    lane = lax.broadcasted_iota(jnp.int32, shape, 1)
    return (lane >= HD) if head else (lane < HD)

def seen(shape, hop, rows, query_axis):
    if hop * rows - (rows - 1) >= 0 and hop * rows + rows - 1 < WINDOW:
        return None
    distance = hop * rows + lax.broadcasted_iota(jnp.int32, shape, query_axis) - lax.broadcasted_iota(jnp.int32, shape, 1 - query_axis)
    return (distance >= 0) & (distance < WINDOW)

def seq_greet(place, count):
    barrier = pltpu.get_barrier_semaphore()
    for step in range(1, count):
        pl.semaphore_signal(
            barrier, inc=1, device_id={"seq": lax.rem(place + step, count)}, device_id_type=MESH
        )
    pl.semaphore_wait(barrier, count - 1)


def attend_kernel(
    q_ref, kv_ref, acc_ref, low_ref, top_ref, far_ref, total_ref, send, recv, *, count, hop_count
):
    rows = q_ref.shape[0]
    pairs = top_ref.shape[0]
    place = lax.axis_index("seq")
    scale = LOG2E * HD**-0.5
    seq_greet(place, count)

    def move(hop, device):
        return pltpu.make_async_remote_copy(
            kv_ref,
            far_ref.at[hop - 1],
            send.at[hop - 1],
            recv.at[hop - 1],
            device_id={"seq": device},
            device_id_type=MESH,
        )

    for hop in range(1, hop_count + 1):

        @pl.when(place + hop < count)
        def _(hop=hop):
            move(hop, place + hop).start()

    low = head_lanes((rows, 128), 0)

    def one_block(hop, pair):
        cols = pl.ds(pl.multiple_of(pair * 128, 128), 128)
        q = q_ref[:, cols]
        keys = kv_ref[0, :, cols] if hop == 0 else far_ref[hop - 1, 0, :, cols]
        values = kv_ref[1, :, cols] if hop == 0 else far_ref[hop - 1, 1, :, cols]
        mask = seen((rows, rows), hop, rows, 0)
        outs = []
        tops = []
        for head in range(2):
            mine = low if head == 0 else jnp.logical_not(low)
            s = nt(jnp.where(mine, q, jnp.zeros_like(q)), keys)
            if mask is not None:
                s = jnp.where(mask, s, -1e30)
            top = jnp.max(s, axis=1, keepdims=True)
            if hop > 0:
                top = jnp.maximum(top, top_ref[pair, :, pl.ds(head * HD, 1)])
            p = jnp.exp2((s - top) * scale).astype(BF16)
            outs.append(nn(p, jnp.where(mine, values, jnp.ones_like(values))))
            tops.append(top)
        top = jnp.where(low, tops[0], tops[1])
        acc = jnp.where(low, outs[0], outs[1])
        total = pltpu.roll(jnp.where(low, outs[1], outs[0]), HD, 1)
        if hop > 0:
            fade = jnp.exp2((top_ref[pair] - top) * scale)
            acc = acc + acc_ref[:, cols] * fade
            total = total + total_ref[pair] * fade
        acc_ref[:, cols] = acc
        top_ref[pair] = top
        total_ref[pair] = total

    def all_pairs(hop):
        def one(pair, carry):
            one_block(hop, pair)
            return carry

        lax.fori_loop(0, pairs, one, 0)

    all_pairs(0)
    for hop in range(1, hop_count + 1):

        @pl.when(place >= hop)
        def _(hop=hop):
            move(hop, place - hop).wait_recv()
            all_pairs(hop)

    def finish(pair, carry):
        cols = pl.ds(pl.multiple_of(pair * 128, 128), 128)
        total = total_ref[pair]
        acc = acc_ref[:, cols] / total
        acc_ref[:, cols] = acc
        low_ref[:, cols] = acc.astype(BF16)
        top_ref[pair] = top_ref[pair] * scale + jnp.log2(total)
        return carry

    lax.fori_loop(0, pairs, finish, 0)
    for hop in range(1, hop_count + 1):

        @pl.when(place + hop < count)
        def _(hop=hop):
            move(hop, place + hop).wait_send()


def attend(q, kv, hop_count, identifier):
    rows, width = q.shape
    pairs = width // 128
    whole = pl.BlockSpec(memory_space=pltpu.VMEM)
    return pl.pallas_call(
        functools.partial(attend_kernel, count=lax.axis_size("seq"), hop_count=hop_count),
        in_specs=[whole] * 2,
        out_specs=[whole] * 4,
        out_shape=[
            jax.ShapeDtypeStruct((rows, width), F32),
            jax.ShapeDtypeStruct((rows, width), BF16),
            jax.ShapeDtypeStruct((pairs, rows, 128), F32),
            jax.ShapeDtypeStruct((hop_count, 2, rows, width), BF16),
        ],
        scratch_shapes=[
            pltpu.VMEM((pairs, rows, 128), F32),
            pltpu.SemaphoreType.DMA((hop_count,)),
            pltpu.SemaphoreType.DMA((hop_count,)),
        ],
        compiler_params=pltpu.CompilerParams(
            collective_id=identifier, has_side_effects=True, vmem_limit_bytes=48 * 2**20
        ),
        cost_estimate=lasting(55),
        name="attend",
    )(q, kv)


def attend_back_kernel(
    q_ref,
    g_ref,
    o_ref,
    lse_ref,
    kv_ref,
    far_ref,
    cosine_ref,
    sine_ref,
    out_ref,
    lines,
    dq_ref,
    dkv_ref,
    leaving,
    landed,
    send,
    recv,
    *,
    count,
    hop_count,
):
    rows, width = q_ref.shape
    pairs = width // 128
    place = lax.axis_index("seq")
    scale = HD**-0.5
    seq_greet(place, count)

    def columns(pair):
        return pl.ds(pl.multiple_of(pair * 128, 128), 128)

    def move(hop, pair, device):
        return pltpu.make_async_remote_copy(
            leaving.at[hop - 1, :, :, columns(pair)],
            landed.at[hop - 1, :, :, columns(pair)],
            send.at[hop - 1, pair],
            recv.at[hop - 1, pair],
            device_id={"seq": device},
            device_id_type=MESH,
        )

    def prepare(pair, carry):
        cols = columns(pair)
        turned = jnp.transpose(lse_ref[pair])
        dots = jnp.transpose(o_ref[:, cols] * g_ref[:, cols].astype(F32))
        lines[pair, 0:1] = turned[0:1]
        lines[pair, 1:2] = turned[HD : HD + 1]
        lines[pair, 2:3] = jnp.sum(dots[:HD], axis=0, keepdims=True)
        lines[pair, 3:4] = jnp.sum(dots[HD:], axis=0, keepdims=True)
        dq_ref[:, cols] = jnp.zeros((rows, 128), F32)
        return carry

    lax.fori_loop(0, pairs, prepare, 0)

    def one_block(hop, pair):
        cols = columns(pair)
        q = q_ref[:, cols]
        g = g_ref[:, cols]
        k = kv_ref[0, :, cols] if hop == 0 else far_ref[hop - 1, 0, :, cols]
        v = kv_ref[1, :, cols] if hop == 0 else far_ref[hop - 1, 1, :, cols]
        mask = seen((rows, rows), hop, rows, 1)
        dk = jnp.zeros((rows, 128), F32)
        dv = jnp.zeros((rows, 128), F32)
        dq = dq_ref[:, cols]
        for head in range(2):
            mine = head_lanes((rows, 128), head)
            qm = jnp.where(mine, q, jnp.zeros_like(q))
            gm = jnp.where(mine, g, jnp.zeros_like(g))
            km = jnp.where(mine, k, jnp.zeros_like(k))
            s = nt(k, qm) * (LOG2E * scale)
            p = jnp.exp2(s - lines[pair, head : head + 1])
            if mask is not None:
                p = jnp.where(mask, p, 0.0)
            dv = dv + nn(p.astype(BF16), gm)
            dp = nt(v, gm)
            ds = (p * (dp - lines[pair, head + 2 : head + 3])).astype(BF16)
            dk = dk + nn(ds, qm)
            dq = dq + tn(ds, km) * scale
        dq_ref[:, cols] = dq
        return dk * scale, dv

    for hop in reversed(range(1, hop_count + 1)):

        @pl.when(place >= hop)
        def _(hop=hop):
            def one(pair, carry):
                dk, dv = one_block(hop, pair)
                leaving[hop - 1, 0, :, columns(pair)] = dk.astype(BF16)
                leaving[hop - 1, 1, :, columns(pair)] = dv.astype(BF16)
                move(hop, pair, place - hop).start()
                return carry

            lax.fori_loop(0, pairs, one, 0)

    def own(pair, carry):
        dk, dv = one_block(0, pair)
        dkv_ref[0, :, columns(pair)] = dk
        dkv_ref[1, :, columns(pair)] = dv
        return carry

    lax.fori_loop(0, pairs, own, 0)

    for hop in range(1, hop_count + 1):

        @pl.when(place + hop < count)
        def _(hop=hop):
            def one(pair, carry):
                cols = columns(pair)
                move(hop, pair, place + hop).wait_recv()
                for which in range(2):
                    dkv_ref[which, :, cols] += landed[hop - 1, which, :, cols].astype(F32)
                return carry

            lax.fori_loop(0, pairs, one, 0)

    def finish(pair, carry):
        cols = columns(pair)
        cosine, sine = cosine_ref[...], sine_ref[...]

        def turned(values):
            return turn(values.astype(BF16).astype(F32), cosine, sine, -1.0).astype(BF16)

        def later(part):
            return pl.ds(pl.multiple_of(part * width + pair * 128, 128), 128)

        out_ref[:, cols] = turned(dq_ref[:, cols])
        out_ref[:, later(1)] = turned(dkv_ref[0, :, cols])
        out_ref[:, later(2)] = dkv_ref[1, :, cols].astype(BF16)
        return carry

    lax.fori_loop(0, pairs, finish, 0)
    for hop in range(1, hop_count + 1):

        @pl.when(place >= hop)
        def _(hop=hop):
            def one(pair, carry):
                move(hop, pair, place - hop).wait_send()
                return carry

            lax.fori_loop(0, pairs, one, 0)


def attend_back(q, g, o, lse, kv, far, cosine, sine, identifier):
    rows, width = q.shape
    pairs = width // 128
    hop_count = far.shape[0]
    whole = pl.BlockSpec(memory_space=pltpu.VMEM)
    return pl.pallas_call(
        functools.partial(attend_back_kernel, count=lax.axis_size("seq"), hop_count=hop_count),
        in_specs=[whole] * 8,
        out_specs=whole,
        out_shape=jax.ShapeDtypeStruct((rows, 3 * width), BF16),
        scratch_shapes=[
            pltpu.VMEM((pairs, 8, rows), F32),
            pltpu.VMEM((rows, width), F32),
            pltpu.VMEM((2, rows, width), F32),
            pltpu.VMEM((hop_count, 2, rows, width), BF16),
            pltpu.VMEM((hop_count, 2, rows, width), BF16),
            pltpu.SemaphoreType.DMA((hop_count, pairs)),
            pltpu.SemaphoreType.DMA((hop_count, pairs)),
        ],
        compiler_params=pltpu.CompilerParams(
            collective_id=identifier, has_side_effects=True, vmem_limit_bytes=48 * 2**20
        ),
        cost_estimate=lasting(55),
        name="attend_back",
    )(q, g, o, lse, kv, far, cosine, sine)


def partners(values):
    lane = lax.broadcasted_iota(jnp.int32, values.shape, 1)
    half = HD // 2
    return jnp.where(
        lax.rem(lane, HD) < half, pltpu.roll(values, 128 - half, 1), pltpu.roll(values, half, 1)
    )


def turn(values, cosine, sine, sign):
    parts = []
    for first in range(0, values.shape[1], 128):
        piece = values[:, first : first + 128]
        parts.append(piece * cosine + partners(piece) * (sine * sign))
    return jnp.concatenate(parts, axis=1) if len(parts) > 1 else parts[0]


def rope_tables(positions):
    half = HD // 2
    frequency = 10000.0 ** (-jnp.arange(half, dtype=F32) / half)
    angles = positions.astype(F32)[:, None] * frequency[None, :]
    cosine, sine = jnp.cos(angles), jnp.sin(angles)
    return jnp.tile(cosine, (1, 4)), jnp.tile(jnp.concatenate([-sine, sine], axis=1), (1, 2))


def qkv_kernel(x_ref, w_ref, cosine_ref, sine_ref, q_ref, kv_ref, *, tiles):
    step = pl.program_id(0)
    result = nn(x_ref[...], w_ref[...])
    turned = turn(result, cosine_ref[...], sine_ref[...], 1.0)

    @pl.when(step < tiles)
    def _():
        q_ref[...] = turned.astype(BF16)

    @pl.when(step >= tiles)
    def _():
        kv_ref[0] = jnp.where(step < 2 * tiles, turned, result).astype(BF16)


def qkv_rows(x, w, first_column, width, cosine, sine):
    rows, depth = x.shape
    tile = 256
    tiles = width // tile
    skip = first_column // tile
    table = pl.BlockSpec((rows, 128), lambda j: (0, 0))

    def kv_at(j):
        later = jnp.maximum(j - tiles, 0)
        return later // tiles, 0, lax.rem(later, tiles)

    return pl.pallas_call(
        functools.partial(qkv_kernel, tiles=tiles),
        grid=(3 * tiles,),
        in_specs=[
            pl.BlockSpec((rows, depth), lambda j: (0, 0)),
            pl.BlockSpec((depth, tile), lambda j: (0, j + skip)),
            table,
            table,
        ],
        out_specs=[
            pl.BlockSpec((rows, tile), lambda j: (0, jnp.minimum(j, tiles - 1))),
            pl.BlockSpec((1, rows, tile), kv_at),
        ],
        out_shape=[
            jax.ShapeDtypeStruct((rows, width), BF16),
            jax.ShapeDtypeStruct((2, rows, width), BF16),
        ],
        compiler_params=pltpu.CompilerParams(vmem_limit_bytes=32 * 2**20),
        cost_estimate=lasting(8),
        name="qkv_rows",
    )(x, w, cosine, sine)


def sigmoid(v):
    return 1.0 / (1.0 + jnp.exp(-v))

def gate_up_kernel(x_ref, wg_ref, wu_ref, gate_ref, up_ref, hid_ref):
    x = x_ref[...]
    gate = nn(x, wg_ref[...])
    up = nn(x, wu_ref[...])
    gate_ref[...] = gate.astype(BF16)
    up_ref[...] = up.astype(BF16)
    hid_ref[...] = (gate * sigmoid(gate) * up).astype(BF16)

def gate_up(x, w, tile):
    rows, depth = x.shape
    units = w.shape[1] // 3
    steps = units // tile
    col = pl.BlockSpec((rows, tile), lambda j: (0, j))
    out = jax.ShapeDtypeStruct((rows, units), BF16)
    return pl.pallas_call(gate_up_kernel, grid=(steps,),
        in_specs=[pl.BlockSpec((rows, depth), lambda j: (0, 0)), pl.BlockSpec((depth, tile), lambda j: (0, j)), pl.BlockSpec((depth, tile), lambda j: (0, j + steps))],
        out_specs=[col] * 3, out_shape=[out] * 3, compiler_params=pltpu.CompilerParams(vmem_limit_bytes=40 * 2**20),
        cost_estimate=lasting(14), name="gate_up")(x, w, w)

def hidden_back_kernel(g_ref, w_ref, gate_ref, up_ref, gg_ref, gu_ref):
    gh = nn(g_ref[...], w_ref[...])
    gate = gate_ref[...].astype(F32)
    up = up_ref[...].astype(F32)
    sig = sigmoid(gate)
    gg_ref[...] = (gh * up * (sig * (1.0 + gate * (1.0 - sig)))).astype(BF16)
    gu_ref[...] = (gh * (gate * sig)).astype(BF16)

def hidden_back(g, w, gate, up, tile):
    rows, depth = g.shape
    units = w.shape[1] // 3
    steps = units // tile
    col = pl.BlockSpec((rows, tile), lambda j: (0, j))
    out = jax.ShapeDtypeStruct((rows, units), BF16)
    return pl.pallas_call(hidden_back_kernel, grid=(steps,),
        in_specs=[pl.BlockSpec((rows, depth), lambda j: (0, 0)), pl.BlockSpec((depth, tile), lambda j: (0, j + 2 * steps)), col, col],
        out_specs=[col] * 2, out_shape=[out] * 2, compiler_params=pltpu.CompilerParams(vmem_limit_bytes=40 * 2**20),
        cost_estimate=lasting(10), name="hidden_back")(g, w, gate, up)

def weight_grads_kernel(*refs, counts):
    n = len(counts)
    lhs, rhs, out_ref, turned = refs[:n], refs[n:2 * n], refs[2 * n], refs[2 * n + 1]
    step = pl.program_id(0)
    first = 0
    for which in range(n):
        @pl.when(step == first)
        def _():
            turned[...] = jnp.transpose(lhs[which][...])
        @pl.when((step >= first) & (step < first + counts[which]))
        def _():
            out_ref[...] = nn(turned[...], rhs[which][...]).astype(BF16)
        first += counts[which]

def weight_grads(pairs, tile):
    rows, depth = pairs[0][0].shape
    counts = [right.shape[1] // tile for _, right in pairs]
    total = sum(counts)
    starts = [sum(counts[:i]) for i in range(len(counts))]
    whole = pl.BlockSpec((rows, depth), lambda j: (0, 0))
    def spec(start, count):
        return pl.BlockSpec((rows, tile), lambda j: (0, jnp.clip(j - start, 0, count - 1)))
    return pl.pallas_call(functools.partial(weight_grads_kernel, counts=counts), grid=(total,),
        in_specs=[whole] * len(pairs) + [spec(s, c) for s, c in zip(starts, counts)],
        out_specs=pl.BlockSpec((depth, tile), lambda j: (0, j)),
        out_shape=jax.ShapeDtypeStruct((depth, total * tile), BF16),
        scratch_shapes=[pltpu.VMEM((depth, rows), BF16)],
        compiler_params=pltpu.CompilerParams(vmem_limit_bytes=40 * 2**20),
        cost_estimate=lasting(1.25 * total), name="weight_grads")(
        *[left for left, _ in pairs], *[right for _, right in pairs])

def group_place(axes):
    me = lax.axis_index(axes[0])
    for a in axes[1:]:
        me = me * lax.axis_size(a) + lax.axis_index(a)
    return me


def group_device(axes, index):
    found = {}
    for a in reversed(axes):
        found[a] = lax.rem(index, lax.axis_size(a))
        index = index // lax.axis_size(a)
    return found


class SmallSum:
    axes = ("dp", "seq")

    def __init__(self, x_ref, out_ref, arrived, total, send, recv, send_out, recv_out):
        self.x_ref, self.out_ref, self.arrived, self.total = x_ref, out_ref, arrived, total
        self.sems = (send, recv, send_out, recv_out)
        self.count = x_ref.shape[0]
        self.me = group_place(self.axes)

    def to(self, step):
        return lax.rem(self.me + step, self.count)

    def back(self, step):
        return lax.rem(self.me - step + self.count, self.count)

    def greet(self, barrier):
        for step in range(1, self.count):
            pl.semaphore_signal(
                barrier,
                inc=1,
                device_id=group_device(self.axes, self.to(step)),
                device_id_type=MESH,
            )
        return self.count - 1

    def part(self, step, device):
        return pltpu.make_async_remote_copy(
            self.x_ref.at[device],
            self.arrived.at[step],
            self.sems[0].at[step],
            self.sems[1].at[step],
            device_id=group_device(self.axes, device),
            device_id_type=MESH,
        )

    def whole(self, step, slot, device):
        return pltpu.make_async_remote_copy(
            self.total,
            self.out_ref.at[slot],
            self.sems[2].at[step],
            self.sems[3].at[step],
            device_id=group_device(self.axes, device),
            device_id_type=MESH,
        )

    def begin(self):
        for step in range(1, self.count):
            self.part(step, self.to(step)).start()

    def middle(self):
        result = self.x_ref[self.me].astype(F32)
        for step in range(1, self.count):
            self.part(step, self.back(step)).wait_recv()
            result = result + self.arrived[step].astype(F32)
        self.total[...] = result.astype(BF16)
        self.out_ref[self.me] = result.astype(BF16)
        for step in range(1, self.count):
            self.whole(step, self.me, self.to(step)).start()

    def end(self):
        for step in range(1, self.count):
            self.whole(step, self.back(step), self.back(step)).wait_recv()
        for step in range(1, self.count):
            self.part(step, self.to(step)).wait_send()
            self.whole(step, self.me, self.to(step)).wait_send()


class OwnGrads:
    lag = 0

    def __init__(self, lefts, rights, uses, counts, tile, out_ref, scratch):
        self.lefts, self.rights, self.uses, self.counts, self.tile = lefts, rights, uses, counts, tile
        self.out_ref = out_ref
        self.turned, self.staged, self.out_sem = scratch
        self.total = sum(counts)

    @staticmethod
    def scratch(rows, depth, total, tile):
        return [
            pltpu.VMEM((depth, rows), BF16),
            pltpu.VMEM((2, depth, tile), BF16),
            pltpu.SemaphoreType.DMA((2,)),
        ]

    def put(self, t):
        slot = lax.rem(t, 2)
        return pltpu.make_async_copy(
            self.staged.at[slot],
            self.out_ref.at[:, pl.ds(pl.multiple_of(t * self.tile, self.tile), self.tile)],
            self.out_sem.at[slot],
        )

    def turn(self, which):
        self.turned[...] = jnp.transpose(self.lefts[self.uses[which]][...])

    def step(self, t):
        first = 0
        for which, count in enumerate(self.counts):
            if which == 0 or self.uses[which] != self.uses[which - 1]:

                @pl.when(t == first)
                def _(which=which):
                    self.turn(which)

            @pl.when((t >= first) & (t < first + count))
            def _(which=which, first=first):
                self.multiply(which, t - first, t)

            first += count

    def greet(self, barrier):
        return 0

    def multiply(self, which, index, t):
        slot = lax.rem(t, 2)
        block = self.rights[which][:, pl.ds(pl.multiple_of(index * self.tile, self.tile), self.tile)]

        @pl.when(t >= 2)
        def _():
            self.put(t - 2).wait()

        self.staged[slot] = nn(self.turned[...], block).astype(BF16)
        self.put(t).start()

    def end(self):
        for t in (self.total - 2, self.total - 1):
            self.put(t).wait()


class ScatterGrads(OwnGrads):
    lags = (1, 3, 4)
    lag = 4

    def __init__(self, lefts, rights, uses, counts, tile, out_ref, scratch):
        self.lefts, self.rights, self.uses, self.counts, self.tile = lefts, rights, uses, counts, tile
        self.out_ref = out_ref
        self.turned, self.sent, self.kept, self.landed, self.crossed, self.last = scratch[:6]
        self.sems = scratch[6:]
        self.total = sum(counts)
        self.dp = lax.axis_index("dp")
        place = lax.axis_index("seq")
        self.low, self.high = lax.rem(place, 2), place // 2
        self.beside = self.high * 2 + 1 - self.low
        self.across = (1 - self.high) * 2 + self.low
        self.half = self.turned.shape[0] // 2
        self.block = self.half // 4

    @staticmethod
    def scratch(rows, depth, total, tile):
        half = depth // 2
        return [
            pltpu.VMEM((depth, rows), BF16),
            pltpu.VMEM((2, half, tile), BF16),
            pltpu.VMEM((3, half, tile), F32),
            pltpu.VMEM((total, half, tile), BF16),
            pltpu.VMEM((total, 2, half // 4, tile), BF16),
            pltpu.VMEM((total, half // 4, tile), BF16),
            pltpu.SemaphoreType.DMA((2, total)),
            pltpu.SemaphoreType.DMA((total, 2)),
            pltpu.SemaphoreType.DMA((total, 2)),
            pltpu.SemaphoreType.DMA((total,)),
            pltpu.SemaphoreType.DMA((total,)),
        ]

    def greet(self, barrier):
        for device in ({"dp": 1 - self.dp}, {"seq": self.beside}, {"seq": self.across}):
            pl.semaphore_signal(barrier, inc=1, device_id=device, device_id_type=MESH)
        return 3

    def part(self, which):
        return self.turned[pl.ds(pl.multiple_of(which * self.half, self.half), self.half)]

    def to_core(self, t):
        return pltpu.make_async_remote_copy(
            self.sent.at[lax.rem(t, 2)],
            self.landed.at[t],
            self.sems[0].at[0, t],
            self.sems[0].at[1, t],
            device_id={"dp": 1 - self.dp},
            device_id_type=MESH,
        )

    def rows(self, index):
        return pl.ds(pl.multiple_of(index * self.block, self.block), self.block)

    def even(self, t, if_even, if_odd):
        return jnp.where(lax.rem(t, 2) == 0, if_even, if_odd)

    def to_first(self, t, k):
        index = self.even(t, 2 * k + 1 - self.low, (1 - self.high) * 2 + k)
        return pltpu.make_async_remote_copy(
            self.landed.at[t, self.rows(index)],
            self.crossed.at[t, k],
            self.sems[1].at[t, k],
            self.sems[2].at[t, k],
            device_id={"seq": self.even(t, self.beside, self.across)},
            device_id_type=MESH,
        )

    def to_second(self, t):
        return pltpu.make_async_remote_copy(
            self.crossed.at[t, self.even(t, 1 - self.high, 1 - self.low)],
            self.last.at[t],
            self.sems[3].at[t],
            self.sems[4].at[t],
            device_id={"seq": self.even(t, self.across, self.beside)},
            device_id_type=MESH,
        )

    def multiply(self, which, index, t):
        slot = lax.rem(t, 2)
        block = self.rights[which][:, pl.ds(pl.multiple_of(index * self.tile, self.tile), self.tile)]

        @pl.when(t >= 2)
        def _():
            self.to_core(t - 2).wait_send()

        self.sent[slot] = nn(self.part(1 - self.dp), block).astype(BF16)
        self.to_core(t).start()
        self.kept[lax.rem(t, 3)] = nn(self.part(self.dp), block)

    def core_sum(self, t):
        self.to_core(t).wait_recv()
        self.landed[t] = (self.kept[lax.rem(t, 3)] + self.landed[t].astype(F32)).astype(BF16)
        for k in range(2):
            self.to_first(t, k).start()

    def first_chip_sum(self, t):
        for k in range(2):
            self.to_first(t, k).wait_recv()
            index = self.even(t, 2 * k + self.low, self.high * 2 + k)
            own = self.landed[t, self.rows(index)].astype(F32)
            self.crossed[t, k] = (own + self.crossed[t, k].astype(F32)).astype(BF16)
        self.to_second(t).start()

    def second_chip_sum(self, t):
        self.to_second(t).wait_recv()
        own = self.crossed[t, self.even(t, self.high, self.low)].astype(F32)
        self.out_ref[:, pl.ds(pl.multiple_of(t * self.tile, self.tile), self.tile)] = (
            own + self.last[t].astype(F32)
        ).astype(BF16)

    def step(self, t):
        super().step(t)
        works = (self.core_sum, self.first_chip_sum, self.second_chip_sum)
        for late, work in zip(self.lags, works):

            @pl.when((t >= late) & (t < self.total + late))
            def _(late=late, work=work):
                work(t - late)

    def end(self):
        for t in (self.total - 2, self.total - 1):
            self.to_core(t).wait_send()

        def finish(t, carry):
            for k in range(2):
                self.to_first(t, k).wait_send()
            self.to_second(t).wait_send()
            return carry

        lax.fori_loop(0, self.total, finish, 0)


def grad_operands(pairs, xs):
    lefts, uses = [], []
    for left, _ in pairs:
        known = [i for i, other in enumerate(lefts) if other is left]
        uses.append(known[0] if known else len(lefts))
        if not known:
            lefts.append(left)
    shared = []
    rights = []
    for _, right in pairs:
        same = [i for i, x in enumerate(xs) if x is right]
        shared.append(same[0] if same else -1)
        if not same:
            rights.append(right)
    return lefts, rights, uses, shared


def matmul_sum_kernel(
    *refs, columns, first_column, tile, splits, with_small, uses, shared, counts, job_kind
):
    refs = list(refs)

    def take(count):
        taken = refs[:count]
        del refs[:count]
        return taken

    xs = take(len(columns))
    (w_ref,) = take(1)
    small_in = take(1 if with_small else 0)
    lefts = take(max(uses) + 1 if uses else 0)
    others = take(sum(which < 0 for which in shared))
    rights = [xs[which] if which >= 0 else others.pop(0) for which in shared]
    (out_ref,) = take(1)
    small_out = take(1 if with_small else 0)
    grads_out = take(1 if uses else 0)
    w_buf, part, a_buf, b_buf, w_sem, a_send, a_recv, b_send, b_recv, c_send, c_recv = take(11)
    small = SmallSum(*small_in, *small_out, *take(6)) if with_small else None
    job = None
    if uses:
        job = job_kind(lefts, rights, uses, counts, tile, *grads_out, refs)
    rows, depth = out_ref.shape
    tiles = depth // tile
    short = rows // splits
    wide = sum(columns)
    z = lax.axis_index("tensor")
    half = lax.axis_size("tensor") // 2
    inner = (z == half - 1) | (z == half)
    low = z < half
    outer_dev = jnp.where(low, half - 2, half + 1)
    inner_dev = jnp.where(low, half - 1, half)
    other = jnp.where(low, half, half - 1)
    barrier = pltpu.get_barrier_semaphore()

    def weights(j, slot):
        return pltpu.make_async_copy(
            w_ref.at[pl.ds(pl.multiple_of(j * tile, tile), tile), pl.ds(first_column, wide)],
            w_buf.at[slot],
            w_sem.at[slot],
        )

    def cells(ref, j, r):
        return ref.at[pl.ds(r * short, short), pl.ds(pl.multiple_of(j * tile, tile), tile)]

    def send(src, dst, sems, j, r, device):
        return pltpu.make_async_remote_copy(
            cells(src, j, r),
            cells(dst, j, r),
            sems[0].at[j, r],
            sems[1].at[j, r],
            device_id={"tensor": device},
            device_id_type=MESH,
        )

    def send_a(j, r):
        return send(part, a_buf, (a_send, a_recv), j, r, inner_dev)

    def send_b(j, r):
        return send(part, b_buf, (b_send, b_recv), j, r, other)

    def send_c(j, r):
        return send(out_ref, out_ref, (c_send, c_recv), j, r, outer_dev)

    weights(0, 0).start()
    greeted = (small.greet(barrier) if with_small else 0) + (job.greet(barrier) if uses else 0)

    @pl.when(jnp.logical_not(inner))
    def _():
        pl.semaphore_signal(barrier, inc=1, device_id={"tensor": inner_dev}, device_id_type=MESH)
        pl.semaphore_wait(barrier, 1 + greeted)

    @pl.when(inner)
    def _():
        pl.semaphore_signal(barrier, inc=1, device_id={"tensor": outer_dev}, device_id_type=MESH)
        pl.semaphore_signal(barrier, inc=1, device_id={"tensor": other}, device_id_type=MESH)
        pl.semaphore_wait(barrier, 2 + greeted)

    if with_small:
        small.begin()

    def first_sum(j, r):
        send_a(j, r).wait_recv()
        mine = cells(part, j, r)
        mine[...] = (mine[...].astype(F32) + cells(a_buf, j, r)[...].astype(F32)).astype(BF16)
        send_b(j, r).start()

    def second_sum(j, r):
        send_b(j, r).wait_recv()
        cells(out_ref, j, r)[...] = (
            cells(part, j, r)[...].astype(F32) + cells(b_buf, j, r)[...].astype(F32)
        ).astype(BF16)
        send_c(j, r).start()

    lag = splits - 1

    def one_tile(j, carry):
        slot = lax.rem(j, 2)
        weights(j, slot).wait()

        @pl.when(j + 1 < tiles)
        def _():
            weights(j + 1, 1 - slot).start()

        total = None
        first = 0
        for x_ref, count in zip(xs, columns):
            term = nt(x_ref[...], w_buf[slot, :, pl.ds(first, count)])
            total = term if total is None else total + term
            first += count
        part[:, pl.ds(pl.multiple_of(j * tile, tile), tile)] = total.astype(BF16)

        @pl.when(jnp.logical_not(inner))
        def _():
            for r in range(splits):
                send_a(j, r).start()

        each = -(-(job.total + job.lag) // tiles) if uses else 0
        for r in range(max(splits, each)):
            if r < splits:

                @pl.when(inner)
                def _(r=r):
                    first_sum(j, r)
                    if r >= lag:
                        second_sum(j, r - lag)
                    else:

                        @pl.when(j > 0)
                        def _():
                            second_sum(j - 1, r + splits - lag)

            if r < each:
                job.step(j * each + r)

        return carry

    if with_small:
        lax.fori_loop(0, tiles // 2, one_tile, 0)
        small.middle()
        lax.fori_loop(tiles // 2, tiles, one_tile, 0)
    else:
        lax.fori_loop(0, tiles, one_tile, 0)

    @pl.when(inner)
    def _():
        for r in range(splits - lag, splits):
            second_sum(tiles - 1, r)

        def finish(j, carry):
            for r in range(splits):
                send_b(j, r).wait_send()
                send_c(j, r).wait_send()
            return carry

        lax.fori_loop(0, tiles, finish, 0)

    @pl.when(jnp.logical_not(inner))
    def _():
        def finish(j, carry):
            for r in range(splits):
                send_c(j, r).wait_recv()
                send_a(j, r).wait_send()
            return carry

        lax.fori_loop(0, tiles, finish, 0)

    if with_small:
        small.end()
    if uses:
        job.end()


def matmul_sum(
    xs, w, first_column, identifier, small=None, pairs=None, scatter=False, tile=256, splits=3
):
    rows = xs[0].shape[0]
    depth = w.shape[0]
    columns = [x.shape[1] for x in xs]
    wide = sum(columns)
    whole = pl.BlockSpec(memory_space=pltpu.VMEM)
    far = pl.BlockSpec(memory_space=pltpu.HBM)
    tiles = depth // tile
    out_shape = [jax.ShapeDtypeStruct((rows, depth), BF16)]
    out_specs = [whole]
    scratch = (
        [pltpu.VMEM((2, tile, wide), BF16)]
        + [pltpu.VMEM((rows, depth), BF16)] * 3
        + [pltpu.SemaphoreType.DMA((2,))]
        + [pltpu.SemaphoreType.DMA((tiles, splits))] * 6
    )
    extra = ()
    if small is not None:
        extra = (small,)
        out_shape.append(jax.ShapeDtypeStruct(small.shape, BF16))
        out_specs.append(whole)
        scratch += [pltpu.VMEM(small.shape, BF16), pltpu.VMEM(small.shape[1:], BF16)]
        scratch += [pltpu.SemaphoreType.DMA((small.shape[0],))] * 4
    uses, shared, counts, job_kind = (), (), (), None
    if pairs is not None:
        job_kind = ScatterGrads if scatter else OwnGrads
        lefts, rights, uses, shared = grad_operands(pairs, xs)
        counts = [right.shape[1] // tile for _, right in pairs]
        extra = (*extra, *lefts, *rights)
        height = depth // 8 if scatter else depth
        out_shape.append(jax.ShapeDtypeStruct((height, sum(counts) * tile), BF16))
        out_specs.append(whole if scatter else far)
        scratch += job_kind.scratch(rows, depth, sum(counts), tile)
    results = pl.pallas_call(
        functools.partial(
            matmul_sum_kernel,
            columns=columns,
            first_column=first_column,
            tile=tile,
            splits=splits,
            with_small=small is not None,
            uses=uses,
            shared=shared,
            counts=counts,
            job_kind=job_kind,
        ),
        out_shape=out_shape,
        in_specs=[whole] * len(xs) + [far] + [whole] * len(extra),
        out_specs=out_specs,
        scratch_shapes=scratch,
        compiler_params=pltpu.CompilerParams(
            collective_id=identifier, has_side_effects=True, vmem_limit_bytes=(40 if pairs is None else 44) * 2**20
        ),
        cost_estimate=lasting(58 if pairs is None else 67),
        name="matmul_sum" + ("_small" if small is not None else "_grads" if uses else ""),
    )(*xs, w, *extra)
    return results if extra else results[0]


def norm_back_kernel(v_ref, gain_ref, normed_ref, out_ref, total_ref, low_ref, gain_out):
    @pl.when(pl.program_id(0) == 0)
    def _():
        gain_out[...] = jnp.zeros_like(gain_out)

    v = v_ref[...].astype(F32)
    grad = normed_ref[...].astype(F32)
    inv_rms = lax.rsqrt(jnp.mean(v * v, axis=1, keepdims=True) + epsilon)
    weighted = grad * gain_ref[...]
    mean_term = jnp.mean(weighted * v, axis=1, keepdims=True)
    total = out_ref[...] + inv_rms * weighted - v * (inv_rms * inv_rms * inv_rms * mean_term)
    total_ref[...] = total
    low_ref[...] = total.astype(BF16)
    gain_out[...] += jnp.sum(grad * (v * inv_rms), axis=0, keepdims=True)


def norm_back(v, gain, grad_normed, grad_out):
    rows, depth = v.shape
    chunk = rows // 11 if rows % 176 == 0 else rows
    block = pl.BlockSpec((chunk, depth), lambda i: (i, 0))
    line = pl.BlockSpec((1, depth), lambda i: (0, 0))
    return pl.pallas_call(
        norm_back_kernel,
        grid=(rows // chunk,),
        in_specs=[block, line, block, block],
        out_specs=[block, block, line],
        out_shape=[
            jax.ShapeDtypeStruct((rows, depth), F32),
            jax.ShapeDtypeStruct((rows, depth), BF16),
            jax.ShapeDtypeStruct((1, depth), F32),
        ],
        compiler_params=pltpu.CompilerParams(vmem_limit_bytes=24 * 2**20),
        cost_estimate=lasting(4),
        name="norm_back",
    )(v, gain.reshape(1, depth), grad_normed, grad_out)


def scattered(grads, axes):
    return lax.optimization_barrier(
        lax.psum_scatter(grads, axes, scatter_dimension=0, tiled=True)
    )


def first_gather_kernel(
    rows_ref, gains_ref, w_ref, full_ref, gains_out, acting_ref, own_sem, gain_sems, sems
):
    dp = lax.axis_index("dp")
    seq = lax.axis_index("seq")
    low, high = lax.rem(seq, 2), seq // 2
    beside = high * 2 + 1 - low
    across = (1 - high) * 2 + low
    far = (1 - high) * 2 + 1 - low
    count = 8
    me = dp * 4 + seq
    height = w_ref.shape[0]
    pieces = 4
    wide = w_ref.shape[1] // pieces
    axes = ("dp", "seq")
    barrier = pltpu.get_barrier_semaphore()
    for step in range(1, count):
        pl.semaphore_signal(
            barrier,
            inc=1,
            device_id=group_device(axes, lax.rem(me + step, count)),
            device_id_type=MESH,
        )
    pl.semaphore_wait(barrier, count - 1)

    def cells(ref, owner_dp, owner_seq, p):
        first = pl.multiple_of((owner_dp * 4 + owner_seq) * height, height)
        return ref.at[pl.ds(first, height), pl.ds(p * wide, wide)]

    def copy(kind, p, owner_dp, owner_seq, device, own=False):
        here = w_ref.at[:, pl.ds(p * wide, wide)] if own else cells(full_ref, owner_dp, owner_seq, p)
        return pltpu.make_async_remote_copy(
            here,
            cells(full_ref, owner_dp, owner_seq, p),
            sems.at[0, kind, p],
            sems.at[1, kind, p],
            device_id=device,
            device_id_type=MESH,
        )

    to_beside, to_across, to_core = {"seq": beside}, {"seq": across}, {"dp": 1 - dp}
    keep = pltpu.make_async_copy(
        w_ref, full_ref.at[pl.ds(pl.multiple_of(me * height, height), height)], own_sem
    )

    def gain_copy(step, slot, device):
        return pltpu.make_async_remote_copy(
            gains_ref,
            gains_out.at[slot],
            gain_sems.at[0, step],
            gain_sems.at[1, step],
            device_id=group_device(axes, device),
            device_id_type=MESH,
        )

    for step in range(1, count):
        gain_copy(step, me, lax.rem(me + step, count)).start()
    for p in range(pieces):
        copy(0, p, dp, seq, to_beside, True).start()
        copy(1, (p + 2) % pieces, dp, seq, to_across, True).start()
    keep.start()
    for p in range(pieces):
        copy(3, p, dp, seq, to_core, True).start()
    gains_out[me] = gains_ref[...]
    for step in range(1, count):
        source = lax.rem(me - step + count, count)
        gain_copy(step, source, source).wait_recv()
    values = rows_ref[...].astype(F32)
    inv_rms = lax.rsqrt(jnp.mean(values * values, axis=1, keepdims=True) + epsilon)
    part = values.shape[1] // count
    for i in range(count):
        at = pl.ds(i * part, part)
        acting_ref[:, at] = (
            values[:, i * part : (i + 1) * part] * inv_rms * gains_out[i, 0:1, :]
        ).astype(BF16)
    for turn_index in range(pieces):
        p = turn_index
        copy(0, p, dp, beside, to_beside).wait_recv()
        if p < pieces // 2:
            copy(2, p, dp, beside, to_across).start()
        copy(4, p, dp, beside, to_core).start()
        p = (turn_index + 2) % pieces
        copy(1, p, dp, across, to_across).wait_recv()
        if p >= pieces // 2:
            copy(2, p, dp, across, to_beside).start()
        copy(5, p, dp, across, to_core).start()
    for p in (0, 2, 1, 3):
        copy(2, p, dp, far, to_across).wait_recv()
        copy(6, p, dp, far, to_core).start()
    for p in range(pieces):
        for kind, owner in ((3, seq), (4, beside), (5, across), (6, far)):
            copy(kind, p, 1 - dp, owner, to_core).wait_recv()
    keep.wait()
    for step in range(1, count):
        gain_copy(step, me, lax.rem(me + step, count)).wait_send()
    for p in range(pieces):
        copy(0, p, dp, seq, to_beside, True).wait_send()
        copy(1, p, dp, seq, to_across, True).wait_send()
        copy(3, p, dp, seq, to_core, True).wait_send()
        if p < pieces // 2:
            copy(2, p, dp, beside, to_across).wait_send()
        else:
            copy(2, p, dp, across, to_beside).wait_send()
        copy(4, p, dp, beside, to_core).wait_send()
        copy(5, p, dp, across, to_core).wait_send()
        copy(6, p, dp, far, to_core).wait_send()


def first_gather(rows, gains, w, identifier):
    whole = pl.BlockSpec(memory_space=pltpu.VMEM)
    far = pl.BlockSpec(memory_space=pltpu.HBM)
    return pl.pallas_call(
        first_gather_kernel,
        in_specs=[whole, whole, far],
        out_specs=[far, whole, whole],
        out_shape=[
            jax.ShapeDtypeStruct((8 * w.shape[0], w.shape[1]), BF16),
            jax.ShapeDtypeStruct((8,) + gains.shape, F32),
            jax.ShapeDtypeStruct(rows.shape, BF16),
        ],
        scratch_shapes=[
            pltpu.SemaphoreType.DMA,
            pltpu.SemaphoreType.DMA((2, 8)),
            pltpu.SemaphoreType.DMA((2, 7, 4)),
        ],
        compiler_params=pltpu.CompilerParams(
            collective_id=identifier, has_side_effects=True, vmem_limit_bytes=32 * 2**20
        ),
        name="first_gather",
        cost_estimate=lasting(42),
    )(rows, gains, w)


def gate_back_kernel(g_ref, w_ref, gate_ref, scanned_ref, input_ref, scan_ref, gate_out, skip_ref):
    grad = nn(g_ref[...], w_ref[...])
    gate = gate_ref[...].astype(F32)
    sig = sigmoid(gate)
    scan = grad * (gate * sig)
    scan_ref[...] = scan
    gate_out[...] = (grad * scanned_ref[...] * (sig * (1.0 + gate * (1.0 - sig)))).astype(BF16)
    skip_ref[...] = jnp.sum(scan * input_ref[...].astype(F32), axis=0, keepdims=True)


def gate_back(g, w, gate, gate_column, scanned, inputs, tile=256):
    rows, depth = g.shape
    width = scanned.shape[1]
    skip = gate_column // tile
    column = pl.BlockSpec((rows, tile), lambda j: (0, j))
    return pl.pallas_call(
        gate_back_kernel,
        grid=(width // tile,),
        in_specs=[
            pl.BlockSpec((rows, depth), lambda j: (0, 0)),
            pl.BlockSpec((depth, tile), lambda j: (0, j)),
            pl.BlockSpec((rows, tile), lambda j: (0, j + skip)),
            column,
            column,
        ],
        out_specs=[column, column, pl.BlockSpec((1, tile), lambda j: (0, j))],
        out_shape=[
            jax.ShapeDtypeStruct((rows, width), F32),
            jax.ShapeDtypeStruct((rows, width), BF16),
            jax.ShapeDtypeStruct((1, width), F32),
        ],
        compiler_params=pltpu.CompilerParams(vmem_limit_bytes=32 * 2**20),
        cost_estimate=lasting(6),
        name="gate_back",
    )(g, w, gate, scanned, inputs)


def ffn_forward(stream, gain, weights, identifier):
    acting = norm_forward(stream, gain).astype(BF16)
    gate, up, hidden_low = gate_up(acting, weights, 256)
    branch = matmul_sum([hidden_low], weights, 2 * hidden_low.shape[1], identifier)
    return (stream + branch.astype(F32), (acting, gate, up, hidden_low))


def shards(
    hidden,
    teacher,
    valid_length,
    mamba_norm,
    mamba_in,
    conv_kernel,
    conv_bias,
    select_weight,
    step_weight,
    step_bias,
    decay_log,
    skip_gain,
    mamba_out,
    attn_norm,
    attn_qkv,
    attn_out,
    first_norm,
    first_gate_up,
    first_down,
    second_norm,
    second_gate_up,
    second_down,
):
    def split(rows, *like):
        parts = []
        first = 0
        for shard in like:
            if len(shard.shape) == 3:
                height, groups, columns = shard.shape
                pieces = [
                    rows[:, first + columns * g : first + columns * (g + 1)] for g in range(groups)
                ]
                parts.append(jnp.stack(pieces).transpose(1, 0, 2).astype(F32))
                columns = columns * groups
            else:
                columns = shard.shape[1]
                parts.append(rows[:, first : first + columns].astype(F32))
            first += columns
        return parts

    rows_here = hidden.shape[1]
    model_width = hidden.shape[2]
    seq_count = lax.axis_size("seq")
    seq_place = lax.axis_index("seq")
    my_length = valid_length[lax.axis_index("dp")]
    positions = seq_place * rows_here + jnp.arange(rows_here, dtype=jnp.int32)
    valid_rows = (positions < my_length).astype(F32)[:, None]
    total_valid = jnp.sum(valid_length).astype(F32)
    total_slots = valid_length.shape[0] * rows_here * seq_count
    stream_zero = hidden[0].astype(F32)
    gains = jnp.stack([mamba_norm, attn_norm, first_norm, second_norm]).astype(F32)
    gains = jnp.pad(gains, ((0, 4), (0, 0)))
    split_four = lax.axis_size("dp") == 2 and seq_count == 4
    mixed = join(mamba_out, attn_qkv, attn_out)
    if split_four:
        gains, mixed = lax.optimization_barrier((gains, mixed))
        in_full, gains, acting_mamba = first_gather(hidden[0], gains, join(mamba_in), 2)
    else:
        gains = direct_gather(gains, ("dp", "seq"), 2)
        in_full = gather_joined(join(mamba_in))
    gain_mamba, gain_attn, gain_first, gain_second = (
        gains[:, which].reshape(model_width) for which in range(4)
    )
    mixed, in_full = lax.optimization_barrier((mixed, in_full))
    mixed_full = gather_joined(mixed)
    channels = mamba_out.shape[1]
    heads_width = attn_out.shape[1]
    qkv_column = channels
    attn_column = channels + 3 * heads_width
    if not split_four:
        acting_mamba = norm_forward(stream_zero, gain_mamba).astype(BF16)
    projected = product(acting_mamba, in_full).astype(BF16)
    ffn_shards = (first_gate_up, first_down, second_gate_up, second_down)
    ffn_shards, projected = lax.optimization_barrier((ffn_shards, projected))
    first_weights = gather_joined(join(*ffn_shards[:2]))
    second_weights = gather_joined(join(*ffn_shards[2:]))
    conv_input = projected[:, :channels]
    gate_input = projected[:, channels:].astype(F32)
    tap_count = conv_kernel.shape[0]
    edge_rows = shifted(conv_input[rows_here - (tap_count - 1) :], "seq", 1)
    padded = jnp.concatenate([edge_rows, conv_input], axis=0).astype(F32)
    conv_pre = conv_bias
    for tap_index in range(tap_count):
        conv_pre = conv_pre + conv_kernel[tap_index] * padded[tap_index : tap_index + rows_here]
    inputs_low = jax.nn.silu(conv_pre).astype(BF16)
    inputs = inputs_low.astype(F32)
    selected = tensor_forward_sum(product(inputs_low, select_weight))
    step_rank = step_weight.shape[0]
    states = decay_log.shape[0]
    step_in = selected[:, :step_rank].astype(BF16)
    input_map = selected[:, step_rank : step_rank + states]
    output_map = selected[:, step_rank + states :]
    step_pre = product(step_in, step_weight) + step_bias
    step_size = jax.nn.softplus(step_pre)
    decay_rate = -jnp.exp(decay_log)
    width = inputs.shape[1]
    run_state, run_scan, run_back_state, run_back = scan_calls(rows_here, width, states)
    rate_two = decay_rate * LOG2E
    in_wide = jnp.broadcast_to(input_map[:, :, None], (rows_here, states, 128))
    out_wide = jnp.broadcast_to(output_map[:, :, None], (rows_here, states, 128))
    moved = step_size * inputs
    end_state = run_state(step_size, moved, in_wide, rate_two)
    step_total = jnp.sum(step_size, axis=0, keepdims=True)
    ends = direct_gather(
        jnp.concatenate([end_state, step_total, jnp.zeros((7, width), F32)], axis=0), ("seq",), 3
    )
    decays = [jnp.exp2(rate_two * ends[place, states][None]) for place in range(seq_count)]
    start_state = jnp.zeros_like(end_state)
    for place in range(seq_count - 1):
        start_state = jnp.where(
            place < seq_place, decays[place] * start_state + ends[place, :states], start_state
        )
    scanned, kept_states = run_scan(step_size, moved, in_wide, out_wide, rate_two, start_state)
    scanned = scanned + skip_gain * inputs
    gate_silu = jax.nn.silu(gate_input)
    gated_low = (scanned * gate_silu).astype(BF16)
    stream_one = stream_zero + matmul_sum([gated_low], mixed_full, 0, 6).astype(F32)
    normed_attn = norm_forward(stream_one, gain_attn)
    acting_attn = normed_attn.astype(BF16)
    cosine, sine = rope_tables(positions)
    queries, own_kv = qkv_rows(acting_attn, mixed_full, qkv_column, heads_width, cosine, sine)
    hop_count = min(seq_count - 1, (WINDOW - 2) // rows_here + 1)
    attended, attended_low, log_sums, far_kv = attend(queries, own_kv, hop_count, 13)
    stream_two = stream_one + matmul_sum([attended_low], mixed_full, attn_column, 7).astype(F32)
    stream_three, first_saved = ffn_forward(stream_two, gain_first, first_weights, 8)
    stream_four, second_saved = ffn_forward(stream_three, gain_second, second_weights, 8)
    residue = (stream_four - teacher[0].astype(F32)) * valid_rows
    local_loss = jnp.sum(residue * residue) / (model_width * total_valid)
    grad_four = residue * (total_slots / total_valid)
    acting, gate, up, hidden_low = second_saved
    grad_low = grad_four.astype(BF16)
    grad_gate, grad_up = hidden_back(grad_low, second_weights, gate, up, 256)
    second_parts = [(acting, grad_gate), (acting, grad_up), (grad_low, hidden_low)]
    grad_normed, second_grads = matmul_sum(
        [grad_gate, grad_up], second_weights, 0, 16, pairs=second_parts
    )
    second_grads = scattered(second_grads, ("dp", "seq"))
    grad_three, grad_low, grad_gain_second = norm_back(
        stream_three, gain_second, grad_normed, grad_four
    )
    acting, gate, up, hidden_low = first_saved
    grad_gate, grad_up = hidden_back(grad_low, first_weights, gate, up, 256)
    first_parts = [(acting, grad_gate), (acting, grad_up), (grad_low, hidden_low)]
    grad_normed, first_grads = matmul_sum(
        [grad_gate, grad_up], first_weights, 0, 16, pairs=first_parts
    )
    grad_two, grad_low_attn, grad_gain_first = norm_back(
        stream_two, gain_first, grad_normed, grad_three
    )
    grad_attended = product(grad_low_attn, mixed_full[:, attn_column:]).astype(BF16)
    grad_projected_attn = attend_back(
        queries, grad_attended, attended, log_sums, own_kv, far_kv, cosine, sine, 14
    )
    grad_projected_attn, second_grads = lax.optimization_barrier(
        (grad_projected_attn, second_grads)
    )
    first_grads = scattered(first_grads, ("dp", "seq"))
    attn_pairs = [(acting_attn, grad_projected_attn), (grad_low_attn, attended_low)]
    grad_normed_attn, attn_grads = matmul_sum(
        [grad_projected_attn], mixed_full, qkv_column, 10, pairs=attn_pairs
    )
    attn_grads = scattered(attn_grads, ("dp", "seq"))
    grad_one, grad_low_mamba, grad_gain_attn = norm_back(
        stream_one, gain_attn, grad_normed_attn, grad_two
    )
    second_both, second_down_grad = split(second_grads, second_gate_up, second_down)
    grad_scanned, grad_gate_low, grad_skip = gate_back(
        grad_low_mamba, mixed_full, projected, channels, scanned, inputs_low
    )
    incoming = run_back_state(step_size, grad_scanned, out_wide, rate_two)
    incomings = direct_gather(incoming, ("seq",), 4)
    arriving_grad = jnp.zeros_like(incoming)
    for place in reversed(range(1, seq_count)):
        arriving_grad = jnp.where(
            place > seq_place, incomings[place] + decays[place] * arriving_grad, arriving_grad
        )
    grad_sizes, grad_inputs_scan, grad_in_map, grad_out_map, grad_rates = run_back(
        step_size, inputs, grad_scanned, in_wide, out_wide, rate_two, kept_states, arriving_grad
    )
    grad_decay_log = grad_rates * decay_rate
    grad_inputs = grad_inputs_scan + grad_scanned * skip_gain
    grad_step_pre = grad_sizes * jax.nn.sigmoid(step_pre)
    grad_step_bias = jnp.sum(grad_step_pre, axis=0)
    grad_step_low = grad_step_pre.astype(BF16)
    grad_step_weight = product_tl(step_in, grad_step_low)
    grad_step_in = product_t(grad_step_low, step_weight)
    grad_selected = tensor_backward_sum(
        jnp.concatenate([grad_step_in, grad_in_map, grad_out_map], axis=1)
    ).astype(BF16)
    grad_selected, first_grads = lax.optimization_barrier((grad_selected, first_grads))
    grad_select = product_tl(grad_selected, inputs_low)
    grad_inputs = grad_inputs + product_t(grad_selected, select_weight)
    grad_conv_pre = grad_inputs * silu_slope(conv_pre)
    grad_conv_bias = jnp.sum(grad_conv_pre, axis=0)
    grad_kernel = jnp.stack(
        [
            jnp.sum(padded[tap_index : tap_index + rows_here] * grad_conv_pre, axis=0)
            for tap_index in range(tap_count)
        ]
    )
    grad_padded = sum(
        (
            jnp.pad(
                conv_kernel[tap_index] * grad_conv_pre,
                ((tap_index, tap_count - 1 - tap_index), (0, 0)),
            )
            for tap_index in range(tap_count)
        )
    )
    back_edge = shifted(grad_padded[: tap_count - 1], "seq", -1)
    grad_conv_input = grad_padded[tap_count - 1 :] + jnp.pad(
        back_edge, ((rows_here - (tap_count - 1), 0), (0, 0))
    )
    grad_conv_low = grad_conv_input.astype(BF16)
    mamba_pairs = [
        (grad_low_mamba, gated_low),
        (acting_mamba, grad_gate_low),
        (acting_mamba, grad_conv_low),
    ]
    loose = (
        grad_kernel,
        grad_conv_bias[None],
        grad_step_bias[None],
        grad_skip,
        jnp.broadcast_to(local_loss, (1, width)),
        grad_gain_attn.reshape(-1, width),
        grad_gain_first.reshape(-1, width),
        grad_gain_second.reshape(-1, width),
    )
    loose_rows = sum(part.shape[0] for part in loose)
    loose_block = jnp.concatenate(
        loose + (jnp.zeros((-loose_rows % 16, width), F32),), axis=0
    ).astype(BF16)
    packed = (grad_select, grad_step_weight, grad_decay_log, loose_block)
    devices = lax.axis_size("dp") * seq_count
    packed_rows = sum(part.shape[0] for part in packed)
    each = -(-packed_rows // (16 * devices)) * 16
    blocks = jnp.concatenate(
        [part.astype(BF16) for part in packed]
        + [jnp.zeros((each * devices - packed_rows, width), BF16)],
        axis=0,
    ).reshape(devices, each, width)
    if split_four:
        grad_normed_mamba, summed, mamba_grads = matmul_sum(
            [grad_conv_low, grad_gate_low],
            in_full,
            0,
            11,
            small=blocks,
            pairs=mamba_pairs,
            scatter=True,
        )
    else:
        grad_normed_mamba, summed = matmul_sum(
            [grad_conv_low, grad_gate_low], in_full, 0, 11, small=blocks
        )
        mamba_grads = scattered(weight_grads(mamba_pairs, 256), ("dp", "seq"))
    input_grad, _, grad_gain_mamba = norm_back(stream_zero, gain_mamba, grad_normed_mamba, grad_one)
    summed = summed.reshape(devices * each, width).astype(F32)

    def unpack(rows, shapes):
        parts = []
        first = 0
        for part in shapes:
            parts.append(rows[first : first + part.shape[0]])
            first += part.shape[0]
        return parts

    sum_select, sum_step_weight, sum_decay_log, loose_sums = unpack(summed, packed)
    (
        sum_kernel,
        sum_conv_bias,
        sum_step_bias,
        sum_skip,
        sum_loss,
        sum_attn,
        sum_first,
        sum_second,
    ) = unpack(loose_sums, loose)
    loss_total = sum_loss[0, 0]
    sum_mamba = jnp.sum(direct_gather(grad_gain_mamba.reshape(8, -1), ("dp", "seq"), 5), axis=0)
    gain_rows = mamba_norm.shape[0]
    place = lax.axis_index("dp") * seq_count + seq_place
    grad_qkv, grad_attn_out = split(attn_grads, attn_qkv, attn_out)
    grad_out, gate_half, conv_half = split(
        mamba_grads, mamba_out, mamba_in[:, 1], mamba_in[:, 0]
    )
    grad_in = jnp.stack([conv_half, gate_half], axis=1)
    grad_first_both, grad_first_down = split(first_grads, first_gate_up, first_down)

    def own(whole_gain):
        return lax.dynamic_slice_in_dim(whole_gain.reshape(-1), place * gain_rows, gain_rows)

    return (
        loss_total,
        stream_four.astype(BF16)[None],
        input_grad[None],
        own(sum_mamba),
        grad_in,
        sum_kernel,
        sum_conv_bias[0],
        sum_select.T,
        sum_step_weight,
        sum_step_bias[0],
        sum_decay_log,
        sum_skip[0],
        grad_out,
        own(sum_attn),
        grad_qkv,
        grad_attn_out,
        own(sum_first),
        grad_first_both,
        grad_first_down,
        own(sum_second),
        second_both,
        second_down_grad,
    )


def solution(mesh):
    placed = (
        P("dp", "seq", None),
        P("dp", "seq", None),
        P(),
        P(("dp", "seq")),
        P(("dp", "seq"), None, "tensor"),
        P(None, "tensor"),
        P("tensor"),
        P("tensor", None),
        P(None, "tensor"),
        P("tensor"),
        P(None, "tensor"),
        P("tensor"),
        P(("dp", "seq"), "tensor"),
        P(("dp", "seq")),
        P(("dp", "seq"), None, "tensor"),
        P(("dp", "seq"), "tensor"),
        P(("dp", "seq")),
        P(("dp", "seq"), None, "tensor"),
        P(("dp", "seq"), "tensor"),
        P(("dp", "seq")),
        P(("dp", "seq"), None, "tensor"),
        P(("dp", "seq"), "tensor"),
    )
    return jax.shard_map(
        shards,
        mesh=mesh,
        in_specs=placed,
        out_specs=(
            P(),
            P("dp", "seq", None),
            P("dp", "seq", None),
            P(("dp", "seq")),
            P(("dp", "seq"), None, "tensor"),
            P(None, "tensor"),
            P("tensor"),
            P("tensor", None),
            P(None, "tensor"),
            P("tensor"),
            P(None, "tensor"),
            P("tensor"),
            P(("dp", "seq"), "tensor"),
            P(("dp", "seq")),
            P(("dp", "seq"), None, "tensor"),
            P(("dp", "seq"), "tensor"),
            P(("dp", "seq")),
            P(("dp", "seq"), None, "tensor"),
            P(("dp", "seq"), "tensor"),
            P(("dp", "seq")),
            P(("dp", "seq"), None, "tensor"),
            P(("dp", "seq"), "tensor"),
        ),
        check_vma=False,
    )
```

time: 3060 us -> 1180 us (0.39)
  waiting for transfers between devices: 1500 us -> 38.2 us
  Pallas kernels: 0 us -> 911 us
  other arithmetic: 527 us -> 61.1 us
  local copies, waits for them, and re-layouts: 464 us -> 115 us
  matrix products: 366 us -> 24.9 us
  blocking collectives: 84.8 us -> 0 us
  starting transfers between devices: 46.5 us -> 4.59 us
    pallas_call x0 -> x30, Pallas kernels: none -> 911 us  [the longest x8 521 us: matmul_sum(): pl.pallas_call(functools.partial(matmul_sum_kernel, columns=columns, firs...]
    psum x11 -> x0, waiting for transfers between devices: 597 us -> none  [the longest x5 334 us: tensor_forward_sum(): lax.psum(partial_sum.astype(jnp.bfloat16), 'tensor').astype(jnp.float32)]
    reduce_scatter x8 -> x3, waiting for transfers between devices: 520 us -> 38.1 us  [scattered(): lax.psum_scatter(grads, axes, scatter_dimension=0, tiled=True)]
    all_gather x8 -> x3, waiting for transfers between devices: 333 us -> 0.01 us  [gather_joined(): return lax.all_gather(joined, ('dp', 'seq'), axis=0, tiled=True)]
    dot_general x30 -> x4, matrix products: 294 us -> 18.9 us  [product(): return jnp.dot(left, right, preferred_element_type=F32)]
    reduce_sum x443 -> x2, other arithmetic: 275 us -> 0.64 us  [the longest x1 0.63 us: shards(): total_valid = jnp.sum(valid_length).astype(F32)]
    slice x178 -> x8, local copies, waits for them, and re-layouts: 192 us -> 5.71 us  [the longest x4 2.68 us: unpack(): parts.append(rows[first:first + part.shape[0]])]
    mul x144 -> x0, local copies, waits for them, and re-layouts: 86 us -> none  [the longest x96 68.1 us: advance(): in_rows[position][:, None]]
  transfers between devices with their start and end apart: 47 -> 8, of which waited for: 28 -> 2; matrix products, arithmetic and copies ran while one was open for 29% -> 11% of each run, Pallas kernels for 0% -> 62%
where the time goes in v1:
time: 1180 us; the launch traced here: 1170 us
  Pallas kernels  911 us (77%)
  local copies, waits for them, and re-layouts  115 us (10%)
  other arithmetic  61.1 us (5%)
  waiting for transfers between devices  38.2 us (3%)
  matrix products  24.9 us (2%)
  between operations  17.6 us (1%)
    pallas_call x8, Pallas kernels, matmul_sum(): pl.pallas_call(functools.partial(matmul_sum_kernel, columns=columns, firs...  521 us
    unnamed x246, local copies, waits for them, and re-layouts  80.5 us
    pallas_call x1, Pallas kernels, attend(): pl.pallas_call(functools.partial(attend_kernel, count=lax.axis_size('seq'...  74 us
    pallas_call x1, Pallas kernels, attend_back(): pl.pallas_call(functools.partial(attend_back_kernel, count=lax.axis_size(...  69.7 us
    pallas_call x1, Pallas kernels, first_gather(): pl.pallas_call(first_gather_kernel, in_specs=[whole, whole, far], out_spe...  42.1 us
    reduce_scatter x3, waiting for transfers between devices, scattered(): lax.psum_scatter(grads, axes, scatter_dimension=0, tiled=True)  38.1 us
    pallas_call x2, Pallas kernels, tensor_sum(): pl.pallas_call(functools.partial(ar_kernel, pieces=pieces, rows=rows // p...  36.7 us
    pallas_call x1, Pallas kernels, shards(): run_back(step_size, inputs, grad_scanned, in_wide, out_wide, rate_two, ke...  35.8 us
  transfers between devices with their start and end apart: 8, of which 2 were waited for; matrix products, arithmetic and copies ran while one was open for 11% of the time, Pallas kernels for 62%

profile of v1, /device:TPU:0, one launch (start us, length us, event | category | flops | bytes accessed | tf_op | source)
XLA Modules:
  0.0 1172.1 jit_solution(3849500408692758221)
XLA Ops:
  15.7 42.1 %first_gather.1 = (bf16[2048,2048]{1,0:T(8,128)(2,1)S(1)}, f32[8,8,256]{2,1,0:T(8,128)S(1)}, bf16[528,2048]{1,0:T(8,128)(2,1)S(1)}) custom-call(bf16[528,2048]{1,0:T(8,128)(2,1)S(1)} %bitcast.142, f32[8,256]{1,0:T(8,128)S(1)} %fusion.40.gains_ref, bf16[256,2048]{1,0:T(8,128)(2,1)S(1)} %bitcast.147), custom_call_target="tpu_custom_call" | custom-call | flops 420000000 | tf_op jit(solution)/shard_map/first_gather/pallas_call | solution.py:1558
  57.8 3.3 copy-done.37
  62.6 10.1 convolution_convert_fusion.gate_ref
  81.4 2.8 collective-permute-start
  95.1 4.2 fusion.47
  102.7 18.6 %tensor_sum.2 = bf16[528,256]{1,0:T(8,128)(2,1)S(1)} custom-call(bf16[528,256]{1,0:T(8,128)(2,1)S(1)} %pad.36.x_ref), custom_call_target="tpu_custom_call" | custom-call | flops 160000000 | tf_op jit(solution)/shard_map/tensor_sum/pallas_call | solution.py:348
  125.9 6.8 scan_state.1
  132.8 7.0 gather_seq.2
  140.4 3.1 broadcast_in_dim.25.c_ref
  143.6 18.8 %scan_rows.1 = (f32[528,1024]{1,0:T(8,128)S(1)}, f32[528,16,1024]{2,1,0:T(8,128)}) custom-call(f32[528,1024]{1,0:T(8,128)S(1)} %get-tuple-element.228.dt_ref, f32[528,1024]{1,0:T(8,128)S(1)} %convert_multiply_fusion.1.dtx_ref, f32[528,16,128]{2,1,0:T(8,128)S(1)} %broadcast_in_dim.24.b_ref, f32[528,16,128]{2,1,0:T(8,128)} %broadcast_in_dim.25.c_ref, ...), custom_call_target="tpu_custom_call" | custom-call | flops 180000000 | tf_op jit(solution)/shard_map/scan_rows/pallas_call | solution.py:1737
  166.1 57.0 %matmul_sum.4 = bf16[528,2048]{1,0:T(8,128)(2,1)S(1)} custom-call(bf16[528,1024]{1,0:T(8,128)(2,1)S(1)} %copy-done.25, bf16[2048,3072]{1,0:T(8,128)(2,1)} %all-gather.4.cloned.1.call-done.refs_1_.w_ref), custom_call_target="tpu_custom_call" | custom-call | flops 580000000 | tf_op jit(solution)/shard_map/matmul_sum/pallas_call | solution.py:1378
  226.1 7.1 qkv_rows.1
  233.2 74.0 %attend.1 = (f32[528,512]{1,0:T(8,128)S(1)}, bf16[528,512]{1,0:T(8,128)(2,1)S(1)}, f32[4,528,128]{2,1,0:T(8,128)S(1)}, bf16[3,2,528,512]{3,2,1,0:T(8,128)(2,1)}) custom-call(bf16[528,512]{1,0:T(8,128)(2,1)S(1)} %get-tuple-element.93.q_ref, bf16[2,528,512]{2,1,0:T(8,128)(2,1)S(1)} %get-tuple-element.94.kv_ref), custom_call_target="tpu_custom_call" | custom-call | flops 550000000 | tf_op jit(solution)/shard_map/attend/pallas_call | solution.py:537
  307.3 58.8 %matmul_sum.5 = bf16[528,2048]{1,0:T(8,128)(2,1)S(1)} custom-call(bf16[528,512]{1,0:T(8,128)(2,1)S(1)} %get-tuple-element.95.refs_0_.refs_4_, bf16[2048,3072]{1,0:T(8,128)(2,1)} %all-gather.4.cloned.1.call-done.refs_1_.w_ref), custom_call_target="tpu_custom_call" | custom-call | flops 580000000 | tf_op jit(solution)/shard_map/matmul_sum/pallas_call | solution.py:1378
  366.2 3.6 multiply_reduce_fusion.2
  375.3 13.6 %gate_up.2 = (bf16[528,2048]{1,0:T(8,128)(2,1)S(1)}, bf16[528,2048]{1,0:T(8,128)(2,1)S(1)}, bf16[528,2048]{1,0:T(8,128)(2,1)S(1)}) custom-call(bf16[528,2048]{1,0:T(8,128)(2,1)S(1)} %copy-done.16, bf16[2048,6144]{1,0:T(8,128)(2,1)} %all-gather.6.cloned.1.call-done.wg_ref.wu_ref.refs_1_.w_ref.refs_2_, ...), custom_call_target="tpu_custom_call" | custom-call | flops 140000000 | tf_op jit(solution)/shard_map/gate_up/pallas_call | solution.py:817
  391.6 58.9 %matmul_sum.6 = bf16[528,2048]{1,0:T(8,128)(2,1)S(1)} custom-call(bf16[528,2048]{1,0:T(8,128)(2,1)S(1)} %get-tuple-element.98.refs_0_.refs_5_, bf16[2048,6144]{1,0:T(8,128)(2,1)} %all-gather.6.cloned.1.call-done.wg_ref.wu_ref.refs_1_.w_ref.refs_2_), custom_call_target="tpu_custom_call" | custom-call | flops 580000000 | tf_op jit(solution)/shard_map/matmul_sum/pallas_call | solution.py:1378
  456.6 13.4 %gate_up.3 = (bf16[528,2048]{1,0:T(8,128)(2,1)S(1)}, bf16[528,2048]{1,0:T(8,128)(2,1)S(1)}, bf16[528,2048]{1,0:T(8,128)(2,1)S(1)}) custom-call(bf16[528,2048]{1,0:T(8,128)(2,1)S(1)} %copy-done.18, bf16[2048,6144]{1,0:T(8,128)(2,1)} %all-gather.8.cloned.1.call-done.wg_ref.wu_ref.refs_1_.w_ref.refs_2_, ...), custom_call_target="tpu_custom_call" | custom-call | flops 140000000 | tf_op jit(solution)/shard_map/gate_up/pallas_call | solution.py:817
  470.0 57.5 %matmul_sum.7 = bf16[528,2048]{1,0:T(8,128)(2,1)S(1)} custom-call(bf16[528,2048]{1,0:T(8,128)(2,1)S(1)} %get-tuple-element.101.refs_0_.refs_5_, bf16[2048,6144]{1,0:T(8,128)(2,1)} %all-gather.8.cloned.1.call-done.wg_ref.wu_ref.refs_1_.w_ref.refs_2_), custom_call_target="tpu_custom_call" | custom-call | flops 580000000 | tf_op jit(solution)/shard_map/matmul_sum/pallas_call | solution.py:1378
  527.5 3.7 multiply_reduce_fusion
  531.2 3.0 broadcast_multiply_fusion
  534.1 10.5 hidden_back.2
  544.6 64.9 %matmul_sum_grads.3 = (bf16[528,2048]{1,0:T(8,128)(2,1)S(1)}, bf16[2048,6144]{1,0:T(8,128)(2,1)}) custom-call(bf16[528,2048]{1,0:T(8,128)(2,1)S(1)} %get-tuple-element.104.refs_0_, bf16[528,2048]{1,0:T(8,128)(2,1)S(1)} %get-tuple-element.105.refs_1_, bf16[2048,6144]{1,0:T(8,128)(2,1)} %all-gather.8.cloned.1.call-done.wg_ref.wu_ref.refs_1_.w_ref.refs_2_, ...), custom_call_target="tpu_custom_call" | custom-call | flops 670000000 | tf_op jit(solution)/shard_map/matmul_sum_grads/pallas_call | solution.py:1378
  617.0 3.1 norm_back.4
  622.6 11.7 hidden_back.3
  634.3 67.0 %matmul_sum_grads.4 = (bf16[528,2048]{1,0:T(8,128)(2,1)S(1)}, bf16[2048,6144]{1,0:T(8,128)(2,1)}) custom-call(bf16[528,2048]{1,0:T(8,128)(2,1)S(1)} %get-tuple-element.110.refs_0_, bf16[528,2048]{1,0:T(8,128)(2,1)S(1)} %get-tuple-element.111.refs_1_, bf16[2048,6144]{1,0:T(8,128)(2,1)} %all-gather.6.cloned.1.call-done.wg_ref.wu_ref.refs_1_.w_ref.refs_2_, ...), custom_call_target="tpu_custom_call" | custom-call | flops 670000000 | tf_op jit(solution)/shard_map/matmul_sum_grads/pallas_call | solution.py:1378
  709.1 3.1 norm_back.5
  712.3 4.8 fusion.11.g_ref
  717.3 69.7 %attend_back.1.refs_0_ = bf16[528,1536]{1,0:T(8,128)(2,1)} custom-call(bf16[528,512]{1,0:T(8,128)(2,1)S(1)} %copy-done.72, bf16[528,512]{1,0:T(8,128)(2,1)S(1)} %fusion.11.g_ref, f32[528,512]{1,0:T(8,128)S(1)} %copy-done.66, f32[4,528,128]{2,1,0:T(8,128)S(1)} %copy-done.68, bf16[2,528,512]{2,1,0:T(8,128)(2,1)S(1)} %copy-done.64, ...), custom_call_target="tpu_custom_call" | custom-call | flops 550000000 | tf_op jit(solution)/shard_map/attend_back/pallas_call | solution.py:706
  787.0 22.6 %reduce-scatter.4.cloned.1.call-done = bf16[256,6144]{1,0:T(8,128)(2,1)} async-done(((bf16[2048,6144]{1,0:T(8,128)(2,1)}), bf16[256,6144]{1,0:T(8,128)(2,1)}) %reduce-scatter.4.cloned.1.call-update) | async-done | bytes 3145744 | tf_op jit(solution)/shard_map/reduce_scatter | solution.py:1443
  815.3 61.1 %matmul_sum_grads.5 = (bf16[528,2048]{1,0:T(8,128)(2,1)S(1)}, bf16[2048,2048]{1,0:T(8,128)(2,1)}) custom-call(bf16[528,1536]{1,0:T(8,128)(2,1)S(1)} %copy-done.38, bf16[2048,3072]{1,0:T(8,128)(2,1)} %all-gather.4.cloned.1.call-done.refs_1_.w_ref, bf16[528,2048]{1,0:T(8,128)(2,1)S(1)} %copy-done.21, bf16[528,2048]{1,0:T(8,128)(2,1)S(1)} %copy-done.45, ...), custom_call_target="tpu_custom_call" | custom-call | flops 670000000 | tf_op jit(solution)/shard_map/matmul_sum_grads/pallas_call | solution.py:1378
  887.5 3.1 norm_back.6
  895.1 5.7 gate_back.1
  901.9 6.9 scan_back_state.1.block_ref
  908.8 9.7 gather_seq.3
  918.7 35.8 %scan_back.1 = (f32[528,1024]{1,0:T(8,128)S(1)}, f32[528,1024]{1,0:T(8,128)S(1)}, f32[528,16]{1,0:T(8,128)S(1)}, f32[528,16]{1,0:T(8,128)S(1)}, f32[16,1024]{1,0:T(8,128)S(1)}) custom-call(f32[528,1024]{1,0:T(8,128)S(1)} %copy-done.9, f32[528,1024]{1,0:T(8,128)S(1)} %copy-done.31, f32[528,1024]{1,0:T(8,128)S(1)} %get-tuple-element.123.g_ref, ...), custom_call_target="tpu_custom_call" | custom-call | flops 360000000 | tf_op jit(solution)/shard_map/scan_back/pallas_call | solution.py:1801
  957.2 15.6 %reduce-scatter.6.cloned.1.call-done = bf16[256,6144]{1,0:T(8,128)(2,1)} async-done(((bf16[2048,6144]{1,0:T(8,128)(2,1)}), bf16[256,6144]{1,0:T(8,128)(2,1)}) %reduce-scatter.6.cloned.1.call-update) | async-done | bytes 3145744 | tf_op jit(solution)/shard_map/reduce_scatter | solution.py:1443
  972.8 3.0 fusion.45
  976.5 18.1 %tensor_sum.3 = bf16[528,256]{1,0:T(8,128)(2,1)S(1)} custom-call(bf16[528,256]{1,0:T(8,128)(2,1)S(1)} %fusion.21.x_ref), custom_call_target="tpu_custom_call" | custom-call | flops 160000000 | tf_op jit(solution)/shard_map/tensor_sum/pallas_call | solution.py:348
  994.7 4.0 multiply_reduce_fusion.4
  1005.8 3.4 slice_convert_fusion
  1018.6 7.6 copy.67
  1026.2 5.2 copy.68
  1033.3 5.3 concatenate.35
  1040.6 95.7 %matmul_sum_small.1 = (bf16[528,2048]{1,0:T(8,128)(2,1)S(1)}, bf16[8,48,1024]{2,1,0:T(8,128)(2,1)S(1)}, bf16[256,3072]{1,0:T(8,128)(2,1)S(1)}) custom-call(bf16[528,1024]{1,0:T(8,128)(2,1)S(1)} %fusion.7.refs_0_, bf16[528,1024]{1,0:T(8,128)(2,1)S(1)} %copy-done.62, bf16[2048,2048]{1,0:T(8,128)(2,1)} %copy-done.37, bf16[8,48,1024]{2,1,0:T(8,128)(2,1)S(1)} %bitcast.148, ...), custom_call_target="tpu_custom_call" | custom-call | flops 670000000 | tf_op jit(solution)/shard_map/matmul_sum_small/pallas_call | solution.py:1378
  1139.4 6.1 norm_back.7
  1146.7 5.0 gather_dp_seq.1
  1154.4 2.9 copy.66
  (363 shorter events, 135.7 us)
Async XLA Ops:
  7.2 93.1 %copy-start = (bf16[1024,160]{0,1:T(8,128)(2,1)S(1)}, bf16[1024,160]{0,1:T(8,128)(2,1)}, u32[]{:S(2)}) copy-start(bf16[1024,160]{0,1:T(8,128)(2,1)} %param.29) | copy-start | bytes 983044
  7.2 157.7 %all-gather.4.cloned.1.call-start = ((), (), s32[]{:S(2)}) async-start(), calls=%async_computation.3 | async-start | bytes 14155776 | tf_op jit(solution)/shard_map/all_gather | solution.py:401
  62.6 311.1 %all-gather.6.cloned.1.call-start = ((), (), s32[]{:S(2)}) async-start(), calls=%async_computation.4 | async-start | bytes 28311552 | tf_op jit(solution)/shard_map/all_gather | solution.py:401
  76.1 378.9 %all-gather.8.cloned.1.call-start = ((), (), s32[]{:S(2)}) async-start(), calls=%async_computation.5 | async-start | bytes 28311552 | tf_op jit(solution)/shard_map/all_gather | solution.py:401
  80.6 728.9 %reduce-scatter.4.cloned.1.call-start = ((), (), s32[]{:S(2)}) async-start(), calls=%async_computation.6 | async-start | bytes 28311552 | tf_op jit(solution)/shard_map/reduce_scatter | solution.py:1443
  81.4 12.0 %collective-permute-start = (bf16[3,1024]{1,0:T(4,128)(2,1)S(1)}, bf16[3,1024]{1,0:T(4,128)(2,1)S(1)}, u32[]{:S(2)}, u32[]{:S(2)}) collective-permute-start(bf16[3,1024]{1,0:T(4,128)(2,1)S(1)} %slice.194), channel_id=1, source_target_pairs={{0,4},{4,8},{8,12},{1,5},{5,9},{9,13},{2,6},{6,10},{10,14},{3,7},{... | collective-permute-start | bytes 18440 | tf_op jit(solution)/shard_map/ppermute | solution.py:366
  101.5 20.0 %copy-start.106 = (f32[1024]{0:T(1024)S(1)}, f32[1024]{0:T(1024)}, u32[]{:S(2)}) copy-start(f32[1024]{0:T(1024)} %param.31) | copy-start | bytes 12292
  102.6 18.9 %copy-start.87 = (bf16[128,1024]{1,0:T(8,128)(2,1)S(1)}, bf16[128,1024]{1,0:T(8,128)(2,1)}, u32[]{:S(2)}) copy-start(bf16[128,1024]{1,0:T(8,128)(2,1)} %param.30) | copy-start | bytes 786436
  124.2 19.3 %copy-start.8 = (f32[528,1024]{1,0:T(8,128)}, f32[528,1024]{1,0:T(8,128)S(1)}, u32[]{:S(2)}) copy-start(f32[528,1024]{1,0:T(8,128)S(1)} %get-tuple-element.228.dt_ref) | copy-start | bytes 6488068
  125.9 17.7 %copy-start.1 = (f32[528,16,128]{2,1,0:T(8,128)}, f32[528,16,128]{2,1,0:T(8,128)S(1)}, u32[]{:S(2)}) copy-start(f32[528,16,128]{2,1,0:T(8,128)S(1)} %broadcast_in_dim.24.b_ref) | copy-start | bytes 12976132
  143.6 18.8 %copy-start.27 = (bf16[528,2048]{1,0:T(8,128)(2,1)S(1)}, bf16[528,2048]{1,0:T(8,128)(2,1)}, u32[]{:S(2)}) copy-start(bf16[528,2048]{1,0:T(8,128)(2,1)} %convolution_convert_fusion.gate_ref) | copy-start | bytes 6488068
  143.6 18.8 %copy-start.103 = (f32[1024]{0:T(1024)S(1)}, f32[1024]{0:T(1024)}, u32[]{:S(2)}) copy-start(f32[1024]{0:T(1024)} %param.33) | copy-start | bytes 12292
  166.1 59.4 %slice-start = ((s8[12582912]{0:T(1024)(128)(4,1)}), s8[4194304]{0:T(1024)(128)(4,1)S(1)}, s32[]{:S(2)}) async-start(s8[12582912]{0:T(1024)(128)(4,1)} %bitcast.138), calls=%async_computation.9 | async-start | bytes 8388608
  166.1 59.4 %slice-start.1 = ((s8[12582912]{0:T(1024)(128)(4,1)}), s8[4194304]{0:T(1024)(128)(4,1)S(1)}, s32[]{:S(2)}) async-start(s8[12582912]{0:T(1024)(128)(4,1)} %bitcast.138), calls=%async_computation.10 | async-start | bytes 8388608
  233.2 133.0 %copy-start.63 = (bf16[2,528,512]{2,1,0:T(8,128)(2,1)}, bf16[2,528,512]{2,1,0:T(8,128)(2,1)S(1)}, u32[]{:S(2)}) copy-start(bf16[2,528,512]{2,1,0:T(8,128)(2,1)S(1)} %get-tuple-element.94.kv_ref) | copy-start | bytes 3244036
  233.2 133.0 %copy-start.71 = (bf16[528,512]{1,0:T(8,128)(2,1)}, bf16[528,512]{1,0:T(8,128)(2,1)S(1)}, u32[]{:S(2)}) copy-start(bf16[528,512]{1,0:T(8,128)(2,1)S(1)} %get-tuple-element.93.q_ref) | copy-start | bytes 1622020
  307.3 58.9 %copy-start.58 = (bf16[528,512]{1,0:T(8,128)(2,1)}, bf16[528,512]{1,0:T(8,128)(2,1)S(1)}, u32[]{:S(2)}) copy-start(bf16[528,512]{1,0:T(8,128)(2,1)S(1)} %get-tuple-element.95.refs_0_.refs_4_) | copy-start | bytes 1622020
  307.3 58.9 %copy-start.65 = (f32[528,512]{1,0:T(8,128)}, f32[528,512]{1,0:T(8,128)S(1)}, u32[]{:S(2)}) copy-start(f32[528,512]{1,0:T(8,128)S(1)} %get-tuple-element.115.o_ref) | copy-start | bytes 3244036
  307.3 58.9 %copy-start.67 = (f32[4,528,128]{2,1,0:T(8,128)}, f32[4,528,128]{2,1,0:T(8,128)S(1)}, u32[]{:S(2)}) copy-start(f32[4,528,128]{2,1,0:T(8,128)S(1)} %get-tuple-element.116.lse_ref) | copy-start | bytes 3244036
  307.3 58.9 %copy-start.12 = (bf16[528,2048]{1,0:T(8,128)(2,1)S(1)}, bf16[528,2048]{1,0:T(8,128)(2,1)}, u32[]{:S(2)}) copy-start(bf16[528,2048]{1,0:T(8,128)(2,1)} %copy-done.11) | copy-start | bytes 6488068
  391.6 58.9 %copy-start.29 = (bf16[528,2048]{1,0:T(8,128)(2,1)}, bf16[528,2048]{1,0:T(8,128)(2,1)S(1)}, u32[]{:S(2)}) copy-start(bf16[528,2048]{1,0:T(8,128)(2,1)S(1)} %get-tuple-element.98.refs_0_.refs_5_) | copy-start | bytes 6488068
  391.6 58.9 %copy-start.3 = (f32[528,2048]{1,0:T(8,128)S(1)}, f32[528,2048]{1,0:T(8,128)}, u32[]{:S(2)}) copy-start(f32[528,2048]{1,0:T(8,128)} %copy-done.2) | copy-start | bytes 12976132
  470.0 57.5 %copy-start.30 = (bf16[528,2048]{1,0:T(8,128)(2,1)}, bf16[528,2048]{1,0:T(8,128)(2,1)S(1)}, u32[]{:S(2)}) copy-start(bf16[528,2048]{1,0:T(8,128)(2,1)S(1)} %get-tuple-element.101.refs_0_.refs_5_) | copy-start | bytes 6488068
  470.0 57.5 %copy-start.6 = (f32[528,2048]{1,0:T(8,128)S(1)}, f32[528,2048]{1,0:T(8,128)}, u32[]{:S(2)}) copy-start(f32[528,2048]{1,0:T(8,128)} %copy-done.5) | copy-start | bytes 12976132
  470.0 57.5 %copy-start.80 = (bf16[1,528,2048]{2,1,0:T(8,128)(2,1)S(1)}, bf16[1,528,2048]{2,1,0:T(8,128)(2,1)}, u32[]{:S(2)}) copy-start(bf16[1,528,2048]{2,1,0:T(8,128)(2,1)} %param.23) | copy-start | bytes 6488068
  610.9 361.9 %reduce-scatter.6.cloned.1.call-start = ((), (), s32[]{:S(2)}) async-start(), calls=%async_computation.7 | async-start | bytes 28311552 | tf_op jit(solution)/shard_map/reduce_scatter | solution.py:1443
  702.6 458.8 %reduce-scatter.8.cloned.1.call-start = ((), (), s32[]{:S(2)}) async-start(), calls=%async_computation.8 | async-start | bytes 9437184 | tf_op jit(solution)/shard_map/reduce_scatter | solution.py:1443
  887.5 14.3 %slice-start.3 = ((s8[4325376]{0:T(1024)(128)(4,1)}), s8[4194304]{0:T(1024)(128)(4,1)S(1)}, s32[]{:S(2)}) async-start(s8[4325376]{0:T(1024)(128)(4,1)} %bitcast.140), calls=%async_computation.12 | async-start | bytes 8388608
  901.8 16.8 %copy-start.33 = (f32[528,1024]{1,0:T(8,128)}, f32[528,1024]{1,0:T(8,128)S(1)}, u32[]{:S(2)}) copy-start(f32[528,1024]{1,0:T(8,128)S(1)} %get-tuple-element.123.g_ref) | copy-start | bytes 6488068
  901.8 16.7 %copy-start.83 = (f32[16,1024]{1,0:T(8,128)S(1)}, f32[16,1024]{1,0:T(8,128)}, u32[]{:S(2)}) copy-start(f32[16,1024]{1,0:T(8,128)} %param.32) | copy-start | bytes 196612
  901.8 16.7 %copy-start.90 = (f32[1,1,1024]{2,1,0:T(1,128)S(1)}, f32[1,1,1024]{2,1,0:T(1,128)}, u32[]{:S(2)}) copy-start(f32[1,1,1024]{2,1,0:T(1,128)} %copy-done.89) | copy-start | bytes 12292
  901.9 16.7 %copy-start.92 = (f32[1,1,1024]{2,1,0:T(1,128)S(1)}, f32[1,1,1024]{2,1,0:T(1,128)}, u32[]{:S(2)}) copy-start(f32[1,1,1024]{2,1,0:T(1,128)} %copy-done.91) | copy-start | bytes 12292
  901.9 16.7 %copy-start.101 = (f32[1,1,1024]{2,1,0:T(1,128)S(1)}, f32[1,1,1024]{2,1,0:T(1,128)}, u32[]{:S(2)}) copy-start(f32[1,1,1024]{2,1,0:T(1,128)} %get-tuple-element.261) | copy-start | bytes 12292
  901.9 16.8 %copy-start.31 = (f32[528,1024]{1,0:T(8,128)S(1)}, f32[528,1024]{1,0:T(8,128)}, u32[]{:S(2)}) copy-start(f32[528,1024]{1,0:T(8,128)} %get-tuple-element.229.x_ref) | copy-start | bytes 6488068
  918.6 54.2 %copy-start.107 = (f32[1024]{0:T(1024)S(1)}, f32[1024]{0:T(1024)}, u32[]{:S(2)}) copy-start(f32[1024]{0:T(1024)} %param.31) | copy-start | bytes 12292
  972.8 21.8 %copy-start.74 = (f32[528,1024]{1,0:T(8,128)S(1)}, f32[528,1024]{1,0:T(8,128)}, u32[]{:S(2)}) copy-start(f32[528,1024]{1,0:T(8,128)} %copy-done.73) | copy-start | bytes 6488068
  972.8 21.8 %copy-start.76 = (f32[531,1024]{1,0:T(8,128)S(1)}, f32[531,1024]{1,0:T(8,128)}, u32[]{:S(2)}) copy-start(f32[531,1024]{1,0:T(8,128)} %copy-done.75) | copy-start | bytes 6524932
  975.8 18.8 %copy-start.34 = (f32[528,1024]{1,0:T(8,128)S(1)}, f32[528,1024]{1,0:T(8,128)}, u32[]{:S(2)}) copy-start(f32[528,1024]{1,0:T(8,128)} %copy-done.33) | copy-start | bytes 6488068
  975.8 18.8 %copy-start.94 = (f32[1,1024]{1,0:T(1,128)S(1)}, f32[1,1024]{1,0:T(1,128)}, u32[]{:S(2)}) copy-start(f32[1,1024]{1,0:T(1,128)} %copy-done.93) | copy-start | bytes 12292
  975.9 18.8 %copy-start.96 = (f32[1,1024]{1,0:T(1,128)S(1)}, f32[1,1024]{1,0:T(1,128)}, u32[]{:S(2)}) copy-start(f32[1,1024]{1,0:T(1,128)} %copy-done.95) | copy-start | bytes 12292
  975.9 18.8 %copy-start.98 = (f32[1,1024]{1,0:T(1,128)S(1)}, f32[1,1024]{1,0:T(1,128)}, u32[]{:S(2)}) copy-start(f32[1,1024]{1,0:T(1,128)} %copy-done.97) | copy-start | bytes 12292
  975.9 18.8 %copy-start.100 = (f32[1,1024]{1,0:T(1,128)S(1)}, f32[1,1024]{1,0:T(1,128)}, u32[]{:S(2)}) copy-start(f32[1,1024]{1,0:T(1,128)} %copy-done.99) | copy-start | bytes 12292
  975.9 18.8 %copy-start.104 = (f32[1024]{0:T(1024)S(1)}, f32[1024]{0:T(1024)}, u32[]{:S(2)}) copy-start(f32[1024]{0:T(1024)} %param.33) | copy-start | bytes 12292
  999.3 39.2 %collective-permute-start.1 = (f32[3,1024]{1,0:T(4,128)}, f32[3,1024]{1,0:T(4,128)}, u32[]{:S(2)}, u32[]{:S(2)}) collective-permute-start(f32[3,1024]{1,0:T(4,128)} %pad_add_fusion.1), channel_id=1, source_target_pairs={{4,0},{8,4},{12,8},{5,1},{9,5},{13,9},{6,2},{10,6},{14,10},{7,3},{... | collective-permute-start | bytes 36872 | tf_op jit(solution)/shard_map/ppermute | solution.py:366
  1040.5 98.8 %slice-start.5 = ((s8[4325376]{0:T(1024)(128)(4,1)}), s8[4194304]{0:T(1024)(128)(4,1)S(1)}, s32[]{:S(2)}) async-start(s8[4325376]{0:T(1024)(128)(4,1)} %bitcast.143), calls=%async_computation.14 | async-start | bytes 8388608
  1040.6 98.8 %slice-start.7 = ((s8[4325376]{0:T(1024)(128)(4,1)}), s8[4194304]{0:T(1024)(128)(4,1)S(1)}, s32[]{:S(2)}) async-start(s8[4325376]{0:T(1024)(128)(4,1)} %bitcast.145), calls=%async_computation.16 | async-start | bytes 8388608
  1040.6 98.8 %slice-start.6 = ((s8[4325376]{0:T(1024)(128)(4,1)}), s8[131072]{0:T(1024)(128)(4,1)S(1)}, s32[]{:S(2)}) async-start(s8[4325376]{0:T(1024)(128)(4,1)} %bitcast.143), calls=%async_computation.15 | async-start | bytes 262144
  1040.6 98.8 %slice-start.8 = ((s8[4325376]{0:T(1024)(128)(4,1)}), s8[131072]{0:T(1024)(128)(4,1)S(1)}, s32[]{:S(2)}) async-start(s8[4325376]{0:T(1024)(128)(4,1)} %bitcast.145), calls=%async_computation.17 | async-start | bytes 262144
  (78 other events, 325.8 us)
Sparse Core Ops, SparseCore 0:
  62.7 72.4 all-gather.3
  137.6 167.9 all-gather.5
  308.1 129.5 all-gather.7
  611.0 198.5 reduce-scatter.3
  813.0 159.7 reduce-scatter.5
  976.1 71.3 reduce-scatter.7

commit v2 on v1

--- a/solution.py
+++ b/solution.py
@@ -1014,8 +1014,8 @@
 
 
 class ScatterGrads(OwnGrads):
-    lags = (1, 3, 4)
-    lag = 4
+    lags = (1, 3, 5)
+    lag = 5
 
     def __init__(self, lefts, rights, uses, counts, tile, out_ref, scratch):
         self.lefts, self.rights, self.uses, self.counts, self.tile = lefts, rights, uses, counts, tile
@@ -1284,7 +1284,7 @@
             for r in range(splits):
                 send_a(j, r).start()
 
-        each = -(-(job.total + job.lag) // tiles) if uses else 0
+        each = (job.total + job.lag) // tiles if uses else 0
         for r in range(max(splits, each)):
             if r < splits:
 
@@ -1315,6 +1315,13 @@
     def _():
         for r in range(splits - lag, splits):
             second_sum(tiles - 1, r)
+
+    if uses:
+        for t in range((job.total + job.lag) // tiles * tiles, job.total + job.lag):
+            job.step(t)
+
+    @pl.when(inner)
+    def _():
 
         def finish(j, carry):
             for r in range(splits):
@@ -1811,7 +1818,15 @@
     grad_selected = tensor_backward_sum(
         jnp.concatenate([grad_step_in, grad_in_map, grad_out_map], axis=1)
     ).astype(BF16)
-    grad_selected, first_grads = lax.optimization_barrier((grad_selected, first_grads))
+    early_grads = weight_grads(
+        [(grad_low_mamba, gated_low), (acting_mamba, grad_gate_low)], 256
+    )
+    grad_selected, first_grads, early_grads, second_both, second_down_grad = (
+        lax.optimization_barrier(
+            (grad_selected, first_grads, early_grads, second_both, second_down_grad)
+        )
+    )
+    early_grads = scattered(early_grads, ("dp", "seq"))
     grad_select = product_tl(grad_selected, inputs_low)
     grad_inputs = grad_inputs + product_t(grad_selected, select_weight)
     grad_conv_pre = grad_inputs * silu_slope(conv_pre)
@@ -1836,11 +1851,7 @@
         back_edge, ((rows_here - (tap_count - 1), 0), (0, 0))
     )
     grad_conv_low = grad_conv_input.astype(BF16)
-    mamba_pairs = [
-        (grad_low_mamba, gated_low),
-        (acting_mamba, grad_gate_low),
-        (acting_mamba, grad_conv_low),
-    ]
+    late_pairs = [(acting_mamba, grad_conv_low)]
     loose = (
         grad_kernel,
         grad_conv_bias[None],
@@ -1865,20 +1876,20 @@
         axis=0,
     ).reshape(devices, each, width)
     if split_four:
-        grad_normed_mamba, summed, mamba_grads = matmul_sum(
+        grad_normed_mamba, summed, late_grads = matmul_sum(
             [grad_conv_low, grad_gate_low],
             in_full,
             0,
             11,
             small=blocks,
-            pairs=mamba_pairs,
+            pairs=late_pairs,
             scatter=True,
         )
     else:
         grad_normed_mamba, summed = matmul_sum(
             [grad_conv_low, grad_gate_low], in_full, 0, 11, small=blocks
         )
-        mamba_grads = scattered(weight_grads(mamba_pairs, 256), ("dp", "seq"))
+        late_grads = scattered(weight_grads(late_pairs, 256), ("dp", "seq"))
     input_grad, _, grad_gain_mamba = norm_back(stream_zero, gain_mamba, grad_normed_mamba, grad_one)
     summed = summed.reshape(devices * each, width).astype(F32)
 
@@ -1906,9 +1917,8 @@
     gain_rows = mamba_norm.shape[0]
     place = lax.axis_index("dp") * seq_count + seq_place
     grad_qkv, grad_attn_out = split(attn_grads, attn_qkv, attn_out)
-    grad_out, gate_half, conv_half = split(
-        mamba_grads, mamba_out, mamba_in[:, 1], mamba_in[:, 0]
-    )
+    grad_out, gate_half = split(early_grads, mamba_out, mamba_in[:, 1])
+    (conv_half,) = split(late_grads, mamba_in[:, 0])
     grad_in = jnp.stack([conv_half, gate_half], axis=1)
     grad_first_both, grad_first_down = split(first_grads, first_gate_up, first_down)
 

time: 1180 us -> 1160 us (0.983)
  Pallas kernels: 911 us -> 899 us
  local copies, waits for them, and re-layouts: 115 us -> 103 us
    pallas_call x8, Pallas kernels: 521 us -> 497 us  [matmul_sum(): pl.pallas_call(functools.partial(matmul_sum_kernel, columns=columns, firs...]
    unnamed x246 -> x242, local copies, waits for them, and re-layouts: 80.5 us -> 68.4 us
    reduce_scatter x3 -> x4, waiting for transfers between devices: 38.1 us -> 36.4 us  [scattered(): lax.psum_scatter(grads, axes, scatter_dimension=0, tiled=True)]
  transfers between devices with their start and end apart: 8 -> 9, of which waited for: 2 -> 2; matrix products, arithmetic and copies ran while one was open for 11% -> 11% of each run, Pallas kernels for 62% -> 62%
where the time goes in v2:
time: 1160 us; the launch traced here: 1150 us
  Pallas kernels  899 us (78%)
  local copies, waits for them, and re-layouts  103 us (9%)
  other arithmetic  58.7 us (5%)
  waiting for transfers between devices  37.2 us (3%)
  matrix products  30.3 us (3%)
  between operations  17.4 us (1%)
    pallas_call x8, Pallas kernels, matmul_sum(): pl.pallas_call(functools.partial(matmul_sum_kernel, columns=columns, firs...  497 us
    pallas_call x1, Pallas kernels, attend(): pl.pallas_call(functools.partial(attend_kernel, count=lax.axis_size('seq'...  73.7 us
    pallas_call x1, Pallas kernels, attend_back(): pl.pallas_call(functools.partial(attend_back_kernel, count=lax.axis_size(...  72.9 us
    unnamed x242, local copies, waits for them, and re-layouts  68.4 us
    pallas_call x1, Pallas kernels, first_gather(): pl.pallas_call(first_gather_kernel, in_specs=[whole, whole, far], out_spe...  42.1 us
    reduce_scatter x4, waiting for transfers between devices, scattered(): lax.psum_scatter(grads, axes, scatter_dimension=0, tiled=True)  36.4 us
    pallas_call x1, Pallas kernels, shards(): run_back(step_size, inputs, grad_scanned, in_wide, out_wide, rate_two, ke...  36 us
    pallas_call x2, Pallas kernels, tensor_sum(): pl.pallas_call(functools.partial(ar_kernel, pieces=pieces, rows=rows // p...  34.8 us
  transfers between devices with their start and end apart: 9, of which 2 were waited for; matrix products, arithmetic and copies ran while one was open for 11% of the time, Pallas kernels for 62%

profile of v2, /device:TPU:0, one launch (start us, length us, event | category | flops | bytes accessed | tf_op | source)
XLA Modules:
  0.0 1150.1 jit_solution(15530282574482907415)
XLA Ops:
  15.7 42.1 %first_gather.1 = (bf16[2048,2048]{1,0:T(8,128)(2,1)S(1)}, f32[8,8,256]{2,1,0:T(8,128)S(1)}, bf16[528,2048]{1,0:T(8,128)(2,1)S(1)}) custom-call(bf16[528,2048]{1,0:T(8,128)(2,1)S(1)} %bitcast.141, f32[8,256]{1,0:T(8,128)S(1)} %fusion.40.gains_ref, bf16[256,2048]{1,0:T(8,128)(2,1)S(1)} %bitcast.146), custom_call_target="tpu_custom_call" | custom-call | flops 420000000 | tf_op jit(solution)/shard_map/first_gather/pallas_call | solution.py:1565
  59.2 3.3 copy-done.38
  62.6 10.1 convolution_convert_fusion.gate_ref
  81.4 2.8 collective-permute-start
  95.1 4.2 fusion.47
  102.7 18.4 %tensor_sum.2 = bf16[528,256]{1,0:T(8,128)(2,1)S(1)} custom-call(bf16[528,256]{1,0:T(8,128)(2,1)S(1)} %pad.36.x_ref), custom_call_target="tpu_custom_call" | custom-call | flops 160000000 | tf_op jit(solution)/shard_map/tensor_sum/pallas_call | solution.py:348
  121.4 2.7 fusion.46
  125.7 6.8 scan_state.1
  132.6 7.2 gather_seq.2
  140.5 3.1 broadcast_in_dim.25.c_ref
  143.6 18.7 %scan_rows.1 = (f32[528,1024]{1,0:T(8,128)S(1)}, f32[528,16,1024]{2,1,0:T(8,128)}) custom-call(f32[528,1024]{1,0:T(8,128)S(1)} %get-tuple-element.234.dt_ref, f32[528,1024]{1,0:T(8,128)S(1)} %convert_multiply_fusion.1.dtx_ref, f32[528,16,128]{2,1,0:T(8,128)S(1)} %broadcast_in_dim.24.b_ref, f32[528,16,128]{2,1,0:T(8,128)} %broadcast_in_dim.25.c_ref, ...), custom_call_target="tpu_custom_call" | custom-call | flops 180000000 | tf_op jit(solution)/shard_map/scan_rows/pallas_call | solution.py:1744
  166.1 57.2 %matmul_sum.4 = bf16[528,2048]{1,0:T(8,128)(2,1)S(1)} custom-call(bf16[528,1024]{1,0:T(8,128)(2,1)S(1)} %copy-done.25, bf16[2048,3072]{1,0:T(8,128)(2,1)} %all-gather.4.cloned.1.call-done.refs_1_.w_ref), custom_call_target="tpu_custom_call" | custom-call | flops 580000000 | tf_op jit(solution)/shard_map/matmul_sum/pallas_call | solution.py:1385
  226.3 7.1 qkv_rows.1
  233.4 73.7 %attend.1 = (f32[528,512]{1,0:T(8,128)S(1)}, bf16[528,512]{1,0:T(8,128)(2,1)S(1)}, f32[4,528,128]{2,1,0:T(8,128)S(1)}, bf16[3,2,528,512]{3,2,1,0:T(8,128)(2,1)}) custom-call(bf16[528,512]{1,0:T(8,128)(2,1)S(1)} %get-tuple-element.96.q_ref, bf16[2,528,512]{2,1,0:T(8,128)(2,1)S(1)} %get-tuple-element.97.kv_ref), custom_call_target="tpu_custom_call" | custom-call | flops 550000000 | tf_op jit(solution)/shard_map/attend/pallas_call | solution.py:537
  307.2 59.1 %matmul_sum.5 = bf16[528,2048]{1,0:T(8,128)(2,1)S(1)} custom-call(bf16[528,512]{1,0:T(8,128)(2,1)S(1)} %get-tuple-element.98.refs_0_.refs_4_, bf16[2048,3072]{1,0:T(8,128)(2,1)} %all-gather.4.cloned.1.call-done.refs_1_.w_ref), custom_call_target="tpu_custom_call" | custom-call | flops 580000000 | tf_op jit(solution)/shard_map/matmul_sum/pallas_call | solution.py:1385
  366.4 3.3 multiply_reduce_fusion.2
  372.3 13.4 %gate_up.2 = (bf16[528,2048]{1,0:T(8,128)(2,1)S(1)}, bf16[528,2048]{1,0:T(8,128)(2,1)S(1)}, bf16[528,2048]{1,0:T(8,128)(2,1)S(1)}) custom-call(bf16[528,2048]{1,0:T(8,128)(2,1)S(1)} %multiply_convert_fusion.1.x_ref.refs_3_, bf16[2048,6144]{1,0:T(8,128)(2,1)} %all-gather.6.cloned.1.call-done.wg_ref.wu_ref.refs_1_.w_ref.refs_2_, ...), custom_call_target="tpu_custom_call" | custom-call | flops 140000000 | tf_op jit(solution)/shard_map/gate_up/pallas_call | solution.py:817
  388.4 60.3 %matmul_sum.6 = bf16[528,2048]{1,0:T(8,128)(2,1)S(1)} custom-call(bf16[528,2048]{1,0:T(8,128)(2,1)S(1)} %get-tuple-element.101.refs_0_.refs_5_, bf16[2048,6144]{1,0:T(8,128)(2,1)} %all-gather.6.cloned.1.call-done.wg_ref.wu_ref.refs_1_.w_ref.refs_2_), custom_call_target="tpu_custom_call" | custom-call | flops 580000000 | tf_op jit(solution)/shard_map/matmul_sum/pallas_call | solution.py:1385
  454.8 13.4 %gate_up.3 = (bf16[528,2048]{1,0:T(8,128)(2,1)S(1)}, bf16[528,2048]{1,0:T(8,128)(2,1)S(1)}, bf16[528,2048]{1,0:T(8,128)(2,1)S(1)}) custom-call(bf16[528,2048]{1,0:T(8,128)(2,1)S(1)} %copy-done.18, bf16[2048,6144]{1,0:T(8,128)(2,1)} %all-gather.8.cloned.1.call-done.wg_ref.wu_ref.refs_1_.w_ref.refs_2_, ...), custom_call_target="tpu_custom_call" | custom-call | flops 140000000 | tf_op jit(solution)/shard_map/gate_up/pallas_call | solution.py:817
  468.2 57.7 %matmul_sum.7 = bf16[528,2048]{1,0:T(8,128)(2,1)S(1)} custom-call(bf16[528,2048]{1,0:T(8,128)(2,1)S(1)} %get-tuple-element.104.refs_0_.refs_5_, bf16[2048,6144]{1,0:T(8,128)(2,1)} %all-gather.8.cloned.1.call-done.wg_ref.wu_ref.refs_1_.w_ref.refs_2_), custom_call_target="tpu_custom_call" | custom-call | flops 580000000 | tf_op jit(solution)/shard_map/matmul_sum/pallas_call | solution.py:1385
  525.9 3.7 multiply_reduce_fusion
  529.6 3.0 broadcast_multiply_fusion
  532.6 10.5 hidden_back.2
  543.0 66.5 %matmul_sum_grads.3 = (bf16[528,2048]{1,0:T(8,128)(2,1)S(1)}, bf16[2048,6144]{1,0:T(8,128)(2,1)}) custom-call(bf16[528,2048]{1,0:T(8,128)(2,1)S(1)} %get-tuple-element.107.refs_0_, bf16[528,2048]{1,0:T(8,128)(2,1)S(1)} %get-tuple-element.108.refs_1_, bf16[2048,6144]{1,0:T(8,128)(2,1)} %all-gather.8.cloned.1.call-done.wg_ref.wu_ref.refs_1_.w_ref.refs_2_, ...), custom_call_target="tpu_custom_call" | custom-call | flops 670000000 | tf_op jit(solution)/shard_map/matmul_sum_grads/pallas_call | solution.py:1385
  617.0 3.1 norm_back.4
  622.2 11.3 hidden_back.3
  633.5 66.9 %matmul_sum_grads.4 = (bf16[528,2048]{1,0:T(8,128)(2,1)S(1)}, bf16[2048,6144]{1,0:T(8,128)(2,1)}) custom-call(bf16[528,2048]{1,0:T(8,128)(2,1)S(1)} %get-tuple-element.113.refs_0_, bf16[528,2048]{1,0:T(8,128)(2,1)S(1)} %get-tuple-element.114.refs_1_, bf16[2048,6144]{1,0:T(8,128)(2,1)} %all-gather.6.cloned.1.call-done.wg_ref.wu_ref.refs_1_.w_ref.refs_2_, ...), custom_call_target="tpu_custom_call" | custom-call | flops 670000000 | tf_op jit(solution)/shard_map/matmul_sum_grads/pallas_call | solution.py:1385
  708.2 3.1 norm_back.5
  711.3 4.7 fusion.11.g_ref
  716.4 72.9 %attend_back.1.refs_0_ = bf16[528,1536]{1,0:T(8,128)(2,1)} custom-call(bf16[528,512]{1,0:T(8,128)(2,1)S(1)} %copy-done.68, bf16[528,512]{1,0:T(8,128)(2,1)S(1)} %fusion.11.g_ref, f32[528,512]{1,0:T(8,128)S(1)} %copy-done.62, f32[4,528,128]{2,1,0:T(8,128)S(1)} %copy-done.64, bf16[2,528,512]{2,1,0:T(8,128)(2,1)S(1)} %copy-done.60, ...), custom_call_target="tpu_custom_call" | custom-call | flops 550000000 | tf_op jit(solution)/shard_map/attend_back/pallas_call | solution.py:706
  789.3 22.0 %reduce-scatter.5.cloned.1.call-done = bf16[256,6144]{1,0:T(8,128)(2,1)} async-done(((bf16[2048,6144]{1,0:T(8,128)(2,1)}), bf16[256,6144]{1,0:T(8,128)(2,1)}) %reduce-scatter.5.cloned.1.call-update) | async-done | bytes 3145744 | tf_op jit(solution)/shard_map/reduce_scatter | solution.py:1450
  815.4 61.3 %matmul_sum_grads.5 = (bf16[528,2048]{1,0:T(8,128)(2,1)S(1)}, bf16[2048,2048]{1,0:T(8,128)(2,1)}) custom-call(bf16[528,1536]{1,0:T(8,128)(2,1)S(1)} %copy-done.39, bf16[2048,3072]{1,0:T(8,128)(2,1)} %all-gather.4.cloned.1.call-done.refs_1_.w_ref, bf16[528,2048]{1,0:T(8,128)(2,1)S(1)} %copy-done.21, bf16[528,2048]{1,0:T(8,128)(2,1)S(1)} %copy-done.48, ...), custom_call_target="tpu_custom_call" | custom-call | flops 670000000 | tf_op jit(solution)/shard_map/matmul_sum_grads/pallas_call | solution.py:1385
  879.3 3.1 norm_back.6
  884.5 5.7 gate_back.1
  890.3 6.9 scan_back_state.1.block_ref
  897.2 9.7 gather_seq.3
  907.1 36.0 %scan_back.1 = (f32[528,1024]{1,0:T(8,128)S(1)}, f32[528,1024]{1,0:T(8,128)S(1)}, f32[528,16]{1,0:T(8,128)S(1)}, f32[528,16]{1,0:T(8,128)S(1)}, f32[16,1024]{1,0:T(8,128)S(1)}) custom-call(f32[528,1024]{1,0:T(8,128)S(1)} %copy-done.9, f32[528,1024]{1,0:T(8,128)S(1)} %copy-done.34, f32[528,1024]{1,0:T(8,128)S(1)} %get-tuple-element.126.g_ref, ...), custom_call_target="tpu_custom_call" | custom-call | flops 360000000 | tf_op jit(solution)/shard_map/scan_back/pallas_call | solution.py:1808
  944.5 11.1 weight_grads.1
  959.1 16.4 %tensor_sum.3 = bf16[528,256]{1,0:T(8,128)(2,1)S(1)} custom-call(bf16[528,256]{1,0:T(8,128)(2,1)S(1)} %fusion.21.x_ref), custom_call_target="tpu_custom_call" | custom-call | flops 160000000 | tf_op jit(solution)/shard_map/tensor_sum/pallas_call | solution.py:348
  984.8 9.5 multiply_reduce_fusion.4
  1010.1 7.6 copy.67
  1017.7 5.2 copy.68
  1024.8 5.3 concatenate.35
  1032.2 67.8 %matmul_sum_small.1 = (bf16[528,2048]{1,0:T(8,128)(2,1)S(1)}, bf16[8,48,1024]{2,1,0:T(8,128)(2,1)S(1)}, bf16[256,1024]{1,0:T(8,128)(2,1)S(1)}) custom-call(bf16[528,1024]{1,0:T(8,128)(2,1)S(1)} %fusion.7.refs_0_, bf16[528,1024]{1,0:T(8,128)(2,1)S(1)} %copy-done.41, bf16[2048,2048]{1,0:T(8,128)(2,1)} %copy-done.38, bf16[8,48,1024]{2,1,0:T(8,128)(2,1)S(1)} %bitcast.147, ...), custom_call_target="tpu_custom_call" | custom-call | flops 670000000 | tf_op jit(solution)/shard_map/matmul_sum_small/pallas_call | solution.py:1385
  1102.8 6.1 norm_back.7
  1110.1 5.7 gather_dp_seq.1
  1122.3 3.0 copy.66
  1125.3 14.4 %reduce-scatter.11.cloned.1.call-done = bf16[256,2048]{1,0:T(8,128)(2,1)} async-done(((bf16[2048,2048]{1,0:T(8,128)(2,1)}), bf16[256,2048]{1,0:T(8,128)(2,1)}) %reduce-scatter.11.cloned.1.call-update) | async-done | bytes 1048592 | tf_op jit(solution)/shard_map/reduce_scatter | solution.py:1450
  (364 shorter events, 125.7 us)
Async XLA Ops:
  7.2 93.1 %copy-start = (bf16[1024,160]{0,1:T(8,128)(2,1)S(1)}, bf16[1024,160]{0,1:T(8,128)(2,1)}, u32[]{:S(2)}) copy-start(bf16[1024,160]{0,1:T(8,128)(2,1)} %param.29) | copy-start | bytes 983044
  7.2 157.7 %all-gather.4.cloned.1.call-start = ((), (), s32[]{:S(2)}) async-start(), calls=%async_computation.4 | async-start | bytes 14155776 | tf_op jit(solution)/shard_map/all_gather | solution.py:401
  62.6 309.7 %all-gather.6.cloned.1.call-start = ((), (), s32[]{:S(2)}) async-start(), calls=%async_computation.5 | async-start | bytes 28311552 | tf_op jit(solution)/shard_map/all_gather | solution.py:401
  76.1 377.0 %all-gather.8.cloned.1.call-start = ((), (), s32[]{:S(2)}) async-start(), calls=%async_computation.6 | async-start | bytes 28311552 | tf_op jit(solution)/shard_map/all_gather | solution.py:401
  80.7 730.6 %reduce-scatter.5.cloned.1.call-start = ((), (), s32[]{:S(2)}) async-start(), calls=%async_computation.7 | async-start | bytes 28311552 | tf_op jit(solution)/shard_map/reduce_scatter | solution.py:1450
  81.4 12.0 %collective-permute-start = (bf16[3,1024]{1,0:T(4,128)(2,1)S(1)}, bf16[3,1024]{1,0:T(4,128)(2,1)S(1)}, u32[]{:S(2)}, u32[]{:S(2)}) collective-permute-start(bf16[3,1024]{1,0:T(4,128)(2,1)S(1)} %slice.191), channel_id=1, source_target_pairs={{0,4},{4,8},{8,12},{1,5},{5,9},{9,13},{2,6},{6,10},{10,14},{3,7},{... | collective-permute-start | bytes 18440 | tf_op jit(solution)/shard_map/ppermute | solution.py:366
  101.6 19.8 %copy-start.104 = (f32[1024]{0:T(1024)S(1)}, f32[1024]{0:T(1024)}, u32[]{:S(2)}) copy-start(f32[1024]{0:T(1024)} %param.31) | copy-start | bytes 12292
  102.6 18.7 %copy-start.85 = (bf16[128,1024]{1,0:T(8,128)(2,1)S(1)}, bf16[128,1024]{1,0:T(8,128)(2,1)}, u32[]{:S(2)}) copy-start(bf16[128,1024]{1,0:T(8,128)(2,1)} %param.30) | copy-start | bytes 786436
  124.1 19.5 %copy-start.8 = (f32[528,1024]{1,0:T(8,128)}, f32[528,1024]{1,0:T(8,128)S(1)}, u32[]{:S(2)}) copy-start(f32[528,1024]{1,0:T(8,128)S(1)} %get-tuple-element.234.dt_ref) | copy-start | bytes 6488068
  125.7 17.9 %copy-start.1 = (f32[528,16,128]{2,1,0:T(8,128)}, f32[528,16,128]{2,1,0:T(8,128)S(1)}, u32[]{:S(2)}) copy-start(f32[528,16,128]{2,1,0:T(8,128)S(1)} %broadcast_in_dim.24.b_ref) | copy-start | bytes 12976132
  143.6 18.8 %copy-start.27 = (bf16[528,2048]{1,0:T(8,128)(2,1)S(1)}, bf16[528,2048]{1,0:T(8,128)(2,1)}, u32[]{:S(2)}) copy-start(bf16[528,2048]{1,0:T(8,128)(2,1)} %convolution_convert_fusion.gate_ref) | copy-start | bytes 6488068
  143.6 18.7 %copy-start.101 = (f32[1024]{0:T(1024)S(1)}, f32[1024]{0:T(1024)}, u32[]{:S(2)}) copy-start(f32[1024]{0:T(1024)} %param.33) | copy-start | bytes 12292
  166.1 59.6 %slice-start = ((s8[12582912]{0:T(1024)(128)(4,1)}), s8[4194304]{0:T(1024)(128)(4,1)S(1)}, s32[]{:S(2)}) async-start(s8[12582912]{0:T(1024)(128)(4,1)} %bitcast.137), calls=%async_computation.11 | async-start | bytes 8388608
  166.1 59.6 %slice-start.1 = ((s8[12582912]{0:T(1024)(128)(4,1)}), s8[4194304]{0:T(1024)(128)(4,1)S(1)}, s32[]{:S(2)}) async-start(s8[12582912]{0:T(1024)(128)(4,1)} %bitcast.137), calls=%async_computation.12 | async-start | bytes 8388608
  233.4 133.0 %copy-start.59 = (bf16[2,528,512]{2,1,0:T(8,128)(2,1)}, bf16[2,528,512]{2,1,0:T(8,128)(2,1)S(1)}, u32[]{:S(2)}) copy-start(bf16[2,528,512]{2,1,0:T(8,128)(2,1)S(1)} %get-tuple-element.97.kv_ref) | copy-start | bytes 3244036
  233.4 133.0 %copy-start.67 = (bf16[528,512]{1,0:T(8,128)(2,1)}, bf16[528,512]{1,0:T(8,128)(2,1)S(1)}, u32[]{:S(2)}) copy-start(bf16[528,512]{1,0:T(8,128)(2,1)S(1)} %get-tuple-element.96.q_ref) | copy-start | bytes 1622020
  307.2 59.2 %copy-start.57 = (bf16[528,512]{1,0:T(8,128)(2,1)}, bf16[528,512]{1,0:T(8,128)(2,1)S(1)}, u32[]{:S(2)}) copy-start(bf16[528,512]{1,0:T(8,128)(2,1)S(1)} %get-tuple-element.98.refs_0_.refs_4_) | copy-start | bytes 1622020
  307.2 59.2 %copy-start.61 = (f32[528,512]{1,0:T(8,128)}, f32[528,512]{1,0:T(8,128)S(1)}, u32[]{:S(2)}) copy-start(f32[528,512]{1,0:T(8,128)S(1)} %get-tuple-element.118.o_ref) | copy-start | bytes 3244036
  307.2 59.2 %copy-start.63 = (f32[4,528,128]{2,1,0:T(8,128)}, f32[4,528,128]{2,1,0:T(8,128)S(1)}, u32[]{:S(2)}) copy-start(f32[4,528,128]{2,1,0:T(8,128)S(1)} %get-tuple-element.119.lse_ref) | copy-start | bytes 3244036
  307.2 59.2 %copy-start.13 = (bf16[528,2048]{1,0:T(8,128)(2,1)S(1)}, bf16[528,2048]{1,0:T(8,128)(2,1)}, u32[]{:S(2)}) copy-start(bf16[528,2048]{1,0:T(8,128)(2,1)} %copy-done.12) | copy-start | bytes 6488068
  388.4 60.3 %copy-start.29 = (bf16[528,2048]{1,0:T(8,128)(2,1)}, bf16[528,2048]{1,0:T(8,128)(2,1)S(1)}, u32[]{:S(2)}) copy-start(bf16[528,2048]{1,0:T(8,128)(2,1)S(1)} %get-tuple-element.101.refs_0_.refs_5_) | copy-start | bytes 6488068
  388.4 60.3 %copy-start.3 = (f32[528,2048]{1,0:T(8,128)S(1)}, f32[528,2048]{1,0:T(8,128)}, u32[]{:S(2)}) copy-start(f32[528,2048]{1,0:T(8,128)} %copy-done.2) | copy-start | bytes 12976132
  468.1 57.8 %copy-start.30 = (bf16[528,2048]{1,0:T(8,128)(2,1)}, bf16[528,2048]{1,0:T(8,128)(2,1)S(1)}, u32[]{:S(2)}) copy-start(bf16[528,2048]{1,0:T(8,128)(2,1)S(1)} %get-tuple-element.104.refs_0_.refs_5_) | copy-start | bytes 6488068
  468.2 57.8 %copy-start.6 = (f32[528,2048]{1,0:T(8,128)S(1)}, f32[528,2048]{1,0:T(8,128)}, u32[]{:S(2)}) copy-start(f32[528,2048]{1,0:T(8,128)} %copy-done.5) | copy-start | bytes 12976132
  468.2 57.8 %copy-start.78 = (bf16[1,528,2048]{2,1,0:T(8,128)(2,1)S(1)}, bf16[1,528,2048]{2,1,0:T(8,128)(2,1)}, u32[]{:S(2)}) copy-start(bf16[1,528,2048]{2,1,0:T(8,128)(2,1)} %param.23) | copy-start | bytes 6488068
  610.9 368.8 %reduce-scatter.7.cloned.1.call-start = ((), (), s32[]{:S(2)}) async-start(), calls=%async_computation.8 | async-start | bytes 28311552 | tf_op jit(solution)/shard_map/reduce_scatter | solution.py:1450
  622.2 11.3 copy-start.37
  701.7 418.1 %reduce-scatter.9.cloned.1.call-start = ((), (), s32[]{:S(2)}) async-start(), calls=%async_computation.9 | async-start | bytes 9437184 | tf_op jit(solution)/shard_map/reduce_scatter | solution.py:1450
  716.4 94.9 %copy-start.21 = (bf16[528,2048]{1,0:T(8,128)(2,1)S(1)}, bf16[528,2048]{1,0:T(8,128)(2,1)}, u32[]{:S(2)}) copy-start(bf16[528,2048]{1,0:T(8,128)(2,1)} %copy-done.20) | copy-start | bytes 6488068
  815.4 61.4 %copy-start.46 = (f32[528,2048]{1,0:T(8,128)S(1)}, f32[528,2048]{1,0:T(8,128)}, u32[]{:S(2)}) copy-start(f32[528,2048]{1,0:T(8,128)} %copy-done.45) | copy-start | bytes 12976132
  890.2 16.9 %copy-start.36 = (f32[528,1024]{1,0:T(8,128)}, f32[528,1024]{1,0:T(8,128)S(1)}, u32[]{:S(2)}) copy-start(f32[528,1024]{1,0:T(8,128)S(1)} %get-tuple-element.126.g_ref) | copy-start | bytes 6488068
  890.2 54.3 %copy-start.40 = (bf16[528,1024]{1,0:T(8,128)(2,1)}, bf16[528,1024]{1,0:T(8,128)(2,1)S(1)}, u32[]{:S(2)}) copy-start(bf16[528,1024]{1,0:T(8,128)(2,1)S(1)} %get-tuple-element.133.refs_3_.refs_1_) | copy-start | bytes 3244036
  890.3 16.7 %copy-start.81 = (f32[16,1024]{1,0:T(8,128)S(1)}, f32[16,1024]{1,0:T(8,128)}, u32[]{:S(2)}) copy-start(f32[16,1024]{1,0:T(8,128)} %param.32) | copy-start | bytes 196612
  890.3 16.7 %copy-start.88 = (f32[1,1,1024]{2,1,0:T(1,128)S(1)}, f32[1,1,1024]{2,1,0:T(1,128)}, u32[]{:S(2)}) copy-start(f32[1,1,1024]{2,1,0:T(1,128)} %copy-done.87) | copy-start | bytes 12292
  890.3 16.7 %copy-start.90 = (f32[1,1,1024]{2,1,0:T(1,128)S(1)}, f32[1,1,1024]{2,1,0:T(1,128)}, u32[]{:S(2)}) copy-start(f32[1,1,1024]{2,1,0:T(1,128)} %copy-done.89) | copy-start | bytes 12292
  890.3 16.7 %copy-start.99 = (f32[1,1,1024]{2,1,0:T(1,128)S(1)}, f32[1,1,1024]{2,1,0:T(1,128)}, u32[]{:S(2)}) copy-start(f32[1,1,1024]{2,1,0:T(1,128)} %get-tuple-element.266) | copy-start | bytes 12292
  890.3 16.8 %copy-start.34 = (f32[528,1024]{1,0:T(8,128)S(1)}, f32[528,1024]{1,0:T(8,128)}, u32[]{:S(2)}) copy-start(f32[528,1024]{1,0:T(8,128)} %get-tuple-element.235.x_ref) | copy-start | bytes 6488068
  907.1 37.4 %copy-start.26 = (bf16[528,1024]{1,0:T(8,128)(2,1)S(1)}, bf16[528,1024]{1,0:T(8,128)(2,1)}, u32[]{:S(2)}) copy-start(bf16[528,1024]{1,0:T(8,128)(2,1)} %get-tuple-element.231.refs_0_.refs_2_) | copy-start | bytes 3244036
  907.1 37.4 %copy-start.32 = (bf16[528,2048]{1,0:T(8,128)(2,1)S(1)}, bf16[528,2048]{1,0:T(8,128)(2,1)}, u32[]{:S(2)}) copy-start(bf16[528,2048]{1,0:T(8,128)(2,1)} %copy-done.31) | copy-start | bytes 6488068
  944.5 11.1 copy-start.105
  955.6 19.9 %copy-start.77 = (bf16[256,6144]{1,0:T(8,128)(2,1)S(1)}, bf16[256,6144]{1,0:T(8,128)(2,1)}, u32[]{:S(2)}) copy-start(bf16[256,6144]{1,0:T(8,128)(2,1)} %reduce-scatter.5.cloned.1.call-done) | copy-start | bytes 9437188
  979.7 160.0 %reduce-scatter.11.cloned.1.call-start = ((), (), s32[]{:S(2)}) async-start(), calls=%async_computation.10 | async-start | bytes 9437184 | tf_op jit(solution)/shard_map/reduce_scatter | solution.py:1450
  994.9 35.2 %collective-permute-start.1 = (f32[3,1024]{1,0:T(4,128)}, f32[3,1024]{1,0:T(4,128)}, u32[]{:S(2)}, u32[]{:S(2)}) collective-permute-start(f32[3,1024]{1,0:T(4,128)} %pad_add_fusion.1), channel_id=1, source_target_pairs={{4,0},{8,4},{12,8},{5,1},{9,5},{13,9},{6,2},{10,6},{14,10},{7,3},{... | collective-permute-start | bytes 36872 | tf_op jit(solution)/shard_map/ppermute | solution.py:366
  1032.1 70.7 %slice-start.5 = ((s8[4325376]{0:T(1024)(128)(4,1)}), s8[4194304]{0:T(1024)(128)(4,1)S(1)}, s32[]{:S(2)}) async-start(s8[4325376]{0:T(1024)(128)(4,1)} %bitcast.142), calls=%async_computation.16 | async-start | bytes 8388608
  1032.1 70.7 %slice-start.7 = ((s8[4325376]{0:T(1024)(128)(4,1)}), s8[4194304]{0:T(1024)(128)(4,1)S(1)}, s32[]{:S(2)}) async-start(s8[4325376]{0:T(1024)(128)(4,1)} %bitcast.144), calls=%async_computation.18 | async-start | bytes 8388608
  1032.1 70.6 %slice-start.6 = ((s8[4325376]{0:T(1024)(128)(4,1)}), s8[131072]{0:T(1024)(128)(4,1)S(1)}, s32[]{:S(2)}) async-start(s8[4325376]{0:T(1024)(128)(4,1)} %bitcast.142), calls=%async_computation.17 | async-start | bytes 262144
  1032.2 70.6 %slice-start.8 = ((s8[4325376]{0:T(1024)(128)(4,1)}), s8[131072]{0:T(1024)(128)(4,1)S(1)}, s32[]{:S(2)}) async-start(s8[4325376]{0:T(1024)(128)(4,1)} %bitcast.144), calls=%async_computation.19 | async-start | bytes 262144
  1110.1 12.1 %copy-start.70 = (bf16[256,1024]{1,0:T(8,128)(2,1)S(1)}, bf16[256,1024]{1,0:T(8,128)(2,1)}, u32[]{:S(2)}) copy-start(bf16[256,1024]{1,0:T(8,128)(2,1)} %copy-done.69) | copy-start | bytes 1572868
  (77 other events, 312.0 us)
Sparse Core Ops, SparseCore 0:
  62.7 72.4 all-gather.3
  137.6 167.8 all-gather.5
  308.0 129.5 all-gather.7
  611.0 200.2 reduce-scatter.4
  814.8 159.7 reduce-scatter.6
  979.8 83.9 reduce-scatter.8
  1067.7 71.9 reduce-scatter.10

commit v3 on v2

--- a/solution.py
+++ b/solution.py
@@ -1762,10 +1762,10 @@
     grad_low = grad_four.astype(BF16)
     grad_gate, grad_up = hidden_back(grad_low, second_weights, gate, up, 256)
     second_parts = [(acting, grad_gate), (acting, grad_up), (grad_low, hidden_low)]
-    grad_normed, second_grads = matmul_sum(
-        [grad_gate, grad_up], second_weights, 0, 16, pairs=second_parts
-    )
+    second_grads = weight_grads(second_parts, 256)
+    grad_gate, grad_up, second_grads = lax.optimization_barrier((grad_gate, grad_up, second_grads))
     second_grads = scattered(second_grads, ("dp", "seq"))
+    grad_normed = matmul_sum([grad_gate, grad_up], second_weights, 0, 9)
     grad_three, grad_low, grad_gain_second = norm_back(
         stream_three, gain_second, grad_normed, grad_four
     )
@@ -1782,19 +1782,18 @@
     grad_projected_attn = attend_back(
         queries, grad_attended, attended, log_sums, own_kv, far_kv, cosine, sine, 14
     )
-    grad_projected_attn, second_grads = lax.optimization_barrier(
-        (grad_projected_attn, second_grads)
+    grad_projected_attn, second_grads, first_grads = lax.optimization_barrier(
+        (grad_projected_attn, second_grads, first_grads)
     )
     first_grads = scattered(first_grads, ("dp", "seq"))
+    second_both, second_down_grad = split(second_grads, second_gate_up, second_down)
     attn_pairs = [(acting_attn, grad_projected_attn), (grad_low_attn, attended_low)]
     grad_normed_attn, attn_grads = matmul_sum(
         [grad_projected_attn], mixed_full, qkv_column, 10, pairs=attn_pairs
     )
-    attn_grads = scattered(attn_grads, ("dp", "seq"))
     grad_one, grad_low_mamba, grad_gain_attn = norm_back(
         stream_one, gain_attn, grad_normed_attn, grad_two
     )
-    second_both, second_down_grad = split(second_grads, second_gate_up, second_down)
     grad_scanned, grad_gate_low, grad_skip = gate_back(
         grad_low_mamba, mixed_full, projected, channels, scanned, inputs_low
     )
@@ -1821,11 +1820,12 @@
     early_grads = weight_grads(
         [(grad_low_mamba, gated_low), (acting_mamba, grad_gate_low)], 256
     )
-    grad_selected, first_grads, early_grads, second_both, second_down_grad = (
+    grad_selected, first_grads, attn_grads, early_grads, second_both, second_down_grad = (
         lax.optimization_barrier(
-            (grad_selected, first_grads, early_grads, second_both, second_down_grad)
-        )
-    )
+            (grad_selected, first_grads, attn_grads, early_grads, second_both, second_down_grad)
+        )
+    )
+    attn_grads = scattered(attn_grads, ("dp", "seq"))
     early_grads = scattered(early_grads, ("dp", "seq"))
     grad_select = product_tl(grad_selected, inputs_low)
     grad_inputs = grad_inputs + product_t(grad_selected, select_weight)

time: 1160 us -> 1130 us (0.974)
  waiting for transfers between devices: 37.2 us -> 16.9 us
    pallas_call x1 -> x2, Pallas kernels: 11.1 us -> 40.6 us  [weight_grads(): pl.pallas_call(functools.partial(weight_grads_kernel, counts=counts), gri...]
    reduce_scatter x4, waiting for transfers between devices: 36.4 us -> 16 us  [scattered(): lax.psum_scatter(grads, axes, scatter_dimension=0, tiled=True)]
    pallas_call x1, Pallas kernels: 72.9 us -> 55.2 us  [attend_back(): pl.pallas_call(functools.partial(attend_back_kernel, count=lax.axis_size(...]
    pallas_call x8, Pallas kernels: 497 us -> 485 us  [matmul_sum(): pl.pallas_call(functools.partial(matmul_sum_kernel, columns=columns, firs...]
    unnamed x242 -> x240, local copies, waits for them, and re-layouts: 68.4 us -> 59.9 us
  transfers between devices with their start and end apart: 9 -> 9, of which waited for: 2 -> 1; matrix products, arithmetic and copies ran while one was open for 11% -> 11% of each run, Pallas kernels for 62% -> 67%
where the time goes in v3:
time: 1130 us; the launch traced here: 1120 us
  Pallas kernels  902 us (80%)
  local copies, waits for them, and re-layouts  94.3 us (8%)
  other arithmetic  55.5 us (5%)
  matrix products  31.6 us (3%)
  between operations  17.8 us (2%)
  waiting for transfers between devices  16.9 us (1%)
    pallas_call x8, Pallas kernels, matmul_sum(): pl.pallas_call(functools.partial(matmul_sum_kernel, columns=columns, firs...  485 us
    pallas_call x1, Pallas kernels, attend(): pl.pallas_call(functools.partial(attend_kernel, count=lax.axis_size('seq'...  74.5 us
    unnamed x240, local copies, waits for them, and re-layouts  59.9 us
    pallas_call x1, Pallas kernels, attend_back(): pl.pallas_call(functools.partial(attend_back_kernel, count=lax.axis_size(...  55.2 us
    pallas_call x1, Pallas kernels, first_gather(): pl.pallas_call(first_gather_kernel, in_specs=[whole, whole, far], out_spe...  42.1 us
    pallas_call x2, Pallas kernels, weight_grads(): pl.pallas_call(functools.partial(weight_grads_kernel, counts=counts), gri...  40.6 us
    pallas_call x1, Pallas kernels, shards(): run_back(step_size, inputs, grad_scanned, in_wide, out_wide, rate_two, ke...  36 us
    pallas_call x2, Pallas kernels, tensor_sum(): pl.pallas_call(functools.partial(ar_kernel, pieces=pieces, rows=rows // p...  34.3 us
  transfers between devices with their start and end apart: 9, of which 1 were waited for; matrix products, arithmetic and copies ran while one was open for 11% of the time, Pallas kernels for 67%

profile of v3, /device:TPU:0, one launch (start us, length us, event | category | flops | bytes accessed | tf_op | source)
XLA Modules:
  0.0 1122.2 jit_solution(300872636169776775)
XLA Ops:
  15.7 42.1 %first_gather.1 = (bf16[2048,2048]{1,0:T(8,128)(2,1)S(1)}, f32[8,8,256]{2,1,0:T(8,128)S(1)}, bf16[528,2048]{1,0:T(8,128)(2,1)S(1)}) custom-call(bf16[528,2048]{1,0:T(8,128)(2,1)S(1)} %bitcast.143, f32[8,256]{1,0:T(8,128)S(1)} %fusion.40.gains_ref, bf16[256,2048]{1,0:T(8,128)(2,1)S(1)} %bitcast.150), custom_call_target="tpu_custom_call" | custom-call | flops 420000000 | tf_op jit(solution)/shard_map/first_gather/pallas_call | solution.py:1565
  59.2 3.3 copy-done.39
  62.6 10.1 convolution_convert_fusion.gate_ref
  81.4 2.8 collective-permute-start
  95.0 4.2 fusion.47
  102.7 18.7 %tensor_sum.2 = bf16[528,256]{1,0:T(8,128)(2,1)S(1)} custom-call(bf16[528,256]{1,0:T(8,128)(2,1)S(1)} %pad.36.x_ref), custom_call_target="tpu_custom_call" | custom-call | flops 160000000 | tf_op jit(solution)/shard_map/tensor_sum/pallas_call | solution.py:348
  121.6 2.7 fusion.46
  126.0 6.8 scan_state.1
  132.8 7.0 gather_seq.2
  140.5 3.1 broadcast_in_dim.25.c_ref
  143.6 18.8 %scan_rows.1 = (f32[528,1024]{1,0:T(8,128)S(1)}, f32[528,16,1024]{2,1,0:T(8,128)}) custom-call(f32[528,1024]{1,0:T(8,128)S(1)} %get-tuple-element.240.dt_ref, f32[528,1024]{1,0:T(8,128)S(1)} %convert_multiply_fusion.1.dtx_ref, f32[528,16,128]{2,1,0:T(8,128)S(1)} %broadcast_in_dim.24.b_ref, f32[528,16,128]{2,1,0:T(8,128)} %broadcast_in_dim.25.c_ref, ...), custom_call_target="tpu_custom_call" | custom-call | flops 180000000 | tf_op jit(solution)/shard_map/scan_rows/pallas_call | solution.py:1744
  166.2 56.4 %matmul_sum.5 = bf16[528,2048]{1,0:T(8,128)(2,1)S(1)} custom-call(bf16[528,1024]{1,0:T(8,128)(2,1)S(1)} %copy-done.23, bf16[2048,3072]{1,0:T(8,128)(2,1)} %all-gather.4.cloned.1.call-done.refs_1_.w_ref), custom_call_target="tpu_custom_call" | custom-call | flops 580000000 | tf_op jit(solution)/shard_map/matmul_sum/pallas_call | solution.py:1385
  225.6 7.1 qkv_rows.1
  232.7 74.5 %attend.1 = (f32[528,512]{1,0:T(8,128)S(1)}, bf16[528,512]{1,0:T(8,128)(2,1)S(1)}, f32[4,528,128]{2,1,0:T(8,128)S(1)}, bf16[3,2,528,512]{3,2,1,0:T(8,128)(2,1)}) custom-call(bf16[528,512]{1,0:T(8,128)(2,1)S(1)} %get-tuple-element.99.q_ref, bf16[2,528,512]{2,1,0:T(8,128)(2,1)S(1)} %get-tuple-element.100.kv_ref), custom_call_target="tpu_custom_call" | custom-call | flops 550000000 | tf_op jit(solution)/shard_map/attend/pallas_call | solution.py:537
  307.3 58.8 %matmul_sum.6 = bf16[528,2048]{1,0:T(8,128)(2,1)S(1)} custom-call(bf16[528,512]{1,0:T(8,128)(2,1)S(1)} %get-tuple-element.101.refs_0_.refs_4_, bf16[2048,3072]{1,0:T(8,128)(2,1)} %all-gather.4.cloned.1.call-done.refs_1_.w_ref), custom_call_target="tpu_custom_call" | custom-call | flops 580000000 | tf_op jit(solution)/shard_map/matmul_sum/pallas_call | solution.py:1385
  366.2 3.6 multiply_reduce_fusion.2
  372.4 14.3 %gate_up.2 = (bf16[528,2048]{1,0:T(8,128)(2,1)S(1)}, bf16[528,2048]{1,0:T(8,128)(2,1)S(1)}, bf16[528,2048]{1,0:T(8,128)(2,1)S(1)}) custom-call(bf16[528,2048]{1,0:T(8,128)(2,1)S(1)} %multiply_convert_fusion.1.x_ref.refs_3_, bf16[2048,6144]{1,0:T(8,128)(2,1)} %all-gather.6.cloned.1.call-done.wg_ref.wu_ref.refs_1_.w_ref.refs_2_, ...), custom_call_target="tpu_custom_call" | custom-call | flops 140000000 | tf_op jit(solution)/shard_map/gate_up/pallas_call | solution.py:817
  389.3 59.0 %matmul_sum.7 = bf16[528,2048]{1,0:T(8,128)(2,1)S(1)} custom-call(bf16[528,2048]{1,0:T(8,128)(2,1)S(1)} %get-tuple-element.104.refs_0_.refs_5_, bf16[2048,6144]{1,0:T(8,128)(2,1)} %all-gather.6.cloned.1.call-done.wg_ref.wu_ref.refs_1_.w_ref.refs_2_), custom_call_target="tpu_custom_call" | custom-call | flops 580000000 | tf_op jit(solution)/shard_map/matmul_sum/pallas_call | solution.py:1385
  451.5 13.4 %gate_up.3 = (bf16[528,2048]{1,0:T(8,128)(2,1)S(1)}, bf16[528,2048]{1,0:T(8,128)(2,1)S(1)}, bf16[528,2048]{1,0:T(8,128)(2,1)S(1)}) custom-call(bf16[528,2048]{1,0:T(8,128)(2,1)S(1)} %multiply_convert_fusion.x_ref.refs_0_.refs_1_, bf16[2048,6144]{1,0:T(8,128)(2,1)} %all-gather.8.cloned.1.call-done.wg_ref.wu_ref.refs_1_.w_ref.refs_2_, ...), custom_call_target="tpu_custom_call" | custom-call | flops 140000000 | tf_op jit(solution)/shard_map/gate_up/pallas_call | solution.py:817
  464.9 57.1 %matmul_sum.8 = bf16[528,2048]{1,0:T(8,128)(2,1)S(1)} custom-call(bf16[528,2048]{1,0:T(8,128)(2,1)S(1)} %get-tuple-element.107.refs_0_.refs_5_, bf16[2048,6144]{1,0:T(8,128)(2,1)} %all-gather.8.cloned.1.call-done.wg_ref.wu_ref.refs_1_.w_ref.refs_2_), custom_call_target="tpu_custom_call" | custom-call | flops 580000000 | tf_op jit(solution)/shard_map/matmul_sum/pallas_call | solution.py:1385
  522.0 3.7 multiply_reduce_fusion
  525.7 3.0 broadcast_multiply_fusion
  528.7 9.6 hidden_back.2
  538.3 29.5 %weight_grads.2 = bf16[2048,6144]{1,0:T(8,128)(2,1)} custom-call(bf16[528,2048]{1,0:T(8,128)(2,1)S(1)} %multiply_convert_fusion.x_ref.refs_0_.refs_1_, bf16[528,2048]{1,0:T(8,128)(2,1)S(1)} %multiply_convert_fusion.x_ref.refs_0_.refs_1_, bf16[528,2048]{1,0:T(8,128)(2,1)S(1)} %get-tuple-element.246.g_ref.refs_2_, ...), custom_call_target="tpu_custom_call" | custom-call | flops 300000000 | tf_op jit(solution)/shard_map/weight_grads/pallas_call | solution.py:863
  573.7 58.2 %matmul_sum.9.normed_ref = bf16[528,2048]{1,0:T(8,128)(2,1)S(1)} custom-call(bf16[528,2048]{1,0:T(8,128)(2,1)S(1)} %copy-done.35, bf16[528,2048]{1,0:T(8,128)(2,1)S(1)} %copy-done.37, bf16[2048,6144]{1,0:T(8,128)(2,1)} %all-gather.8.cloned.1.call-done.wg_ref.wu_ref.refs_1_.w_ref.refs_2_), custom_call_target="tpu_custom_call" | custom-call | flops 580000000 | tf_op jit(solution)/shard_map/matmul_sum/pallas_call | solution.py:1385
  636.5 3.1 norm_back.4
  641.6 10.9 hidden_back.3
  652.6 67.4 %matmul_sum_grads.2 = (bf16[528,2048]{1,0:T(8,128)(2,1)S(1)}, bf16[2048,6144]{1,0:T(8,128)(2,1)}) custom-call(bf16[528,2048]{1,0:T(8,128)(2,1)S(1)} %get-tuple-element.117.refs_0_, bf16[528,2048]{1,0:T(8,128)(2,1)S(1)} %get-tuple-element.118.refs_1_, bf16[2048,6144]{1,0:T(8,128)(2,1)} %all-gather.6.cloned.1.call-done.wg_ref.wu_ref.refs_1_.w_ref.refs_2_, ...), custom_call_target="tpu_custom_call" | custom-call | flops 670000000 | tf_op jit(solution)/shard_map/matmul_sum_grads/pallas_call | solution.py:1385
  720.1 3.1 norm_back.5
  723.3 4.7 fusion.11.g_ref
  728.3 55.2 %attend_back.1.refs_0_ = bf16[528,1536]{1,0:T(8,128)(2,1)} custom-call(bf16[528,512]{1,0:T(8,128)(2,1)S(1)} %copy-done.64, bf16[528,512]{1,0:T(8,128)(2,1)S(1)} %fusion.11.g_ref, f32[528,512]{1,0:T(8,128)S(1)} %copy-done.58, f32[4,528,128]{2,1,0:T(8,128)S(1)} %copy-done.60, bf16[2,528,512]{2,1,0:T(8,128)(2,1)S(1)} %copy-done.56, ...), custom_call_target="tpu_custom_call" | custom-call | flops 550000000 | tf_op jit(solution)/shard_map/attend_back/pallas_call | solution.py:706
  788.2 59.7 %matmul_sum_grads.3 = (bf16[528,2048]{1,0:T(8,128)(2,1)S(1)}, bf16[2048,2048]{1,0:T(8,128)(2,1)}) custom-call(bf16[528,1536]{1,0:T(8,128)(2,1)S(1)} %copy-done.40, bf16[2048,3072]{1,0:T(8,128)(2,1)} %all-gather.4.cloned.1.call-done.refs_1_.w_ref, bf16[528,2048]{1,0:T(8,128)(2,1)S(1)} %copy-done.20, bf16[528,2048]{1,0:T(8,128)(2,1)S(1)} %copy-done.48, ...), custom_call_target="tpu_custom_call" | custom-call | flops 670000000 | tf_op jit(solution)/shard_map/matmul_sum_grads/pallas_call | solution.py:1385
  850.3 3.1 norm_back.6
  855.4 6.0 gate_back.1
  861.5 6.9 scan_back_state.1.block_ref
  868.4 12.4 %gather_seq.3 = f32[4,16,1024]{2,1,0:T(8,128)S(1)} custom-call(f32[16,1024]{1,0:T(8,128)S(1)} %scan_back_state.1.block_ref), custom_call_target="tpu_custom_call" | custom-call | flops 60000000 | tf_op jit(solution)/shard_map/gather_seq/pallas_call | solution.py:272
  881.0 36.0 %scan_back.1 = (f32[528,1024]{1,0:T(8,128)S(1)}, f32[528,1024]{1,0:T(8,128)S(1)}, f32[528,16]{1,0:T(8,128)S(1)}, f32[528,16]{1,0:T(8,128)S(1)}, f32[16,1024]{1,0:T(8,128)S(1)}) custom-call(f32[528,1024]{1,0:T(8,128)S(1)} %copy-done.8, f32[528,1024]{1,0:T(8,128)S(1)} %copy-done.31, f32[528,1024]{1,0:T(8,128)S(1)} %get-tuple-element.131.g_ref, ...), custom_call_target="tpu_custom_call" | custom-call | flops 360000000 | tf_op jit(solution)/shard_map/scan_back/pallas_call | solution.py:1807
  918.4 11.1 weight_grads.3
  933.0 15.6 %tensor_sum.3 = bf16[528,256]{1,0:T(8,128)(2,1)S(1)} custom-call(bf16[528,256]{1,0:T(8,128)(2,1)S(1)} %fusion.21.x_ref), custom_call_target="tpu_custom_call" | custom-call | flops 160000000 | tf_op jit(solution)/shard_map/tensor_sum/pallas_call | solution.py:348
  962.1 9.3 multiply_reduce_fusion.4
  982.1 5.2 copy.67
  987.4 5.2 copy.68
  994.5 5.3 concatenate.35
  1001.8 68.4 %matmul_sum_small.1 = (bf16[528,2048]{1,0:T(8,128)(2,1)S(1)}, bf16[8,48,1024]{2,1,0:T(8,128)(2,1)S(1)}, bf16[256,1024]{1,0:T(8,128)(2,1)S(1)}) custom-call(bf16[528,1024]{1,0:T(8,128)(2,1)S(1)} %fusion.7.refs_0_, bf16[528,1024]{1,0:T(8,128)(2,1)S(1)} %copy-done.42, bf16[2048,2048]{1,0:T(8,128)(2,1)} %copy-done.39, bf16[8,48,1024]{2,1,0:T(8,128)(2,1)S(1)} %bitcast.151, ...), custom_call_target="tpu_custom_call" | custom-call | flops 670000000 | tf_op jit(solution)/shard_map/matmul_sum_small/pallas_call | solution.py:1385
  1073.1 6.1 norm_back.7
  1080.4 5.7 gather_dp_seq.1
  1092.6 2.9 copy.66
  1095.6 16.0 %reduce-scatter.11.cloned.1.call-done = bf16[256,2048]{1,0:T(8,128)(2,1)} async-done(((bf16[2048,2048]{1,0:T(8,128)(2,1)}), bf16[256,2048]{1,0:T(8,128)(2,1)}) %reduce-scatter.11.cloned.1.call-update) | async-done | bytes 1048592 | tf_op jit(solution)/shard_map/reduce_scatter | solution.py:1450
  (365 shorter events, 117.6 us)
Async XLA Ops:
  7.2 93.1 %copy-start = (bf16[1024,160]{0,1:T(8,128)(2,1)S(1)}, bf16[1024,160]{0,1:T(8,128)(2,1)}, u32[]{:S(2)}) copy-start(bf16[1024,160]{0,1:T(8,128)(2,1)} %param.29) | copy-start | bytes 983044
  7.2 157.7 %all-gather.4.cloned.1.call-start = ((), (), s32[]{:S(2)}) async-start(), calls=%async_computation.4 | async-start | bytes 14155776 | tf_op jit(solution)/shard_map/all_gather | solution.py:401
  62.6 309.8 %all-gather.6.cloned.1.call-start = ((), (), s32[]{:S(2)}) async-start(), calls=%async_computation.5 | async-start | bytes 28311552 | tf_op jit(solution)/shard_map/all_gather | solution.py:401
  76.1 375.4 %all-gather.8.cloned.1.call-start = ((), (), s32[]{:S(2)}) async-start(), calls=%async_computation.6 | async-start | bytes 28311552 | tf_op jit(solution)/shard_map/all_gather | solution.py:401
  80.6 702.8 %reduce-scatter.5.cloned.1.call-start = ((), (), s32[]{:S(2)}) async-start(), calls=%async_computation.7 | async-start | bytes 28311552 | tf_op jit(solution)/shard_map/reduce_scatter | solution.py:1450
  81.4 12.0 %collective-permute-start = (bf16[3,1024]{1,0:T(4,128)(2,1)S(1)}, bf16[3,1024]{1,0:T(4,128)(2,1)S(1)}, u32[]{:S(2)}, u32[]{:S(2)}) collective-permute-start(bf16[3,1024]{1,0:T(4,128)(2,1)S(1)} %slice.191), channel_id=1, source_target_pairs={{0,4},{4,8},{8,12},{1,5},{5,9},{9,13},{2,6},{6,10},{10,14},{3,7},{... | collective-permute-start | bytes 18440 | tf_op jit(solution)/shard_map/ppermute | solution.py:366
  101.5 20.1 %copy-start.99 = (f32[1024]{0:T(1024)S(1)}, f32[1024]{0:T(1024)}, u32[]{:S(2)}) copy-start(f32[1024]{0:T(1024)} %param.31) | copy-start | bytes 12292
  102.6 19.0 %copy-start.80 = (bf16[128,1024]{1,0:T(8,128)(2,1)S(1)}, bf16[128,1024]{1,0:T(8,128)(2,1)}, u32[]{:S(2)}) copy-start(bf16[128,1024]{1,0:T(8,128)(2,1)} %param.30) | copy-start | bytes 786436
  124.3 19.3 %copy-start.7 = (f32[528,1024]{1,0:T(8,128)}, f32[528,1024]{1,0:T(8,128)S(1)}, u32[]{:S(2)}) copy-start(f32[528,1024]{1,0:T(8,128)S(1)} %get-tuple-element.240.dt_ref) | copy-start | bytes 6488068
  125.9 17.6 %copy-start.1 = (f32[528,16,128]{2,1,0:T(8,128)}, f32[528,16,128]{2,1,0:T(8,128)S(1)}, u32[]{:S(2)}) copy-start(f32[528,16,128]{2,1,0:T(8,128)S(1)} %broadcast_in_dim.24.b_ref) | copy-start | bytes 12976132
  143.6 18.8 %copy-start.25 = (bf16[528,2048]{1,0:T(8,128)(2,1)S(1)}, bf16[528,2048]{1,0:T(8,128)(2,1)}, u32[]{:S(2)}) copy-start(bf16[528,2048]{1,0:T(8,128)(2,1)} %convolution_convert_fusion.gate_ref) | copy-start | bytes 6488068
  143.6 18.8 %copy-start.96 = (f32[1024]{0:T(1024)S(1)}, f32[1024]{0:T(1024)}, u32[]{:S(2)}) copy-start(f32[1024]{0:T(1024)} %param.33) | copy-start | bytes 12292
  166.2 58.9 %slice-start = ((s8[12582912]{0:T(1024)(128)(4,1)}), s8[4194304]{0:T(1024)(128)(4,1)S(1)}, s32[]{:S(2)}) async-start(s8[12582912]{0:T(1024)(128)(4,1)} %bitcast.137), calls=%async_computation.11 | async-start | bytes 8388608
  166.2 58.9 %slice-start.1 = ((s8[12582912]{0:T(1024)(128)(4,1)}), s8[4194304]{0:T(1024)(128)(4,1)S(1)}, s32[]{:S(2)}) async-start(s8[12582912]{0:T(1024)(128)(4,1)} %bitcast.137), calls=%async_computation.12 | async-start | bytes 8388608
  232.7 133.4 %copy-start.55 = (bf16[2,528,512]{2,1,0:T(8,128)(2,1)}, bf16[2,528,512]{2,1,0:T(8,128)(2,1)S(1)}, u32[]{:S(2)}) copy-start(bf16[2,528,512]{2,1,0:T(8,128)(2,1)S(1)} %get-tuple-element.100.kv_ref) | copy-start | bytes 3244036
  232.7 133.4 %copy-start.63 = (bf16[528,512]{1,0:T(8,128)(2,1)}, bf16[528,512]{1,0:T(8,128)(2,1)S(1)}, u32[]{:S(2)}) copy-start(bf16[528,512]{1,0:T(8,128)(2,1)S(1)} %get-tuple-element.99.q_ref) | copy-start | bytes 1622020
  307.2 58.9 %copy-start.53 = (bf16[528,512]{1,0:T(8,128)(2,1)}, bf16[528,512]{1,0:T(8,128)(2,1)S(1)}, u32[]{:S(2)}) copy-start(bf16[528,512]{1,0:T(8,128)(2,1)S(1)} %get-tuple-element.101.refs_0_.refs_4_) | copy-start | bytes 1622020
  307.3 58.9 %copy-start.57 = (f32[528,512]{1,0:T(8,128)}, f32[528,512]{1,0:T(8,128)S(1)}, u32[]{:S(2)}) copy-start(f32[528,512]{1,0:T(8,128)S(1)} %get-tuple-element.122.o_ref) | copy-start | bytes 3244036
  307.3 58.9 %copy-start.59 = (f32[4,528,128]{2,1,0:T(8,128)}, f32[4,528,128]{2,1,0:T(8,128)S(1)}, u32[]{:S(2)}) copy-start(f32[4,528,128]{2,1,0:T(8,128)S(1)} %get-tuple-element.123.lse_ref) | copy-start | bytes 3244036
  307.3 58.9 %copy-start.12 = (bf16[528,2048]{1,0:T(8,128)(2,1)S(1)}, bf16[528,2048]{1,0:T(8,128)(2,1)}, u32[]{:S(2)}) copy-start(bf16[528,2048]{1,0:T(8,128)(2,1)} %copy-done.11) | copy-start | bytes 6488068
  372.3 14.3 %copy-start.17 = (bf16[528,2048]{1,0:T(8,128)(2,1)}, bf16[528,2048]{1,0:T(8,128)(2,1)S(1)}, u32[]{:S(2)}) copy-start(bf16[528,2048]{1,0:T(8,128)(2,1)S(1)} %multiply_convert_fusion.1.x_ref.refs_3_) | copy-start | bytes 6488068
  389.3 59.0 %copy-start.27 = (bf16[528,2048]{1,0:T(8,128)(2,1)}, bf16[528,2048]{1,0:T(8,128)(2,1)S(1)}, u32[]{:S(2)}) copy-start(bf16[528,2048]{1,0:T(8,128)(2,1)S(1)} %get-tuple-element.104.refs_0_.refs_5_) | copy-start | bytes 6488068
  389.3 59.0 %copy-start.3 = (f32[528,2048]{1,0:T(8,128)S(1)}, f32[528,2048]{1,0:T(8,128)}, u32[]{:S(2)}) copy-start(f32[528,2048]{1,0:T(8,128)} %copy-done.2) | copy-start | bytes 12976132
  464.9 57.1 %copy-start.5 = (f32[528,2048]{1,0:T(8,128)S(1)}, f32[528,2048]{1,0:T(8,128)}, u32[]{:S(2)}) copy-start(f32[528,2048]{1,0:T(8,128)} %copy-done.4) | copy-start | bytes 12976132
  464.9 57.1 %copy-start.73 = (bf16[1,528,2048]{2,1,0:T(8,128)(2,1)S(1)}, bf16[1,528,2048]{2,1,0:T(8,128)(2,1)}, u32[]{:S(2)}) copy-start(bf16[1,528,2048]{2,1,0:T(8,128)(2,1)} %param.23) | copy-start | bytes 6488068
  570.5 382.2 %reduce-scatter.7.cloned.1.call-start = ((), (), s32[]{:S(2)}) async-start(), calls=%async_computation.8 | async-start | bytes 28311552 | tf_op jit(solution)/shard_map/reduce_scatter | solution.py:1450
  652.5 67.5 %slice-start.5 = ((s8[4325376]{0:T(1024)(128)(4,1)}), s8[4194304]{0:T(1024)(128)(4,1)S(1)}, s32[]{:S(2)}) async-start(s8[4325376]{0:T(1024)(128)(4,1)} %bitcast.141), calls=%async_computation.16 | async-start | bytes 8388608
  652.5 67.5 %slice-start.11 = ((s8[4325376]{0:T(1024)(128)(4,1)}), s8[4194304]{0:T(1024)(128)(4,1)S(1)}, s32[]{:S(2)}) async-start(s8[4325376]{0:T(1024)(128)(4,1)} %bitcast.148), calls=%async_computation.22 | async-start | bytes 8388608
  652.6 67.5 %slice-start.6 = ((s8[4325376]{0:T(1024)(128)(4,1)}), s8[131072]{0:T(1024)(128)(4,1)S(1)}, s32[]{:S(2)}) async-start(s8[4325376]{0:T(1024)(128)(4,1)} %bitcast.141), calls=%async_computation.17 | async-start | bytes 262144
  652.6 67.5 %slice-start.12 = ((s8[4325376]{0:T(1024)(128)(4,1)}), s8[131072]{0:T(1024)(128)(4,1)S(1)}, s32[]{:S(2)}) async-start(s8[4325376]{0:T(1024)(128)(4,1)} %bitcast.148), calls=%async_computation.23 | async-start | bytes 262144
  783.5 306.6 %reduce-scatter.9.cloned.1.call-start = ((), (), s32[]{:S(2)}) async-start(), calls=%async_computation.9 | async-start | bytes 9437184 | tf_op jit(solution)/shard_map/reduce_scatter | solution.py:1450
  788.2 59.7 %copy-start.45 = (f32[528,2048]{1,0:T(8,128)S(1)}, f32[528,2048]{1,0:T(8,128)}, u32[]{:S(2)}) copy-start(f32[528,2048]{1,0:T(8,128)} %copy-done.44) | copy-start | bytes 12976132
  861.4 19.6 %copy-start.33 = (f32[528,1024]{1,0:T(8,128)}, f32[528,1024]{1,0:T(8,128)S(1)}, u32[]{:S(2)}) copy-start(f32[528,1024]{1,0:T(8,128)S(1)} %get-tuple-element.131.g_ref) | copy-start | bytes 6488068
  861.4 57.0 %copy-start.41 = (bf16[528,1024]{1,0:T(8,128)(2,1)}, bf16[528,1024]{1,0:T(8,128)(2,1)S(1)}, u32[]{:S(2)}) copy-start(bf16[528,1024]{1,0:T(8,128)(2,1)S(1)} %get-tuple-element.139.refs_3_.refs_1_) | copy-start | bytes 3244036
  861.5 19.4 %copy-start.76 = (f32[16,1024]{1,0:T(8,128)S(1)}, f32[16,1024]{1,0:T(8,128)}, u32[]{:S(2)}) copy-start(f32[16,1024]{1,0:T(8,128)} %param.32) | copy-start | bytes 196612
  861.5 19.4 %copy-start.83 = (f32[1,1,1024]{2,1,0:T(1,128)S(1)}, f32[1,1,1024]{2,1,0:T(1,128)}, u32[]{:S(2)}) copy-start(f32[1,1,1024]{2,1,0:T(1,128)} %copy-done.82) | copy-start | bytes 12292
  861.5 19.4 %copy-start.85 = (f32[1,1,1024]{2,1,0:T(1,128)S(1)}, f32[1,1,1024]{2,1,0:T(1,128)}, u32[]{:S(2)}) copy-start(f32[1,1,1024]{2,1,0:T(1,128)} %copy-done.84) | copy-start | bytes 12292
  861.5 19.4 %copy-start.94 = (f32[1,1,1024]{2,1,0:T(1,128)S(1)}, f32[1,1,1024]{2,1,0:T(1,128)}, u32[]{:S(2)}) copy-start(f32[1,1,1024]{2,1,0:T(1,128)} %get-tuple-element.272) | copy-start | bytes 12292
  861.5 19.5 %copy-start.31 = (f32[528,1024]{1,0:T(8,128)S(1)}, f32[528,1024]{1,0:T(8,128)}, u32[]{:S(2)}) copy-start(f32[528,1024]{1,0:T(8,128)} %get-tuple-element.241.x_ref) | copy-start | bytes 6488068
  881.0 37.4 %copy-start.24 = (bf16[528,1024]{1,0:T(8,128)(2,1)S(1)}, bf16[528,1024]{1,0:T(8,128)(2,1)}, u32[]{:S(2)}) copy-start(bf16[528,1024]{1,0:T(8,128)(2,1)} %get-tuple-element.237.refs_0_.refs_2_) | copy-start | bytes 3244036
  881.0 37.4 %copy-start.29 = (bf16[528,2048]{1,0:T(8,128)(2,1)S(1)}, bf16[528,2048]{1,0:T(8,128)(2,1)}, u32[]{:S(2)}) copy-start(bf16[528,2048]{1,0:T(8,128)(2,1)} %copy-done.28) | copy-start | bytes 6488068
  929.5 19.1 %copy-start.72 = (bf16[256,6144]{1,0:T(8,128)(2,1)S(1)}, bf16[256,6144]{1,0:T(8,128)(2,1)}, u32[]{:S(2)}) copy-start(bf16[256,6144]{1,0:T(8,128)(2,1)} %reduce-scatter.5.cloned.1.call-done) | copy-start | bytes 9437188
  952.8 158.8 %reduce-scatter.11.cloned.1.call-start = ((), (), s32[]{:S(2)}) async-start(), calls=%async_computation.10 | async-start | bytes 9437184 | tf_op jit(solution)/shard_map/reduce_scatter | solution.py:1450
  972.1 27.7 %collective-permute-start.1 = (f32[3,1024]{1,0:T(4,128)}, f32[3,1024]{1,0:T(4,128)}, u32[]{:S(2)}, u32[]{:S(2)}) collective-permute-start(f32[3,1024]{1,0:T(4,128)} %pad_add_fusion.1), channel_id=1, source_target_pairs={{4,0},{8,4},{12,8},{5,1},{9,5},{13,9},{6,2},{10,6},{14,10},{7,3},{... | collective-permute-start | bytes 36872 | tf_op jit(solution)/shard_map/ppermute | solution.py:366
  1001.8 71.3 %slice-start.7 = ((s8[4325376]{0:T(1024)(128)(4,1)}), s8[4194304]{0:T(1024)(128)(4,1)S(1)}, s32[]{:S(2)}) async-start(s8[4325376]{0:T(1024)(128)(4,1)} %bitcast.144), calls=%async_computation.18 | async-start | bytes 8388608
  1001.8 71.3 %slice-start.9 = ((s8[4325376]{0:T(1024)(128)(4,1)}), s8[4194304]{0:T(1024)(128)(4,1)S(1)}, s32[]{:S(2)}) async-start(s8[4325376]{0:T(1024)(128)(4,1)} %bitcast.146), calls=%async_computation.20 | async-start | bytes 8388608
  1001.8 71.3 %slice-start.8 = ((s8[4325376]{0:T(1024)(128)(4,1)}), s8[131072]{0:T(1024)(128)(4,1)S(1)}, s32[]{:S(2)}) async-start(s8[4325376]{0:T(1024)(128)(4,1)} %bitcast.144), calls=%async_computation.19 | async-start | bytes 262144
  1001.8 71.3 %slice-start.10 = ((s8[4325376]{0:T(1024)(128)(4,1)}), s8[131072]{0:T(1024)(128)(4,1)S(1)}, s32[]{:S(2)}) async-start(s8[4325376]{0:T(1024)(128)(4,1)} %bitcast.146), calls=%async_computation.21 | async-start | bytes 262144
  (76 other events, 346.1 us)
Sparse Core Ops, SparseCore 0:
  62.7 72.4 all-gather.3
  137.6 167.9 all-gather.5
  308.0 129.5 all-gather.7
  570.6 166.9 reduce-scatter.4
  783.7 164.8 reduce-scatter.6
  952.9 82.7 reduce-scatter.8
  1039.5 71.9 reduce-scatter.10
